TPU v7x, 32 devices: a whole 2x2x4 slice. The times are simulated.
32 devices in a mesh: dp: 8 (over y, x, core), band: 4 (over z).
Axes of the slice: x: 2, y: 2, z: 4, core: 2. Of those that a mesh axis runs over, the one named last changes fastest.
Arguments:
- patches: bfloat16 [128, 64, 128, 256], P('dp', None, 'band'), may hold values from -6 to 6
- bias_token: bfloat16 [128], replicated, may hold values from -6 to 6
- gen_attn: bfloat16 [4, 128, 128], replicated, may hold values from -2 to 2
- gen_gain: bfloat16 [2, 128], replicated, may hold values from 0.5 to 1.5
- gen_ff_in: bfloat16 [128, 2048], replicated, may hold values from -0.5 to 0.5
- gen_ff_out: bfloat16 [2048, 128], replicated, may hold values from -0.125 to 0.125
- gen_kernel: bfloat16 [128, 196608], P(None, ('dp', 'band')), may hold values from -0.0029296875 to 0.0029296875
- gen_bias: bfloat16 [128, 768], replicated, may hold values from -0.4375 to 0.4375
- pos_table: bfloat16 [196, 768], replicated, may hold values from -6 to 6
- norm_gain: bfloat16 [2, 768], replicated, may hold values from 0.5 to 1.5
- norm_bias: bfloat16 [2, 768], replicated, may hold values from -4 to 4
- w_qkv: bfloat16 [768, 2304], P(('dp', 'band')), may hold values from -0.21875 to 0.21875
- w_out: bfloat16 [768, 768], P(('dp', 'band')), may hold values from -1.5 to 1.5
- w_fc1: bfloat16 [768, 3072], P(('dp', 'band')), may hold values from -0.21875 to 0.21875
- bias_in: bfloat16 [3072], replicated, may hold values from -4 to 4
- w_fc2: bfloat16 [3072, 768], P(('dp', 'band')), may hold values from -0.109375 to 0.109375
- wavelengths: int32 [128], replicated, may hold values from 400 to 2499
- kept: int32 [128, 64], P(('dp', 'band')), may hold values from 0 to 195, as said below
- counts: int32 [128], P(('dp', 'band')), may hold values from 34 to 64, as said below
- cotangent: bfloat16 [128, 64, 768], P(('dp', 'band')), may hold values from -6 to 6
Outputs:
- output: bfloat16 [128, 64, 768], P(('dp', 'band'))
- grad_patches: bfloat16 [128, 64, 128, 256], P('dp', None, 'band')
- grad_bias_token: float32 [128], replicated
- grad_gen_attn: float32 [4, 128, 128], replicated
- grad_gen_gain: float32 [2, 128], replicated
- grad_gen_ff_in: float32 [128, 2048], replicated
- grad_gen_ff_out: float32 [2048, 128], replicated
- grad_gen_kernel: float32 [128, 196608], P(None, ('dp', 'band'))
- grad_gen_bias: float32 [128, 768], replicated
- grad_pos_table: float32 [196, 768], replicated
- grad_norm_gain: float32 [2, 768], replicated
- grad_norm_bias: float32 [2, 768], replicated
- grad_w_qkv: float32 [768, 2304], P(('dp', 'band'))
- grad_w_out: float32 [768, 768], P(('dp', 'band'))
- grad_w_fc1: float32 [768, 3072], P(('dp', 'band'))
- grad_bias_in: float32 [3072], replicated
- grad_w_fc2: float32 [3072, 768], P(('dp', 'band'))
Inputs may be any that keep to these rules, and one draw needn't show every extreme that they name: `kept`: each row names 64 different patch positions; slots at or after the image's count hold positions that no output reads. `counts`: slots of an image at or after its count are padding; in every draw some image keeps 64 patches.
All inputs are finite; a program needn't handle non-finite values.
Results may differ from a plain program's by a relative error of at most 0.03.
Values may be sent and summed in bfloat16 or wider, within the bound.
No kernel may reach another device: no remote copies, remote signals or barrier semaphores. Data moves between devices by JAX's collectives and lax.ppermute only.
A program may use at most 256 MiB of HBM per device.

v0:
```python
from functools import partial
import math

import jax
import jax.numpy as jnp
from jax import lax
from jax.experimental import pallas as pl
from jax.experimental.pallas import tpu as pltpu
from jax.sharding import PartitionSpec as P

HEADS = 12
HDIM = 64
GEN_HEADS = 4


def inner(left_arr, right_arr):
    return lax.dot_general(
        left_arr, right_arr, (((0,), (0,)), ((), ())), preferred_element_type=jnp.float32
    )


def times_transpose(left_arr, right_arr):
    return lax.dot_general(
        left_arr, right_arr, (((1,), (1,)), ((), ())), preferred_element_type=jnp.float32
    )


def bit_steps(size):
    steps = []
    step = 1
    while step < size:
        steps.append(step)
        step *= 2
    return steps


def swap(values, axis, step):
    size = lax.axis_size(axis)
    return lax.ppermute(values, axis, [(spot, spot ^ step) for spot in range(size)])


def turn(items, by):
    by = by % max(len(items), 1)
    return items[by:] + items[:by]


def gather_core(blocks):
    return [([key ^ 1 for key in keys], swap(block, "dp", 1)) for keys, block in blocks]


def place(blocks, axis, at):
    spot = lax.axis_index(axis)
    first = blocks[0][1]
    count = sum(len(keys) for keys, _ in blocks)
    shape = first.shape[1 : at + 1] + (count,) + first.shape[at + 1 :]
    whole = jnp.zeros(shape, first.dtype)
    for keys, block in blocks:
        for number, key in enumerate(keys):
            whole = lax.dynamic_update_index_in_dim(whole, block[number], spot ^ key, at)
    return whole


def add_low(left_arr, right_arr):
    return (left_arr.astype(jnp.float32) + right_arr.astype(jnp.float32)).astype(left_arr.dtype)


def split_half(values, at, step, left):
    left = sorted(left, reverse=True)
    shape = values.shape
    values = values.reshape(shape[:at] + (2,) * len(left) + shape[at + 1 :])
    dim = at + left.index(step)
    bit = (lax.axis_index("dp") // step) % 2
    rest = shape[:at] + (-1,) + shape[at + 1 :]
    send = lax.dynamic_index_in_dim(values, 1 - bit, dim, keepdims=False)
    keep = lax.dynamic_index_in_dim(values, bit, dim, keepdims=False)
    return send.reshape(rest), keep.reshape(rest)


def together(*arrays):
    return lax.optimization_barrier(arrays)


def column_blocks(matrix, width):
    return [matrix[:, spot : spot + width] for spot in range(0, matrix.shape[1], width)]


def run_kernel(body, args, in_specs, after=(), **options):
    count = len(after)

    def whole(*refs):
        body(*refs[count:])

    return pl.pallas_call(
        whole,
        in_specs=[pl.BlockSpec(memory_space=pl.ANY)] * count + in_specs,
        compiler_params=pltpu.CompilerParams(vmem_limit_bytes=60 * 1024 * 1024),
        cost_estimate=pl.CostEstimate(flops=1000, bytes_accessed=1000, transcendentals=0),
        **options,
    )(*after, *args)


def dot_nn(left_arr, right_arr):
    return lax.dot_general(
        left_arr, right_arr, (((1,), (0,)), ((), ())), preferred_element_type=jnp.float32
    )


def norm_stats(values):
    center = values - jnp.mean(values, axis=-1, keepdims=True)
    spread = jnp.mean(center * center, axis=-1, keepdims=True)
    scale = lax.rsqrt(spread + 1e-06)
    return center * scale, scale


def norm_back(unit, scale, gain, grad):
    weighted = grad * gain
    first = jnp.mean(weighted, axis=-1, keepdims=True)
    second = jnp.mean(weighted * unit, axis=-1, keepdims=True)
    grad_values = (weighted - first - unit * second) * scale
    grad_gain = jnp.sum(grad * unit, axis=0, keepdims=True)
    grad_shift = jnp.sum(grad, axis=0, keepdims=True)
    return grad_values, grad_gain, grad_shift


def stash_spans(width, hidden):
    sizes = {
        "normed": width,
        "mixed": width,
        "normed_two": width,
        "act": hidden,
        "qkv_grad": 3 * width,
        "branch": width,
        "pre_grad": hidden,
        "cot": width,
        "small": width,
    }
    spans = {}
    first = 0
    for name, size in sizes.items():
        spans[name] = (first, size)
        first += size
    return spans


def block_body(part_count, tile_rows, ff_step, keys_lists, *refs):
    part_refs = refs[:part_count]
    weight_count = sum(len(keys_list) for keys_list in keys_lists)
    weight_refs = refs[part_count : part_count + weight_count]
    (
        spot_ref,
        base_ref,
        cot_ref,
        keep_ref,
        mask_ref,
        gain_ref,
        shift_ref,
        bias_ref,
        kept_ref,
        result_ref,
        embed_grad_ref,
        stash_ref,
        sums_ref,
        qkv_w,
        out_w,
        fc_in_w,
        fc_out_w,
        qkv_ref,
        probs_ref,
        total_ref,
        back_ref,
        mixed_grad_ref,
        bias_grad_ref,
        sems,
    ) = refs[part_count + weight_count :]
    bf16 = jnp.bfloat16
    f32 = jnp.float32
    width = base_ref.shape[1]
    hidden = fc_in_w.shape[1]
    spans = stash_spans(width, hidden)
    views = {name: stash_ref.at[:, pl.ds(first, size)] for name, (first, size) in spans.items()}
    normed_ref = views["normed"]
    mixed_ref = views["mixed"]
    normed_two_ref = views["normed_two"]
    act_ref = views["act"]
    qkv_grad_ref = views["qkv_grad"]
    branch_ref = views["branch"]
    pre_grad_ref = views["pre_grad"]
    views["cot"][...] = cot_ref[...]
    share = width // sum(len(keys) for keys in keys_lists[0])
    targets = (
        [(qkv_w, column, share) for column in range(3)]
        + [(out_w, 0, share)]
        + [(fc_in_w, column, share) for column in range(hidden // width)]
        + [(fc_out_w, 0, share * hidden // width)]
    )
    copies = {}
    for number, (target_ref, column, rows) in enumerate(targets):
        half, first = (0, number * share) if number < 6 else (1, (number - 6) * share)
        half_refs = weight_refs[: len(keys_lists[0])] if half == 0 else weight_refs[len(keys_lists[0]) :]
        for keys, weight_ref in zip(keys_lists[half], half_refs):
            for index, key in enumerate(keys):
                at = pl.multiple_of(jnp.bitwise_xor(spot_ref[0], key) * rows, rows)
                copy = pltpu.make_async_copy(
                    weight_ref.at[index, pl.ds(first, rows), :],
                    target_ref.at[pl.ds(at, rows), pl.ds(column * width, width)],
                    sems.at[sum(len(some) for some in copies.values())],
                )
                copy.start()
                copies.setdefault(id(target_ref), []).append(copy)

    def arrive(target_ref):
        for copy in copies[id(target_ref)]:
            copy.wait()

    row_total, width = base_ref.shape
    tiles = row_total // tile_rows
    head_pairs = HEADS // 2
    lanes = 2 * HDIM

    start = base_ref[...]
    for part_ref in part_refs:
        start = start + part_ref[...].astype(f32)
    unit_one, scale_one = norm_stats(start)
    normed = (unit_one * gain_ref[0:1] + shift_ref[0:1]).astype(bf16)
    normed_ref[...] = normed
    arrive(qkv_w)
    for spot in range(3):
        cols = slice(spot * width, (spot + 1) * width)
        qkv_ref[:, cols] = dot_nn(normed, qkv_w[:, cols]).astype(bf16)

    low_lanes = lax.broadcasted_iota(jnp.int32, (tile_rows, lanes), 1) < HDIM

    def half(values, odd):
        keep = jnp.logical_not(low_lanes) if odd else low_lanes
        return jnp.where(keep, values, jnp.zeros_like(values))

    def head_slices(pair, tile):
        rows = pl.ds(tile * tile_rows, tile_rows)
        cols = [
            pl.ds(pl.multiple_of(which * width + pair * lanes, lanes), lanes) for which in range(3)
        ]
        return rows, cols

    def attend(pair, carry):
        for tile in range(tiles):
            rows, cols = head_slices(pair, tile)
            queries, keys_arr, values_arr = [qkv_ref[rows, col] for col in cols]
            mixed = jnp.zeros((tile_rows, lanes), f32)
            for odd in range(2):
                scores = times_transpose(half(queries, odd), keys_arr) * HDIM ** (-0.5)
                scores = scores + mask_ref[tile]
                exponent = jnp.exp(scores - jnp.max(scores, axis=-1, keepdims=True))
                probs = exponent * (1.0 / jnp.sum(exponent, axis=-1, keepdims=True))
                probs_ref[(pair * 2 + odd) * tiles + tile] = probs
                mixed = mixed + dot_nn(probs.astype(bf16), half(values_arr, odd))
            mixed_ref[rows, cols[0]] = mixed.astype(bf16)
        return carry

    lax.fori_loop(0, head_pairs, attend, 0)
    arrive(out_w)
    middle = start + dot_nn(mixed_ref[...], out_w[...])
    unit_two, scale_two = norm_stats(middle)
    normed_two = (unit_two * gain_ref[1:2] + shift_ref[1:2]).astype(bf16)
    normed_two_ref[...] = normed_two
    total_ref[...] = middle
    back_ref[...] = jnp.zeros_like(back_ref)
    arrive(fc_in_w)
    arrive(fc_out_w)

    def feed(step, carry):
        cols = pl.ds(pl.multiple_of(step * ff_step, ff_step), ff_step)
        pre = dot_nn(normed_two_ref[...], fc_in_w[:, cols]) + bias_ref[:, cols]
        cdf = 0.5 * (1.0 + lax.erf(pre * 0.5**0.5))
        act = (pre * cdf).astype(bf16)
        act_ref[:, cols] = act
        slope = cdf + pre * (jnp.exp(-0.5 * pre * pre) * (2.0 * math.pi) ** (-0.5))
        pre_grad = slope * times_transpose(cot_ref[...], fc_out_w[cols, :])
        pre_grad = pre_grad.astype(bf16)
        pre_grad_ref[:, cols] = pre_grad
        bias_grad_ref[:, cols] = jnp.sum(pre_grad.astype(f32), axis=0, keepdims=True)
        total_ref[...] += dot_nn(act, fc_out_w[cols, :])
        back_ref[...] += times_transpose(pre_grad, fc_in_w[:, cols])
        return carry

    lax.fori_loop(0, fc_in_w.shape[1] // ff_step, feed, 0)
    result_ref[...] = (total_ref[...] * keep_ref[...]).astype(bf16)
    grad_norm, gain_two, shift_two = norm_back(unit_two, scale_two, gain_ref[1:2], back_ref[...])
    grad_middle = cot_ref[...].astype(f32) + grad_norm
    grad_branch = grad_middle.astype(bf16)
    branch_ref[...] = grad_branch
    mixed_grad_ref[...] = times_transpose(grad_branch, out_w[...]).astype(bf16)

    def attend_back(pair, carry):
        for tile in range(tiles):
            rows, cols = head_slices(pair, tile)
            queries, keys_arr, values_arr = [qkv_ref[rows, col] for col in cols]
            grad_mixed = mixed_grad_ref[rows, cols[0]]
            grads = [jnp.zeros((tile_rows, lanes), f32) for _ in range(3)]
            for odd in range(2):
                probs = probs_ref[(pair * 2 + odd) * tiles + tile]
                own_grad = half(grad_mixed, odd)
                grad_probs = times_transpose(own_grad, values_arr)
                grad_scores = probs * (
                    grad_probs - jnp.sum(grad_probs * probs, axis=-1, keepdims=True)
                )
                grad_scores = grad_scores.astype(bf16)
                grads[0] = grads[0] + dot_nn(grad_scores, half(keys_arr, odd))
                grads[1] = grads[1] + inner(grad_scores, half(queries, odd))
                grads[2] = grads[2] + inner(probs.astype(bf16), own_grad)
            for which, factor in enumerate((HDIM ** (-0.5), HDIM ** (-0.5), 1.0)):
                qkv_grad_ref[rows, cols[which]] = (grads[which] * factor).astype(bf16)
        return carry

    lax.fori_loop(0, head_pairs, attend_back, 0)
    back = jnp.zeros((row_total, width), f32)
    for spot in range(3):
        cols = slice(spot * width, (spot + 1) * width)
        back = back + times_transpose(qkv_grad_ref[:, cols], qkv_w[:, cols])
    grad_norm, gain_one, shift_one = norm_back(unit_one, scale_one, gain_ref[0:1], back)
    grad_start = grad_middle + grad_norm
    embed_grad_ref[...] = grad_start.astype(bf16)
    sums = jnp.concatenate(
        [jnp.sum(grad_start, axis=0, keepdims=True), gain_one, gain_two, shift_one, shift_two]
        + [jnp.zeros((3, width), f32)],
        axis=0,
    )
    sums_ref[...] = sums
    small_ref = views["small"]
    positions = small_ref.shape[0] - 16
    spots_at = lax.broadcasted_iota(jnp.int32, (positions, row_total), 0)
    one_hot = jnp.where(spots_at == kept_ref[...], 1.0, 0.0)
    by_position = lax.dot_general(
        one_hot,
        grad_start,
        (((1,), (0,)), ((), ())),
        precision=lax.Precision.HIGHEST,
        preferred_element_type=f32,
    )
    cuts = [bias_grad_ref[:, spot : spot + width] for spot in range(0, hidden, width)]
    cuts.append(jnp.zeros((8 - len(cuts), width), f32))
    small_ref[...] = jnp.concatenate([by_position, sums, *cuts], axis=0).astype(bf16)


def block(parts, weight_halves, spots, base, cot, keep, mask, gains, shifts, bias, kept):
    row_total, width = base.shape
    tile_rows = mask.shape[1]
    hidden = bias.shape[1]
    bf16 = jnp.bfloat16
    f32 = jnp.float32
    keys_lists = [[keys for keys, _ in blocks] for blocks in weight_halves]
    weight_args = [block for blocks in weight_halves for _, block in blocks]
    pieces = sum(len(keys) for keys in keys_lists[0])
    inside = pl.BlockSpec(memory_space=pltpu.VMEM)
    outside = pl.BlockSpec(memory_space=pl.ANY)
    rows = (row_total, width)
    shapes = [
        (rows, bf16),
        (rows, bf16),
        ((row_total, sum(stash_spans(width, hidden)["small"])), bf16),
        ((8, width), f32),
    ]
    return run_kernel(
        partial(block_body, len(parts), tile_rows, 512, keys_lists),
        (*parts, *weight_args, spots, base, cot, keep, mask, gains, shifts, bias, kept),
        [inside] * len(parts)
        + [outside] * len(weight_args)
        + [pl.BlockSpec(memory_space=pltpu.SMEM)]
        + [inside] * 8,
        out_shape=[jax.ShapeDtypeStruct(shape, kind) for shape, kind in shapes],
        out_specs=[inside] * len(shapes),
        scratch_shapes=[
            pltpu.VMEM((width, 3 * width), bf16),
            pltpu.VMEM((width, width), bf16),
            pltpu.VMEM((width, hidden), bf16),
            pltpu.VMEM((hidden, width), bf16),
            pltpu.VMEM((row_total, 3 * width), bf16),
            pltpu.VMEM((HEADS * row_total // tile_rows, tile_rows, tile_rows), f32),
            pltpu.VMEM(rows, f32),
            pltpu.VMEM(rows, f32),
            pltpu.VMEM(rows, bf16),
            pltpu.VMEM((1, hidden), f32),
            pltpu.SemaphoreType.DMA(((5 + hidden // width) * pieces,)),
        ],
    )


def dot_full(left_arr, right_arr, left_dim=1, right_dim=0):
    return lax.dot_general(
        left_arr,
        right_arr,
        (((left_dim,), (right_dim,)), ((), ())),
        precision=lax.Precision.HIGHEST,
        preferred_element_type=jnp.float32,
    )


def head_part(values, head):
    size = values.shape[1] // GEN_HEADS
    lane = lax.broadcasted_iota(jnp.int32, values.shape, 1)
    inside = jnp.logical_and(lane >= head * size, lane < (head + 1) * size)
    return jnp.where(inside, values, 0.0)


def generate_body(
    waves_ref,
    token_ref,
    attn_hbm,
    gain_hbm,
    ff_in_hbm,
    ff_out_hbm,
    bias_w_hbm,
    columns_hbm,
    kernel_ref,
    embed_bias_ref,
    low_ref,
    states_ref,
    rows_ref,
    weights_ref,
    pre_ref,
    scales_ref,
    attn_ref,
    gain_ref,
    ff_in_ref,
    ff_out_ref,
    bias_w_ref,
    columns_ref,
    sems,
):
    f32 = jnp.float32
    copies = [
        pltpu.make_async_copy(source, target, sems.at[number])
        for number, (source, target) in enumerate(
            (
                (attn_hbm, attn_ref),
                (gain_hbm, gain_ref),
                (ff_in_hbm, ff_in_ref),
                (ff_out_hbm, ff_out_ref),
                (columns_hbm, columns_ref),
                (bias_w_hbm, bias_w_ref),
            )
        )
    ]
    for copy in copies:
        copy.start()
    bands = waves_ref.shape[1]
    width = token_ref.shape[1]
    padded = rows_ref.shape[1]
    square = (bands, bands)
    diagonal = lax.broadcasted_iota(jnp.int32, square, 0) == lax.broadcasted_iota(
        jnp.int32, square, 1
    )
    waves = jnp.broadcast_to(waves_ref[...].astype(f32), square)
    column = jnp.sum(jnp.where(diagonal, waves, 0.0), axis=1, keepdims=True)
    lane = lax.broadcasted_iota(jnp.int32, (bands, width), 1)
    half_width = width // 2
    number = jnp.where(lane < half_width, lane, lane - half_width).astype(f32)
    angles = column * jnp.exp(number * (-math.log(10000.0) / half_width))
    wave = jnp.where(lane < half_width, jnp.sin(angles), jnp.cos(angles))
    sequence = jnp.concatenate(
        [wave, token_ref[...].astype(f32), jnp.zeros((padded - bands - 1, width), f32)], axis=0
    )
    rows_ref[0] = sequence
    copies[0].wait()
    copies[1].wait()
    for which in range(3):
        rows_ref[1 + which] = dot_full(sequence, attn_ref[which].astype(f32))
    queries = rows_ref[1]
    keys_arr = rows_ref[2]
    values_arr = rows_ref[3]
    key_spot = lax.broadcasted_iota(jnp.int32, (padded, padded), 1)
    mixed = jnp.zeros((padded, width), f32)
    for head in range(GEN_HEADS):
        scores = dot_full(head_part(queries, head), keys_arr, 1, 1)
        scores = scores * (1.0 / math.sqrt(width // GEN_HEADS))
        scores = jnp.where(key_spot <= bands, scores, -1e30)
        exponent = jnp.exp(scores - jnp.max(scores, axis=-1, keepdims=True))
        weights = exponent / jnp.sum(exponent, axis=-1, keepdims=True)
        weights_ref[head] = weights
        mixed = mixed + dot_full(weights, head_part(values_arr, head))
    rows_ref[4] = mixed
    unit_one, scale_one = norm_stats(sequence + dot_full(mixed, attn_ref[3].astype(f32)))
    rows_ref[5] = unit_one
    first = unit_one * gain_ref[0:1].astype(f32)
    copies[2].wait()
    pre = dot_full(first, ff_in_ref[...].astype(f32))
    pre_ref[...] = pre
    hidden = pre * (0.5 * (1.0 + lax.erf(pre * 0.5**0.5)))
    copies[3].wait()
    unit_two, scale_two = norm_stats(first + dot_full(hidden, ff_out_ref[...].astype(f32)))
    rows_ref[6] = unit_two
    states = unit_two * gain_ref[1:2].astype(f32)
    states_ref[...] = states
    scales_ref[0] = jnp.broadcast_to(scale_one, (padded, width))
    scales_ref[1] = jnp.broadcast_to(scale_two, (padded, width))
    low = states[:bands].astype(jnp.bfloat16)
    low_ref[...] = low
    features = kernel_ref.shape[2]
    copies[4].wait()
    for pixel in range(kernel_ref.shape[0]):
        cols = slice(pixel * features, (pixel + 1) * features)
        kernel_ref[pixel] = dot_nn(low, columns_ref[:, cols]).astype(jnp.bfloat16)
    copies[5].wait()
    token_state = states[bands : bands + 8]
    embed_bias_ref[...] = dot_full(token_state, bias_w_ref[...].astype(f32))


def generate_fast(wavelengths, token, gen_attn, gen_gain, ff_in, ff_out, gen_bias, columns):
    f32 = jnp.float32
    bf16 = jnp.bfloat16
    bands = wavelengths.shape[0]
    width = token.shape[0]
    padded = -(-(bands + 1) // 8) * 8
    features = gen_bias.shape[1]
    shapes = [
        ((columns.shape[1] // features, bands, features), bf16),
        ((8, features), f32),
        ((bands, width), bf16),
        ((padded, width), f32),
        ((7, padded, width), f32),
        ((GEN_HEADS, padded, padded), f32),
        ((padded, ff_in.shape[1]), f32),
        ((2, padded, width), f32),
    ]
    inside = pl.BlockSpec(memory_space=pltpu.VMEM)
    outside = pl.BlockSpec(memory_space=pl.ANY)
    weights = (gen_attn, gen_gain, ff_in, ff_out, gen_bias, columns)
    return run_kernel(
        generate_body,
        (wavelengths[None], token[None], *weights),
        out_shape=[jax.ShapeDtypeStruct(shape, kind) for shape, kind in shapes],
        in_specs=[inside] * 2 + [outside] * 6,
        out_specs=[inside] * len(shapes),
        scratch_shapes=[pltpu.VMEM(weight.shape, bf16) for weight in weights]
        + [pltpu.SemaphoreType.DMA((6,))],
    )


def generate_back_body(
    tail_ref,
    attn_ref,
    gain_ref,
    ff_in_ref,
    ff_out_ref,
    bias_w_ref,
    states_ref,
    rows_ref,
    weights_ref,
    pre_ref,
    scales_ref,
    token_out,
    attn_out,
    gain_out,
    ff_in_out,
    ff_out_out,
    bias_out,
):
    f32 = jnp.float32
    padded, width = states_ref.shape
    features = bias_w_ref.shape[1]
    bands = padded - 8
    head_scale = 1.0 / math.sqrt(width // GEN_HEADS)
    cuts = [tail_ref[bands + spot : bands + spot + 1, :] for spot in range(features // width)]
    bias_grad = jnp.concatenate(cuts, axis=1)
    bias_grad = jnp.concatenate([bias_grad, jnp.zeros((7, features), f32)], axis=0)
    row_spot = lax.broadcasted_iota(jnp.int32, (padded - bands, width), 0)
    token_grad = dot_full(bias_grad, bias_w_ref[...].astype(f32), 1, 1)
    token_grad = jnp.where(row_spot == 0, token_grad[0:1], 0.0)
    grad_states = jnp.concatenate([tail_ref[:bands, :], token_grad], axis=0)
    token_state = states_ref[bands : bands + 8]
    first_row = lax.broadcasted_iota(jnp.int32, token_state.shape, 0) == 0
    bias_out[...] = dot_full(jnp.where(first_row, token_state, 0.0), bias_grad, 0, 0)
    unit_one = rows_ref[5]
    gain_one = gain_ref[0:1].astype(f32)
    gain_two = gain_ref[1:2].astype(f32)
    grad_two, gain_two_grad, _ = norm_back(rows_ref[6], scales_ref[1], gain_two, grad_states)
    pre = pre_ref[...]
    cdf = 0.5 * (1.0 + lax.erf(pre * 0.5**0.5))
    ff_out_out[...] = dot_full(pre * cdf, grad_two, 0, 0)
    slope = cdf + pre * (jnp.exp(-0.5 * pre * pre) * (2.0 * math.pi) ** (-0.5))
    grad_pre = slope * dot_full(grad_two, ff_out_ref[...].astype(f32), 1, 1)
    ff_in_out[...] = dot_full(unit_one * gain_one, grad_pre, 0, 0)
    grad_first = grad_two + dot_full(grad_pre, ff_in_ref[...].astype(f32), 1, 1)
    grad_one, gain_one_grad, _ = norm_back(unit_one, scales_ref[0], gain_one, grad_first)
    gain_out[...] = jnp.concatenate([gain_one_grad, gain_two_grad], axis=0)
    attn_out[3] = dot_full(rows_ref[4], grad_one, 0, 0)
    grad_mixed = dot_full(grad_one, attn_ref[3].astype(f32), 1, 1)
    sequence = rows_ref[0]
    queries = rows_ref[1]
    keys_arr = rows_ref[2]
    values_arr = rows_ref[3]
    grads = [jnp.zeros((padded, width), f32) for _ in range(3)]
    for head in range(GEN_HEADS):
        weights = weights_ref[head]
        own_grad = head_part(grad_mixed, head)
        grad_weights = dot_full(own_grad, values_arr, 1, 1)
        grad_scores = weights * (
            grad_weights - jnp.sum(grad_weights * weights, axis=-1, keepdims=True)
        )
        grad_scores = grad_scores * head_scale
        grads[0] = grads[0] + dot_full(grad_scores, head_part(keys_arr, head))
        grads[1] = grads[1] + dot_full(grad_scores, head_part(queries, head), 0, 0)
        grads[2] = grads[2] + dot_full(weights, own_grad, 0, 0)
    grad_sequence = grad_one
    for which in range(3):
        attn_out[which] = dot_full(sequence, grads[which], 0, 0)
        grad_sequence = grad_sequence + dot_full(
            grads[which], attn_ref[which].astype(f32), 1, 1
        )
    token_out[...] = grad_sequence[bands : bands + 1]


def generate_back(tail, gen_attn, gen_gain, ff_in, ff_out, gen_bias, kept_arrs):
    f32 = jnp.float32
    width = gen_gain.shape[1]
    shapes = [
        (1, width),
        gen_attn.shape,
        gen_gain.shape,
        ff_in.shape,
        ff_out.shape,
        gen_bias.shape,
    ]
    inside = pl.BlockSpec(memory_space=pltpu.VMEM)
    return run_kernel(
        generate_back_body,
        (tail, gen_attn, gen_gain, ff_in, ff_out, gen_bias, *kept_arrs),
        out_shape=[jax.ShapeDtypeStruct(shape, f32) for shape in shapes],
        in_specs=[inside] * (6 + len(kept_arrs)),
        out_specs=[inside] * len(shapes),
    )


def fill_kernel(keys_lists, piece_refs, spot, mat_ref, bands, pixels):
    for keys, piece_ref in zip(keys_lists, piece_refs):
        for number, key in enumerate(keys):
            share = piece_ref.shape[2]
            first = jnp.bitwise_xor(spot, key) * share
            for band in range(bands):
                rows = pl.ds(pl.multiple_of(band * pixels + first, share), share)
                mat_ref[rows, :] = piece_ref[number, band]


def fill_step(keys_lists, piece_refs, spot, mat_ref, band_step, group_steps):
    pixels = mat_ref.shape[0] // band_step
    step = pl.program_id(0)
    used = 0
    for group, keys_list in enumerate(keys_lists):
        group_refs = piece_refs[used : used + len(keys_list)]
        used += len(keys_list)

        @pl.when(step // group_steps == group)
        def _(keys_list=keys_list, group_refs=group_refs):
            fill_kernel(keys_list, group_refs, spot, mat_ref, band_step, pixels)


def embed_body(keys_lists, group_steps, band_step, *refs):
    spot_ref, patch_ref = refs[:2]
    count = sum(len(keys_list) for keys_list in keys_lists)
    piece_refs = refs[2 : 2 + count]
    *out_refs, mat_ref, total_ref = refs[2 + count :]
    step = pl.program_id(0)
    fill_step(keys_lists, piece_refs, spot_ref[0], mat_ref, band_step, group_steps)

    @pl.when(step == 0)
    def _():
        total_ref[...] = jnp.zeros_like(total_ref)

    total_ref[...] += dot_nn(patch_ref[...], mat_ref[...])

    @pl.when(step == pl.num_programs(0) - 1)
    def _():
        for key, out_ref in enumerate(out_refs):
            rows = out_ref.shape[0]
            first = pl.multiple_of(jnp.bitwise_xor(spot_ref[1], key) * rows, rows)
            out_ref[...] = total_ref[pl.ds(first, rows), :].astype(out_ref.dtype)


def group_band_count(kernel_groups):
    return min(block.shape[1] for blocks in kernel_groups for _, block in blocks)


def piece_specs(kernel_groups, band_step):
    group_steps = group_band_count(kernel_groups) // band_step
    specs = []
    arrays = []
    for group, blocks in enumerate(kernel_groups):
        for keys, block in blocks:
            whole = block.shape[1] > group_steps * band_step
            first = group * group_steps

            def pick(step, first=first, whole=whole):
                here = jnp.clip(step - first, 0, group_steps - 1)
                return (0, here + first if whole else here, 0, 0)

            specs.append(pl.BlockSpec((len(keys), band_step) + block.shape[2:], pick))
            arrays.append(block)
    keys_lists = [[keys for keys, _ in blocks] for blocks in kernel_groups]
    return specs, arrays, keys_lists, group_steps


def embed_share(spots, patch_rows, kernel_groups, owners):
    row_total = patch_rows.shape[0]
    blocks = kernel_groups[0]
    group_bands = group_band_count(kernel_groups)
    width = blocks[0][1].shape[3]
    pixels = sum(len(keys) for keys, _ in blocks) * blocks[0][1].shape[2]
    band_step = min(4, group_bands)
    depth = band_step * pixels
    specs, arrays, keys_lists, group_steps = piece_specs(kernel_groups, band_step)
    rows = row_total // owners
    return run_kernel(
        partial(embed_body, keys_lists, group_steps, band_step),
        [spots, patch_rows, *arrays],
        [
            pl.BlockSpec(memory_space=pltpu.SMEM),
            pl.BlockSpec((row_total, depth), lambda step: (0, step)),
        ]
        + specs,
        grid=(group_steps * len(kernel_groups),),
        out_shape=[jax.ShapeDtypeStruct((rows, width), jnp.bfloat16)] * owners,
        out_specs=[pl.BlockSpec((rows, width), lambda step: (0, 0))] * owners,
        scratch_shapes=[
            pltpu.VMEM((depth, width), jnp.bfloat16),
            pltpu.VMEM((row_total, width), jnp.float32),
        ],
    )


def kernel_grad_body(dp_size, band_step, *refs):
    spot_ref, patch_ref = refs[:2]
    *grad_refs, first_ref, last_ref, keep_ref, hold_ref = refs[2:]
    rows = grad_refs[0].shape[0]
    total = 0.0
    for key, grad_ref in enumerate(grad_refs):
        first = pl.multiple_of(jnp.bitwise_xor(spot_ref[1], key) * rows, rows)
        total = total + inner(patch_ref[pl.ds(first, rows), :], grad_ref[...])
    hold_ref[...] = total.astype(hold_ref.dtype)
    pixels = hold_ref.shape[0] // band_step
    share = pixels // dp_size
    core = lax.rem(spot_ref[0], 2)
    for band in range(band_step):
        for chip in range(dp_size // 2):
            base = band * pixels + chip * 2 * share
            kept = pl.multiple_of(base + core * share, share)
            keep_ref[band, chip] = hold_ref[pl.ds(kept, share), :]

    half = pl.num_programs(0) // 2
    for number, send_ref in enumerate((first_ref, last_ref)):

        @pl.when(pl.program_id(0) // half == number)
        def _(send_ref=send_ref):
            for band in range(band_step):
                for chip in range(dp_size // 2):
                    base = band * pixels + chip * 2 * share
                    sent = pl.multiple_of(base + (1 - core) * share, share)
                    send_ref[band, chip] = hold_ref[pl.ds(sent, share), :]


def kernel_grad_part(spots, patch_rows, grads, first_band, group_bands, bands_dev, dp_size, after):
    row_total = patch_rows.shape[0]
    width = grads[0].shape[1]
    band_step = min(2, group_bands // 2)
    pixels = patch_rows.shape[1] // bands_dev
    depth = band_step * pixels
    offset = first_band // band_step
    share = pixels // dp_size
    chips = (dp_size // 2, share, width)
    steps = group_bands // band_step
    block = (band_step,) + chips
    return run_kernel(
        partial(kernel_grad_body, dp_size, band_step),
        (spots, patch_rows, *grads),
        after=after,
        grid=(steps,),
        out_shape=[
            jax.ShapeDtypeStruct((bands,) + chips, jnp.bfloat16)
            for bands in (group_bands // 2, group_bands // 2, group_bands)
        ],
        in_specs=[
            pl.BlockSpec(memory_space=pltpu.SMEM),
            pl.BlockSpec((row_total, depth), lambda step: (0, offset + step)),
        ]
        + [pl.BlockSpec(grad.shape, lambda step: (0, 0)) for grad in grads],
        out_specs=[
            pl.BlockSpec(block, lambda step: (jnp.minimum(step, steps // 2 - 1), 0, 0, 0)),
            pl.BlockSpec(block, lambda step: (jnp.maximum(step - steps // 2, 0), 0, 0, 0)),
            pl.BlockSpec(block, lambda step: (step, 0, 0, 0)),
        ],
        scratch_shapes=[pltpu.VMEM((depth, width), jnp.bfloat16)],
    )


def patch_grad_body(keys_lists, grad_count, group_steps, band_step, *refs):
    spot_ref = refs[0]
    grad_refs = refs[1 : 1 + grad_count]
    out_ref, mat_ref = refs[-2:]
    piece_refs = refs[1 + grad_count : -2]
    fill_step(keys_lists, piece_refs, spot_ref[0], mat_ref, band_step, group_steps)
    for key, grad_ref in enumerate(grad_refs):
        rows = grad_ref.shape[0]
        first = pl.multiple_of(jnp.bitwise_xor(spot_ref[1], key) * rows, rows)
        out_ref[pl.ds(first, rows), :] = times_transpose(grad_ref[...], mat_ref[...]).astype(
            out_ref.dtype
        )


def patch_grad(spots, grads, kernel_groups, pixels, after):
    rows, width = grads[0].shape
    row_total = rows * len(grads)
    band_step = min(4, group_band_count(kernel_groups))
    depth = band_step * pixels
    specs, arrays, keys_lists, group_steps = piece_specs(kernel_groups, band_step)
    steps = group_steps * len(kernel_groups)
    return run_kernel(
        partial(patch_grad_body, keys_lists, len(grads), group_steps, band_step),
        [spots, *grads, *arrays],
        [pl.BlockSpec(memory_space=pltpu.SMEM)]
        + [pl.BlockSpec(grad.shape, lambda step: (0, 0)) for grad in grads]
        + specs,
        after=after,
        grid=(steps,),
        out_shape=jax.ShapeDtypeStruct((row_total, steps * depth), jnp.bfloat16),
        out_specs=pl.BlockSpec((row_total, depth), lambda step: (0, step)),
        scratch_shapes=[pltpu.VMEM((depth, width), jnp.bfloat16)],
    )


def states_grad_body(batches, low_ref, columns_ref, *refs):
    *piece_refs, sums_ref, spot_ref, grad_ref, part_ref, hold_ref = refs
    pixels, bands, width = piece_refs[0].shape
    for number, piece_ref in enumerate(piece_refs):
        key, batch = divmod(number, batches)
        first = (jnp.bitwise_xor(spot_ref[1], key) * batches + batch) * bands
        hold_ref[:, pl.ds(pl.multiple_of(first, bands), bands), :] = piece_ref[...]
    total = 0.0
    for pixel in range(pixels):
        cols = slice(pixel * width, (pixel + 1) * width)
        grads = hold_ref[pixel]
        grad_ref[:, cols] = inner(low_ref[...], grads)
        total = total + times_transpose(grads, columns_ref[:, cols])
    bands, states = total.shape
    part_ref[:bands, :] = total
    rows = [sums_ref[0:1, spot : spot + states] for spot in range(0, width, states)]
    rows.append(jnp.zeros((part_ref.shape[0] - bands - len(rows), states), jnp.float32))
    part_ref[bands:, :] = jnp.concatenate(rows, axis=0)


def states_grad(spots, low, columns, pieces, sums):
    pixels, bands, width = pieces[0].shape
    tail_rows = low.shape[0] + -(-width // low.shape[1] // 8) * 8
    if bands % 16:
        blocks = [([key], piece[None]) for key, piece in enumerate(pieces)]
        whole = place(blocks, "band", 1).reshape(pixels, -1, width)
        grads = whole.transpose(1, 0, 2).reshape(low.shape[0], -1)
        rows = [times_transpose(grads, columns), sums[0].reshape(-1, low.shape[1])]
        tail = jnp.concatenate(rows, axis=0)
        tail = jnp.pad(tail, ((0, tail_rows - tail.shape[0]), (0, 0)))
        return inner(low, grads), tail
    inside = pl.BlockSpec(memory_space=pltpu.VMEM)
    return run_kernel(
        partial(states_grad_body, 1),
        (low, columns, *pieces, sums, spots),
        out_shape=[
            jax.ShapeDtypeStruct(columns.shape, jnp.float32),
            jax.ShapeDtypeStruct((tail_rows, low.shape[1]), jnp.float32),
        ],
        in_specs=[inside] * (3 + len(pieces)) + [pl.BlockSpec(memory_space=pltpu.SMEM)],
        out_specs=[inside, inside],
        scratch_shapes=[pltpu.VMEM((pixels, bands * len(pieces), width), jnp.bfloat16)],
    )


def flatten_body(in_ref, out_ref):
    out_ref[...] = in_ref[...].reshape(out_ref.shape)


def flatten_rows(cube, after):
    rows, bands, pixels = cube.shape
    step_rows = 64
    return run_kernel(
        flatten_body,
        (cube,),
        [pl.BlockSpec((step_rows, bands, pixels), lambda step: (step, 0, 0))],
        after=after,
        grid=(rows // step_rows,),
        out_shape=jax.ShapeDtypeStruct((rows, bands * pixels), cube.dtype),
        out_specs=pl.BlockSpec((step_rows, bands * pixels), lambda step: (step, 0)),
    )


def unflatten_rows(flat, bands, after):
    rows, depth = flat.shape
    step_rows = 64
    return run_kernel(
        flatten_body,
        (flat,),
        [pl.BlockSpec((step_rows, depth), lambda step: (step, 0))],
        after=after,
        grid=(rows // step_rows,),
        out_shape=jax.ShapeDtypeStruct((rows, bands, depth // bands), flat.dtype),
        out_specs=pl.BlockSpec((step_rows, bands, depth // bands), lambda step: (step, 0, 0)),
    )


def stack_body(*refs):
    *part_refs, out_ref, hold_ref = refs
    width = out_ref.shape[1]
    first = 0
    for part_ref in part_refs:
        rows = part_ref.shape[0]
        for spot in range(0, part_ref.shape[1], width):
            hold_ref[pl.ds(first, rows), :] = part_ref[:, spot : spot + width].astype(jnp.float32)
            first += rows
    out_ref[...] = hold_ref[...].astype(out_ref.dtype)


def stack_weights(shards_in):
    width = shards_in[-1].shape[1]
    if any(shard.shape[0] % 8 for shard in shards_in):
        return jnp.concatenate(
            [part for shard in shards_in for part in column_blocks(shard, width)], axis=0
        )
    row_total = sum(shard.size for shard in shards_in) // width
    inside = pl.BlockSpec(memory_space=pltpu.VMEM)
    return run_kernel(
        stack_body,
        shards_in,
        [inside] * len(shards_in),
        out_shape=jax.ShapeDtypeStruct((row_total, width), shards_in[0].dtype),
        out_specs=inside,
        scratch_shapes=[pltpu.VMEM((row_total, width), jnp.float32)],
    )


def plane_body(block_rows, spot_ref, *refs):
    *stack_refs, first_ref, last_ref, hold_ref = refs
    band_size = len(stack_refs)
    for key, stack_ref in enumerate(stack_refs):
        owner = jnp.bitwise_xor(spot_ref[1], key)
        values = stack_ref[...].astype(jnp.float32)
        done = 0
        for rows in block_rows:
            at = pl.multiple_of(done * band_size + owner * rows, 8)
            hold_ref[pl.ds(at, rows), :] = values[done : done + rows]
            done += rows
    half = first_ref.shape[0]
    first_ref[...] = hold_ref[:half, :].astype(first_ref.dtype)
    last_ref[...] = hold_ref[half:, :].astype(last_ref.dtype)


def plane_weights(spots, stacks, block_rows):
    row_total, width = stacks[0].shape
    band_size = len(stacks)
    half = row_total * band_size // 2
    if any(rows % 8 for rows in block_rows):
        whole = place([([key], stack[None]) for key, stack in enumerate(stacks)], "band", 0)
        parts = []
        done = 0
        for rows in block_rows:
            parts.append(whole[:, done : done + rows].reshape(-1, width))
            done += rows
        merged = jnp.concatenate(parts, axis=0)
        return merged[:half], merged[half:]
    inside = pl.BlockSpec(memory_space=pltpu.VMEM)
    return run_kernel(
        partial(plane_body, block_rows),
        (spots, *stacks),
        [pl.BlockSpec(memory_space=pltpu.SMEM)] + [inside] * band_size,
        out_shape=[jax.ShapeDtypeStruct((half, width), stacks[0].dtype)] * 2,
        out_specs=[inside] * 2,
        scratch_shapes=[pltpu.VMEM((row_total * band_size, width), jnp.float32)],
    )


def weight_grad_body(dp_size, first_steps, hidden, spot_ref, own_ref, other_ref, *refs):
    *out_refs, turned_ref, hold_ref, feed_ref, small_ref, sems = refs
    width = hold_ref.shape[2]
    row_total = own_ref.shape[0]
    spans = stash_spans(width, hidden)
    share = width // dp_size
    chips = dp_size // 2
    core = lax.rem(spot_ref[0], 2)
    copies = []

    def view(name, column=0, size=None):
        first, whole = spans[name]
        first = first + column * width
        return [ref[:, first : first + (size or whole)] for ref in (own_ref, other_ref)]

    def turn_rows(name, at):
        first, size = spans[name]
        for spot in range(0, size, width):
            for number, ref in enumerate((own_ref, other_ref)):
                cols = slice(number * row_total, (number + 1) * row_total)
                turned = ref[:, first + spot : first + spot + width].T
                turned_ref[at + spot : at + spot + width, cols] = turned

    def pick(at, rows):
        parts = []
        for chip in range(chips):
            first = at + (chip * 2 + core) * rows
            parts.append(turned_ref[pl.ds(pl.multiple_of(first, 16), rows), :])
        return jnp.concatenate(parts, axis=0)

    def send(source_ref, rows, half, first, stride=None):
        step = first_steps[half] // 2
        bit = lax.rem(lax.div(spot_ref[0], first_steps[half]), 2)
        for index in range(chips // 2):
            for which in range(2):
                own_bit = bit if which == 0 else 1 - bit
                chip = index // step * 2 * step + own_bit * step + index % step
                at = chip * (stride or rows)
                copy = pltpu.make_async_copy(
                    source_ref.at[pl.ds(pl.multiple_of(at, 16), rows), :],
                    out_refs[half * 2 + which].at[index, pl.ds(first, rows), :],
                    sems.at[len(copies)],
                )
                copy.start()
                copies.append(copy)

    def product(left, names, column):
        right = view(names, column, width)
        total = dot_nn(left[:, :row_total], right[0])
        return total + dot_nn(left[:, row_total:], right[1])

    blocks = (
        [("normed", "qkv_grad", column) for column in range(3)]
        + [("mixed", "branch", 0)]
        + [("normed_two", "pre_grad", column) for column in range(hidden // width)]
    )
    turned_at = {"normed": 0, "mixed": width, "normed_two": 2 * width, "act": 3 * width}
    picked = {}
    for number, (left, right, column) in enumerate(blocks):
        if left not in picked:
            turn_rows(left, turned_at[left])
            picked = {left: pick(turned_at[left], share)}
        hold_ref[number] = product(picked[left], right, column).astype(hold_ref.dtype)
        send(hold_ref.at[number], share, number // 6, number % 6 * share)
    small = sum(part.astype(jnp.float32) for part in view("small"))
    small_ref[...] = small.astype(small_ref.dtype)
    small_share = row_total // dp_size
    turn_rows("act", turned_at["act"])
    feed_rows = hidden // dp_size
    for chip in range(chips):
        at = turned_at["act"] + (chip * 2 + core) * feed_rows
        left = turned_ref[pl.ds(pl.multiple_of(at, 16), feed_rows), :]
        feed_ref[chip * feed_rows : (chip + 1) * feed_rows, :] = product(left, "cot", 0).astype(
            feed_ref.dtype
        )
    send(feed_ref, feed_rows, 1, (len(blocks) - 6) * share)
    own_small = small_ref.at[pl.ds(pl.multiple_of(core * small_share, 16), (dp_size - 1) * small_share), :]
    send(own_small, small_share, 0, 6 * share, 2 * small_share)
    for copy in copies:
        copy.wait()


def weight_grad(spots, dp_size, first_steps, hidden, own, other):
    row_total, columns = own.shape
    width = (columns - 2 * hidden) // 9
    bf16 = jnp.bfloat16
    blocks = 4 + hidden // width
    chips = dp_size // 2
    share = width // dp_size
    rows = [6 * share + row_total // dp_size, (blocks - 6) * share + hidden // dp_size]
    inside = pl.BlockSpec(memory_space=pltpu.VMEM)
    outside = pl.BlockSpec(memory_space=pl.ANY)
    return run_kernel(
        partial(weight_grad_body, dp_size, first_steps, hidden),
        (spots, own, other),
        [pl.BlockSpec(memory_space=pltpu.SMEM), inside, inside],
        out_shape=[
            jax.ShapeDtypeStruct((chips // 2, rows[half], width), bf16)
            for half in range(2)
            for _ in range(2)
        ],
        out_specs=[outside] * 4,
        scratch_shapes=[
            pltpu.VMEM((3 * width + hidden, 2 * row_total), bf16),
            pltpu.VMEM((blocks, chips * share, width), bf16),
            pltpu.VMEM((hidden // 2, width), bf16),
            pltpu.VMEM((row_total, width), bf16),
            pltpu.SemaphoreType.DMA(((blocks + 2) * chips,)),
        ],
    )


def add_split_body(step, part_steps, spot_ref, keep_ref, *refs):
    *got_refs, send_ref, held_ref = refs
    bit = lax.rem(lax.div(spot_ref[0], step), 2)
    for number, got_ref in enumerate(got_refs):

        @pl.when(pl.program_id(0) // part_steps == number)
        def _(got_ref=got_ref):
            for out_ref, which in ((send_ref, 1 - bit), (held_ref, bit)):
                values = keep_ref[:, which].astype(jnp.float32)
                values = values + got_ref[:, which].astype(jnp.float32)
                out_ref[...] = values.astype(out_ref.dtype)


def add_split(spots, keep, gots, at, step, left):
    left = sorted(left, reverse=True)
    place_of = left.index(step)
    shape = keep.shape
    width = shape[-1]
    outer = math.prod(shape[:at]) * 2**place_of
    part_outer = outer // len(gots)
    inner_rows = keep.size // (outer * 2 * width)
    rows_step = inner_rows
    while rows_step > 320 and rows_step % 32 == 0:
        rows_step //= 2
    outer_step = 1
    while part_outer % (2 * outer_step) == 0 and 2 * outer_step * rows_step <= 320:
        outer_step *= 2
    part_steps = part_outer // outer_step
    block_in = (outer_step, 2, rows_step, width)
    block_out = pl.BlockSpec((outer_step, rows_step, width), lambda first, rows: (first, rows, 0))

    def part_spec(number):
        def pick(first, rows):
            return (jnp.clip(first - number * part_steps, 0, part_steps - 1), 0, rows, 0)

        return pl.BlockSpec(block_in, pick)

    outs = run_kernel(
        partial(add_split_body, step, part_steps),
        (spots, keep.reshape((outer, 2, inner_rows, width)))
        + tuple(got.reshape((part_outer, 2, inner_rows, width)) for got in gots),
        [
            pl.BlockSpec(memory_space=pltpu.SMEM),
            pl.BlockSpec(block_in, lambda first, rows: (first, 0, rows, 0)),
        ]
        + [part_spec(number) for number in range(len(gots))],
        grid=(outer // outer_step, inner_rows // rows_step),
        out_shape=[jax.ShapeDtypeStruct((outer, inner_rows, width), keep.dtype)] * 2,
        out_specs=[block_out] * 2,
    )
    rest = shape[:at] + (-1,) + shape[at + 1 :]
    return outs[0].reshape(rest), outs[1].reshape(rest)


def shards(
    patches,
    bias_token,
    gen_attn,
    gen_gain,
    gen_ff_in,
    gen_ff_out,
    gen_kernel,
    gen_bias,
    pos_table,
    norm_gain,
    norm_bias,
    w_qkv,
    w_out,
    w_fc1,
    bias_in,
    w_fc2,
    wavelengths,
    kept,
    counts,
    cotangent,
):
    group_size, slot_count, bands_dev, pixel_count = patches.shape
    dp_size = lax.axis_size("dp")
    band_size = lax.axis_size("band")
    device_count = dp_size * band_size
    local_images = group_size // band_size
    model_width = w_out.shape[1]
    row_total = local_images * slot_count
    own_pixels = pixel_count // device_count
    share = own_pixels * band_size
    groups = 2
    group_bands = bands_dev // groups
    f32 = jnp.float32
    bf16 = jnp.bfloat16
    spot = lax.axis_index("band")
    spots = jnp.stack([lax.axis_index("dp"), spot]).astype(jnp.int32)

    own_kernel, embed_bias, band_states, *gen_kept = generate_fast(
        wavelengths,
        bias_token,
        gen_attn,
        gen_gain,
        gen_ff_in,
        gen_ff_out,
        gen_bias,
        gen_kernel,
    )
    hidden = w_fc1.shape[1]
    weight_rows = [w_qkv.shape[0]] * (4 + hidden // model_width) + [w_fc2.shape[0]]
    stack = stack_weights((w_qkv, w_out, w_fc1, w_fc2))
    patch_rows = flatten_rows(
        patches.reshape(group_size * slot_count, bands_dev, pixel_count), (own_kernel,)
    )
    own_kernel = own_kernel.reshape(own_pixels, band_size, bands_dev, model_width)
    other_bands = range(1, band_size)
    dp_steps = bit_steps(dp_size)[1:]
    orders = [turn(dp_steps, group) for group in range(groups)]

    sent = [
        lax.dynamic_index_in_dim(own_kernel, spot ^ key, 1, keepdims=False).transpose(1, 0, 2)
        for key in range(band_size)
    ]
    got = [swap(sent[key], "band", key) for key in other_bands]
    *got, patch_rows, stack = together(*got, patch_rows, stack)
    piece = place(
        [([key], block[None]) for key, block in enumerate([sent[0]] + got)], "band", 1
    ).reshape(bands_dev, share, model_width)

    own_pieces = [piece[group * group_bands : (group + 1) * group_bands] for group in range(groups)]
    held = [own_piece[None] for own_piece in own_pieces]
    held_keys = [[0] for _ in range(groups)]
    kernel_groups = [[([0], piece[None])] for _ in range(groups)]
    waiting = []
    stacks = {0: stack}
    stack_keys = [band_size // 2] + [key for key in other_bands if key != band_size // 2]
    for stage in range(len(dp_steps)):
        last = stage == len(dp_steps) - 1
        now_keys = stack_keys if last else stack_keys[:1]
        stack_keys = stack_keys[len(now_keys) :]
        got = [swap(held[group], "dp", orders[group][stage]) for group in range(groups)]
        if stage == 0:
            core_got = swap(piece, "dp", 1)
        elif waiting:
            core_got = swap(waiting[0][2], "dp", 1)
        stack_got = [swap(stack, "band", key) for key in now_keys]
        got[0], got[1], core_got, stack, *stack_got = together(*got, core_got, stack, *stack_got)
        stacks.update(zip(now_keys, stack_got))
        if stage == 0:
            for blocks in kernel_groups:
                blocks.append(([1], core_got[None]))
        elif waiting:
            group, keys, _ = waiting.pop(0)
            kernel_groups[group].append(([key ^ 1 for key in keys], core_got))
        for group in range(groups):
            keys = [key ^ orders[group][stage] for key in held_keys[group]]
            kernel_groups[group].append((keys, got[group]))
            waiting.append((group, keys, got[group]))
            if not last:
                held[group] = jnp.concatenate([held[group], got[group]], axis=0)
                held_keys[group] = held_keys[group] + keys
    for group, keys, last_got in waiting:
        kernel_groups[group].append(([key ^ 1 for key in keys], swap(last_got, "dp", 1)))

    planes = plane_weights(spots, [stacks[key] for key in range(band_size)], weight_rows)
    got = [swap(plane, "dp", orders[half][0]) for half, plane in enumerate(planes)]
    embedded = embed_share(spots, patch_rows, kernel_groups, band_size)
    *embedded, first_got, last_got = together(*embedded, *got)
    held = [
        jnp.concatenate([plane[None], got[None]], axis=0)
        for plane, got in zip(planes, (first_got, last_got))
    ]
    held_keys = [[0, orders[half][0]] for half in range(2)]
    for stage in range(1, len(dp_steps) - 1):
        for half in range(2):
            step = orders[half][stage]
            held[half] = jnp.concatenate([held[half], swap(held[half], "dp", step)], axis=0)
            held_keys[half] = held_keys[half] + [key ^ step for key in held_keys[half]]
    got = [swap(held[half], "dp", orders[half][-1]) for half in range(2)]
    parts = [embedded[0]] + [swap(embedded[key], "band", key) for key in other_bands]
    held[0], held[1], got[0], got[1], *parts = together(*held, *got, *parts)
    weight_halves = []
    for half in range(2):
        blocks = [(held_keys[half], held[half])]
        blocks.append(([key ^ orders[half][-1] for key in held_keys[half]], got[half]))
        weight_halves.append(blocks + gather_core(blocks))

    valid_mask = jnp.arange(slot_count)[None, :] < counts[:, None]
    keep_col = valid_mask.reshape(row_total, 1)
    kept_flat = kept.reshape(row_total)
    pos_rows = jnp.take(pos_table, kept_flat, axis=0).astype(f32)
    base = embed_bias[0:1] + pos_rows
    tile_images = 2 if local_images % 2 == 0 else 1
    tile_rows = tile_images * slot_count
    image_spot = jnp.arange(tile_rows) // slot_count
    same_image = image_spot[:, None] == image_spot[None, :]
    mask = jnp.where(same_image[None] & valid_mask.reshape(-1, 1, tile_rows), 0.0, -1e30)
    cot = jnp.where(keep_col, cotangent.reshape(row_total, model_width), 0)
    (
        result,
        grad_embed,
        stash,
        sums,
    ) = block(
        parts,
        weight_halves,
        spots,
        base,
        cot,
        keep_col.astype(f32),
        mask.astype(f32),
        norm_gain.astype(f32),
        norm_bias.astype(f32),
        bias_in.astype(f32)[None],
        kept_flat[None],
    )

    grads = [grad_embed] + [swap(grad_embed, "band", key) for key in other_bands]
    first_steps = [order[0] for order in orders]
    weight_split = weight_grad(
        spots, dp_size, first_steps, hidden, stash, swap(stash, "dp", 1)
    )
    mixed = together(*grads, *weight_split)
    grads, weight_split = list(mixed[:band_size]), mixed[band_size:]

    weight_got = [
        swap(weight_split[2 * half + 1], "dp", first_steps[half]) for half in range(2)
    ]
    kernel_split = []
    for group in range(groups):
        *sends, keep = kernel_grad_part(
            spots,
            patch_rows,
            grads,
            group * group_bands,
            group_bands,
            bands_dev,
            dp_size,
            (),
        )
        core_got = [swap(send, "dp", 1) for send in sends]
        kernel_split += add_split(spots, keep, core_got, 1, orders[group][0], dp_steps)
    weight_got[0], weight_got[1], *kernel_split = together(*weight_got, *kernel_split)
    weight_sums = [add_low(weight_split[2 * half], weight_got[half]) for half in range(2)]
    small_share = row_total // device_count
    half_rows = [weight_rows[:6] + [small_share], weight_rows[6:]]
    early_blocks = [0, 1, 2, 3, 6]
    late_blocks = [4, 5]

    def cut_blocks(values, rows_list, numbers):
        lead = values.shape[0]
        parts = []
        for number in numbers:
            rows = rows_list[number]
            first = sum(rows_list[:number]) * band_size
            part = values[:, first : first + rows * band_size]
            parts.append(part.reshape(lead, band_size, rows, model_width))
        return parts

    def over_band(by_band):
        sent = [
            lax.dynamic_index_in_dim(by_band, spot ^ key, 1, keepdims=False)
            for key in range(band_size)
        ]
        return [sent[0]] + [swap(sent[key], "band", key) for key in other_bands]

    def total(blocks):
        return sum(block_sum.astype(f32) for block_sum in blocks)

    def over_chips(values, order, first=0):
        for stage in range(first, len(order)):
            send, keep = split_half(values, 0, order[stage], order[stage:])
            values = add_low(keep, swap(send, "dp", order[stage]))
        return values

    update = patch_grad(spots, grads, kernel_groups, pixel_count, ())
    for stage in range(len(dp_steps)):
        last = stage == len(dp_steps) - 1
        got = [swap(kernel_split[2 * group], "dp", orders[group][stage]) for group in range(groups)]
        if stage == 0:
            early = cut_blocks(weight_sums[0], half_rows[0], early_blocks)
            part_got = over_band(jnp.concatenate(early, axis=2))
            got[0], got[1], update, weight_sums[1], *part_got = together(
                *got, update, weight_sums[1], *part_got
            )
            early = total(part_got).astype(bf16)
            early_rows = early.shape[1]
            late = cut_blocks(weight_sums[0], half_rows[0], late_blocks)
            late = [part.reshape(part.shape[0], -1, model_width) for part in late]
            weight_sums[0] = jnp.concatenate([early, *late], axis=1)
        else:
            got[0], got[1], weight_sums[0] = together(*got, weight_sums[0])
        if not last:
            kernel_split = [
                part
                for group in range(groups)
                for part in add_split(
                    spots,
                    kernel_split[2 * group + 1],
                    [got[group]],
                    1,
                    orders[group][stage + 1],
                    orders[group][stage + 1 :],
                )
            ]
    kernel_sums = [add_low(kernel_split[2 * group + 1], got[group]) for group in range(groups)]

    own_part = jnp.concatenate(kernel_sums, axis=0)
    own_part = own_part.reshape(bands_dev, band_size, own_pixels, model_width)
    own_part = own_part.transpose(1, 2, 0, 3)
    sent = [
        lax.dynamic_index_in_dim(own_part, spot ^ key, 0, keepdims=False)
        for key in range(band_size)
    ]
    pieces = [sent[0]] + [swap(sent[key], "band", key) for key in other_bands]
    weight_sums = [over_chips(weight_sums[half], orders[half], 1) for half in range(2)]
    grad_patches = unflatten_rows(update, bands_dev, (sent[0],))
    weight_sums[0], weight_sums[1], grad_patches, *pieces = together(
        *weight_sums, grad_patches, *pieces
    )
    grad_gen_kernel, tail = states_grad(spots, band_states, gen_kernel, pieces, sums)
    weight_sums[0], weight_sums[1], tail = together(*weight_sums, tail)

    small = weight_sums[0][:, early_rows - small_share : early_rows]
    small_steps = [("band", step) for step in bit_steps(band_size)]
    small_steps += [("dp", step) for step in turn(bit_steps(dp_size), 1)]

    def widen(values, number):
        return jnp.concatenate([values, swap(values, *small_steps[number])], axis=0)

    tail = total([tail] + [swap(tail, "band", key) for key in other_bands])
    small = widen(small, 0)
    tail, small, weight_sums[0], weight_sums[1] = together(tail, small, *weight_sums)
    late_rows = [half_rows[0][number] for number in late_blocks]
    late = cut_blocks(weight_sums[0][:, early_rows:], late_rows, range(len(late_rows)))
    late += cut_blocks(weight_sums[1], half_rows[1], range(len(half_rows[1])))
    last_sum = total(over_band(jnp.concatenate(late, axis=2)))
    for number, step in enumerate(turn(bit_steps(dp_size), 1)):
        got = swap(tail, "dp", step)
        if number + 1 < len(small_steps):
            small = widen(small, number + 1)
        got, small = together(got, small)
        tail = tail + got
    for number in range(len(bit_steps(dp_size)) + 1, len(small_steps)):
        small = widen(small, number)
    own_grads = jnp.concatenate(
        [weight_sums[0][0, : early_rows - small_share].astype(f32), last_sum[0]], axis=0
    )
    small_order = (jnp.arange(dp_size) ^ spots[0])[:, None] * band_size
    small_order = (small_order + (jnp.arange(band_size) ^ spots[1])[None, :]).reshape(-1)
    small = small.reshape(2, dp_size // 2, band_size, small_share, model_width)
    small = small.transpose(1, 0, 2, 3, 4).reshape(-1, small_share, model_width)
    small = jnp.take(small, small_order, axis=0).reshape(row_total, model_width)
    own_blocks = []
    done = 0
    for rows in weight_rows:
        own_blocks.append(own_grads[done : done + rows])
        done += rows
    grad_qkv_own = jnp.concatenate(own_blocks[:3], axis=1)
    grad_out_own = own_blocks[3]
    grad_fc_in_own = jnp.concatenate(own_blocks[4:-1], axis=1)
    grad_fc_out_own = own_blocks[-1]
    grad_token, grad_attn, grad_gain_gen, grad_ff_first, grad_ff_second, grad_gen_bias = (
        generate_back(
            tail,
            gen_attn,
            gen_gain,
            gen_ff_in,
            gen_ff_out,
            gen_bias,
            gen_kept,
        )
    )

    small = small.astype(f32)
    sums_at = small.shape[0] - 16
    grad_pos_all = small[: pos_table.shape[0]]
    grad_gains = small[sums_at + 1 : sums_at + 3]
    grad_shifts = small[sums_at + 3 : sums_at + 5]
    grad_bias_all = small[sums_at + 8 : sums_at + 8 + hidden // model_width].reshape(-1)
    grad_patches = grad_patches.reshape(group_size, slot_count, bands_dev, pixel_count)
    return (
        result.reshape(local_images, slot_count, model_width),
        grad_patches,
        grad_token[0],
        grad_attn,
        grad_gain_gen,
        grad_ff_first,
        grad_ff_second,
        grad_gen_kernel,
        grad_gen_bias,
        grad_pos_all,
        grad_gains,
        grad_shifts,
        grad_qkv_own,
        grad_out_own,
        grad_fc_in_own,
        grad_bias_all,
        grad_fc_out_own,
    )


def solution(mesh):
    placed = (
        P("dp", None, "band", None),
        P(),
        P(),
        P(),
        P(),
        P(),
        P(None, ("dp", "band")),
        P(),
        P(),
        P(),
        P(),
        P(("dp", "band"), None),
        P(("dp", "band"), None),
        P(("dp", "band"), None),
        P(),
        P(("dp", "band"), None),
        P(),
        P(("dp", "band"), None),
        P(("dp", "band")),
        P(("dp", "band"), None, None),
    )
    return jax.shard_map(
        shards,
        mesh=mesh,
        in_specs=placed,
        out_specs=(
            P(("dp", "band"), None, None),
            P("dp", None, "band", None),
            P(),
            P(),
            P(),
            P(),
            P(),
            P(None, ("dp", "band")),
            P(),
            P(),
            P(),
            P(),
            P(("dp", "band"), None),
            P(("dp", "band"), None),
            P(("dp", "band"), None),
            P(),
            P(("dp", "band"), None),
        ),
        check_vma=False,
    )
```

profile of v0, /device:TPU:1, one launch (start us, length us, event | category | flops | bytes accessed | tf_op | source)
XLA Modules:
  0.0 490.1 jit_solution(4816066401834122409)
XLA Ops:
  0.7 8.8 %shard_map.323 = (bf16[8,128,768]{2,1,0:T(8,128)(2,1)}, f32[8,768]{1,0:T(8,128)}, bf16[128,128]{1,0:T(8,128)(2,1)}, f32[136,128]{1,0:T(8,128)}, f32[7,136,128]{2...) custom-call(s32[1,128]{1,0:T(1,128)} %bitcast.188, bf16[1,128]{1,0:T(2,128)(2,1)} %bitcast.189, ...), custom_call_target="tpu_custom_call" | custom-call | flops 1000 | bytes 1000 | tf_op jit(solution)/shard_map/pallas_call | solution.py:93
  16.4 18.9 %shard_map.324.refs_1_ = bf16[1024,8192]{1,0:T(8,128)(2,1)} custom-call(bf16[8,128,768]{2,1,0:T(8,128)(2,1)} %get-tuple-element.135.refs_0_, bf16[1024,32,256]{2,1,0:T(8,128)(2,1)} %bitcast.161), custom_call_target="tpu_custom_call" | custom-call | flops 1000 | bytes 1000 | tf_op jit(solution)/shard_map/pallas_call | solution.py:93
  49.5 8.3 %collective-permute-start.6 = (bf16[288,768]{1,0:T(8,128)(2,1)S(1)}, bf16[288,768]{1,0:T(8,128)(2,1)S(1)}, u32[]{:S(2)}, u32[]{:S(2)}) collective-permute-start(bf16[288,768]{1,0:T(8,128)(2,1)S(1)} %copy-done.18), channel_id=1, source_target_pairs={{0,2},{1,3},{2,0},{3,1},{4,6},{5,7},{6,4},{7,5},{8,10},{9,11},{10,... | collective-permute-start | bytes 1327112 | tf_op jit(solution)/shard_map/ppermute | solution.py:39
  57.8 19.0 %collective-permute-done.6.refs_3_ = bf16[288,768]{1,0:T(8,128)(2,1)S(1)} collective-permute-done((bf16[288,768]{1,0:T(8,128)(2,1)S(1)}, bf16[288,768]{1,0:T(8,128)(2,1)S(1)}, u32[]{:S(2)}, u32[]{:S(2)}) %collective-permute-start.6) | collective-permute-done | bytes 442400 | tf_op jit(solution)/shard_map/ppermute | solution.py:39
  82.9 11.0 %collective-permute-done.10.refs_2_ = bf16[288,768]{1,0:T(8,128)(2,1)S(1)} collective-permute-done((bf16[288,768]{1,0:T(8,128)(2,1)S(1)}, bf16[288,768]{1,0:T(8,128)(2,1)S(1)}, u32[]{:S(2)}, u32[]{:S(2)}) %collective-permute-start.10) | collective-permute-done | bytes 442400 | tf_op jit(solution)/shard_map/ppermute | solution.py:39
  93.9 9.0 %collective-permute-done.11.refs_4_ = bf16[288,768]{1,0:T(8,128)(2,1)S(1)} collective-permute-done((bf16[288,768]{1,0:T(8,128)(2,1)S(1)}, bf16[288,768]{1,0:T(8,128)(2,1)S(1)}, u32[]{:S(2)}, u32[]{:S(2)}) %collective-permute-start.11) | collective-permute-done | bytes 442400 | tf_op jit(solution)/shard_map/ppermute | solution.py:39
  103.0 10.3 %collective-permute-done.8.refs_11_.refs_14_ = bf16[2,16,32,768]{3,2,1,0:T(8,128)(2,1)S(1)} collective-permute-done((bf16[2,16,32,768]{3,2,1,0:T(8,128)(2,1)S(1)}, bf16[2,16,32,768]{3,2,1,0:T(8,128)(2,1)S(1)}, u32[]{:S(2)}, u32[]{:S(2)}) %collective-permute-start.8) | collective-permute-done | bytes 1572896 | tf_op jit(solution)/shard_map/ppermute | solution.py:39
  125.2 20.3 %shard_map.327 = (bf16[256,768]{1,0:T(8,128)(2,1)}, bf16[256,768]{1,0:T(8,128)(2,1)}, bf16[256,768]{1,0:T(8,128)(2,1)}, bf16[256,768]{1,0:T(8,128)(2,1)}) custom-call(s32[2]{0:T(128)} %pad_add_fusion.refs_0_.refs_12_.refs_7_, bf16[1024,8192]{1,0:T(8,128)(2,1)} %shard_map.324.refs_1_, bf16[1,32,32,768]{3,2,1,0:T(8,128)(2,1)} %bitcast.153, ...), custom_call_target="tpu_custom_call" | custom-call | flops 1000 | bytes 1000 | tf_op jit(solution)/shard_map/pallas_call | solution.py:93
  155.2 13.5 %collective-permute-done.19.refs_1_ = bf16[256,768]{1,0:T(8,128)(2,1)S(1)} collective-permute-done((bf16[256,768]{1,0:T(8,128)(2,1)}, bf16[256,768]{1,0:T(8,128)(2,1)S(1)}, u32[]{:S(2)}, u32[]{:S(2)}) %collective-permute-start.19) | collective-permute-done | bytes 393248 | tf_op jit(solution)/shard_map/ppermute | solution.py:39
  168.6 10.9 %collective-permute-done.20.refs_2_ = bf16[256,768]{1,0:T(8,128)(2,1)S(1)} collective-permute-done((bf16[256,768]{1,0:T(8,128)(2,1)}, bf16[256,768]{1,0:T(8,128)(2,1)S(1)}, u32[]{:S(2)}, u32[]{:S(2)}) %collective-permute-start.20) | collective-permute-done | bytes 393248 | tf_op jit(solution)/shard_map/ppermute | solution.py:39
  202.8 29.1 %shard_map.328 = (bf16[256,768]{1,0:T(8,128)(2,1)}, bf16[256,768]{1,0:T(8,128)(2,1)}, bf16[256,13056]{1,0:T(8,128)(2,1)}, f32[8,768]{1,0:T(8,128)}) custom-call(bf16[256,768]{1,0:T(8,128)(2,1)} %get-tuple-element.163.refs_0_, bf16[256,768]{1,0:T(8,128)(2,1)} %copy-done.31, bf16[256,768]{1,0:T(8,128)(2,1)} %copy-done.32, bf16[256,768]{1,0:T(8,128)(2,1)} %copy-done.33, ...), custom_call_target="tpu_custom_call" | custom-call | flops 1000 | bytes 1000 | tf_op jit(solution)/shard_map/pallas_call | solution.py:93
  243.1 11.2 %shard_map.329 = (bf16[2,608,768]{2,1,0:T(8,128)(2,1)}, bf16[2,608,768]{2,1,0:T(8,128)(2,1)}, bf16[2,576,768]{2,1,0:T(8,128)(2,1)}, bf16[2,576,768]{2,1,0:T(8,128)(2,1)}) custom-call(s32[2]{0:T(128)} %pad_add_fusion.refs_0_.refs_12_.refs_7_, bf16[256,13056]{1,0:T(8,128)(2,1)} %get-tuple-element.174.refs_1_, bf16[256,13056]{1,0:T(8,128)(2,1)} %collective-permute-done.29.refs_2_), custom_call_target="tpu_custom_call" | custom-call | flops 1000 | bytes 1000 | tf_op jit(solution)/shard_map/pallas_call | solution.py:93
  261.8 13.2 %shard_map.332 = (bf16[8,4,32,768]{3,2,1,0:T(8,128)(2,1)}, bf16[8,4,32,768]{3,2,1,0:T(8,128)(2,1)}, bf16[16,4,32,768]{3,2,1,0:T(8,128)(2,1)}) custom-call(s32[2]{0:T(128)} %pad_add_fusion.refs_0_.refs_12_.refs_7_, bf16[1024,8192]{1,0:T(8,128)(2,1)} %shard_map.324.refs_1_, bf16[256,768]{1,0:T(8,128)(2,1)} %get-tuple-element.181.refs_2_.refs_1_, ...), custom_call_target="tpu_custom_call" | custom-call | flops 1000 | bytes 1000 | tf_op jit(solution)/shard_map/pallas_call | solution.py:93
  279.1 13.2 %shard_map.330 = (bf16[8,4,32,768]{3,2,1,0:T(8,128)(2,1)}, bf16[8,4,32,768]{3,2,1,0:T(8,128)(2,1)}, bf16[16,4,32,768]{3,2,1,0:T(8,128)(2,1)}) custom-call(s32[2]{0:T(128)} %pad_add_fusion.refs_0_.refs_12_.refs_7_, bf16[1024,8192]{1,0:T(8,128)(2,1)} %shard_map.324.refs_1_, bf16[256,768]{1,0:T(8,128)(2,1)} %get-tuple-element.181.refs_2_.refs_1_, ...), custom_call_target="tpu_custom_call" | custom-call | flops 1000 | bytes 1000 | tf_op jit(solution)/shard_map/pallas_call | solution.py:93
  293.0 20.4 %shard_map.334.refs_1_ = bf16[1024,8192]{1,0:T(8,128)(2,1)} custom-call(s32[2]{0:T(128)} %pad_add_fusion.refs_0_.refs_12_.refs_7_, bf16[256,768]{1,0:T(8,128)(2,1)} %get-tuple-element.181.refs_2_.refs_1_, bf16[256,768]{1,0:T(8,128)(2,1)} %copy-done.11, bf16[256,768]{1,0:T(8,128)(2,1)} %copy-done.12, bf16[256,768]{1,0:T(8,128)(2,1)} %copy-done.13, ...), custom_call_target="tpu_custom_call" | custom-call | flops 1000 | bytes 1000 | tf_op jit(solution)/shard_map/pallas_call | solution.py:93
  329.1 8.1 %collective-permute-start.38 = (bf16[2,104,768]{2,1,0:T(8,128)(2,1)S(1)}, bf16[2,104,768]{2,1,0:T(8,128)(2,1)S(1)}, u32[]{:S(2)}, u32[]{:S(2)}) collective-permute-start(bf16[2,104,768]{2,1,0:T(8,128)(2,1)S(1)} %get-tuple-element.269), channel_id=1, source_target_pairs={{0,1},{1,0},{2,3},{3,2},{4,5},{5,4},{6,7},{7,6},{8,9},{9,8},{10,11... | collective-permute-start | bytes 958472 | tf_op jit(solution)/shard_map/ppermute | solution.py:39
  342.4 7.8 %collective-permute-done.38 = bf16[2,104,768]{2,1,0:T(8,128)(2,1)S(1)} collective-permute-done((bf16[2,104,768]{2,1,0:T(8,128)(2,1)S(1)}, bf16[2,104,768]{2,1,0:T(8,128)(2,1)S(1)}, u32[]{:S(2)}, u32[]{:S(2)}) %collective-permute-start.38) | collective-permute-done | bytes 319520 | tf_op jit(solution)/shard_map/ppermute | solution.py:39
  350.4 8.7 %collective-permute-done.40 = bf16[2,104,768]{2,1,0:T(8,128)(2,1)S(1)} collective-permute-done((bf16[2,104,768]{2,1,0:T(8,128)(2,1)S(1)}, bf16[2,104,768]{2,1,0:T(8,128)(2,1)S(1)}, u32[]{:S(2)}, u32[]{:S(2)}) %collective-permute-start.40) | collective-permute-done | bytes 319520 | tf_op jit(solution)/shard_map/ppermute | solution.py:39
  371.8 9.1 %collective-permute-done.42 = bf16[16,1,32,768]{3,2,0,1:T(8,128)(2,1)} collective-permute-done((bf16[16,1,32,768]{3,2,0,1:T(8,128)(2,1)}, bf16[16,1,32,768]{3,2,0,1:T(8,128)(2,1)}, u32[]{:S(2)}, u32[]{:S(2)}) %collective-permute-start.42) | collective-permute-done | bytes 786464 | tf_op jit(solution)/shard_map/ppermute | solution.py:39
  389.1 9.6 %collective-permute-start.45 = (bf16[8,32,768]{2,1,0:T(8,128)(2,1)}, bf16[8,32,768]{2,1,0:T(8,128)(2,1)}, u32[]{:S(2)}, u32[]{:S(2)}) collective-permute-start(bf16[8,32,768]{2,1,0:T(8,128)(2,1)} %get-tuple-element.259), channel_id=1, source_target_pairs={{0,1},{1,0},{2,3},{3,2},{4,5},{5,4},{6,7},{7,6},{8,9},{9,8},{10,11... | collective-permute-start | bytes 1179656 | tf_op jit(solution)/shard_map/ppermute | solution.py:39
  400.8 18.9 %shard_map.337 = bf16[1024,32,256]{2,1,0:T(8,128)(2,1)} custom-call(bf16[8,32,768]{2,1,0:T(8,128)(2,1)} %get-tuple-element.222.refs_0_.refs_2_, bf16[1024,8192]{1,0:T(8,128)(2,1)} %shard_map.334.refs_1_), custom_call_target="tpu_custom_call" | custom-call | flops 1000 | bytes 1000 | tf_op jit(solution)/shard_map/pallas_call | solution.py:93
  428.2 9.5 %collective-permute-start.51 = (bf16[1,8,768]{2,1,0:T(8,128)(2,1)S(1)}, bf16[1,8,768]{2,1,0:T(8,128)(2,1)S(1)}, u32[]{:S(2)}, u32[]{:S(2)}) collective-permute-start(bf16[1,8,768]{2,1,0:T(8,128)(2,1)S(1)} %slice.130), channel_id=1, source_target_pairs={{0,1},{1,0},{2,3},{3,2},{4,5},{5,4},{6,7},{7,6},{8,9},{9,8},{10,11... | collective-permute-start | bytes 36872 | tf_op jit(solution)/shard_map/ppermute | solution.py:39
  461.4 9.2 %collective-permute-start.56 = (f32[136,128]{1,0:T(8,128)S(1)}, f32[136,128]{1,0:T(8,128)S(1)}, u32[]{:S(2)}, u32[]{:S(2)}) collective-permute-start(f32[136,128]{1,0:T(8,128)S(1)} %add.232), channel_id=1, source_target_pairs={{0,4},{4,0},{8,12},{12,8},{16,20},{20,16},{24,28},{28,24},{1,5},{5... | collective-permute-start | bytes 208904 | tf_op jit(solution)/shard_map/ppermute | solution.py:39
  473.4 12.0 %shard_map.339 = (f32[1,128]{1,0:T(1,128)}, f32[4,128,128]{2,1,0:T(8,128)}, f32[2,128]{1,0:T(2,128)}, f32[128,2048]{1,0:T(8,128)}, f32[2048,128]{1,0:T(8,128)}, /*index=5*/f32[128,768]{1,0:T(8,128)}) custom-call(f32[136,128]{1,0:T(8,128)} %add.233.refs_0_, bf16[4,128,128]{2,1,0:T(8,128)(2,1)} %refs_1_.5, bf16[2,128]{1,0:T(2,128)(2,1)} %refs_2_.5, ...), custom_call_target="tpu_custom_call" | custom-call | flops 1000 | bytes 1000 | tf_op jit(solution)/shard_map/pallas_call | solution.py:93
  (307 shorter events, 178.4 us)
Async XLA Ops:
  43.4 34.2 %collective-permute-start.5 = (bf16[32,32,768]{2,1,0:T(8,128)(2,1)S(1)}, bf16[32,32,768]{2,1,0:T(8,128)(2,1)S(1)}, u32[]{:S(2)}, u32[]{:S(2)}) collective-permute-start(bf16[32,32,768]{2,1,0:T(8,128)(2,1)S(1)} %bitcast.152), channel_id=1, source_target_pairs={{0,4},{4,0},{8,12},{12,8},{16,20},{20,16},{24,28},{28,24},{1,5},{5... | collective-permute-start | bytes 4718600 | tf_op jit(solution)/shard_map/ppermute | solution.py:39
  47.0 29.8 %collective-permute-start.3 = (bf16[1,16,32,768]{3,2,1,0:T(8,128)(2,1)S(1)}, bf16[1,16,32,768]{3,2,1,0:T(8,128)(2,1)S(1)}, u32[]{:S(2)}, u32[]{:S(2)}) collective-permute-start(bf16[1,16,32,768]{3,2,1,0:T(8,128)(2,1)S(1)} %get-tuple-element.262), channel_id=1, source_target_pairs={{0,8},{4,12},{8,0},{12,4},{16,24},{20,28},{24,16},{28,20},{1,9},{5... | collective-permute-start | bytes 2359304 | tf_op jit(solution)/shard_map/ppermute | solution.py:39
  48.2 28.5 %collective-permute-start.4 = (bf16[1,16,32,768]{3,2,1,0:T(8,128)(2,1)S(1)}, bf16[1,16,32,768]{3,2,1,0:T(8,128)(2,1)S(1)}, u32[]{:S(2)}, u32[]{:S(2)}) collective-permute-start(bf16[1,16,32,768]{3,2,1,0:T(8,128)(2,1)S(1)} %get-tuple-element.261), channel_id=1, source_target_pairs={{0,16},{4,20},{8,24},{12,28},{16,0},{20,4},{24,8},{28,12},{1,17},{... | collective-permute-start | bytes 2359304 | tf_op jit(solution)/shard_map/ppermute | solution.py:39
  49.5 27.3 %collective-permute-start.6 = (bf16[288,768]{1,0:T(8,128)(2,1)S(1)}, bf16[288,768]{1,0:T(8,128)(2,1)S(1)}, u32[]{:S(2)}, u32[]{:S(2)}) collective-permute-start(bf16[288,768]{1,0:T(8,128)(2,1)S(1)} %copy-done.18), channel_id=1, source_target_pairs={{0,2},{1,3},{2,0},{3,1},{4,6},{5,7},{6,4},{7,5},{8,10},{9,11},{10,... | collective-permute-start | bytes 1327112 | tf_op jit(solution)/shard_map/ppermute | solution.py:39
  78.9 34.4 %collective-permute-start.8 = (bf16[2,16,32,768]{3,2,1,0:T(8,128)(2,1)S(1)}, bf16[2,16,32,768]{3,2,1,0:T(8,128)(2,1)S(1)}, u32[]{:S(2)}, u32[]{:S(2)}) collective-permute-start(bf16[2,16,32,768]{3,2,1,0:T(8,128)(2,1)S(1)} %pad_maximum_fusion.3), channel_id=1, source_target_pairs={{0,8},{4,12},{8,0},{12,4},{16,24},{20,28},{24,16},{28,20},{1,9},{5... | collective-permute-start | bytes 4718600 | tf_op jit(solution)/shard_map/ppermute | solution.py:39
  79.4 34.2 %collective-permute-start.7 = (bf16[2,16,32,768]{3,2,1,0:T(8,128)(2,1)S(1)}, bf16[2,16,32,768]{3,2,1,0:T(8,128)(2,1)}, u32[]{:S(2)}, u32[]{:S(2)}) collective-permute-start(bf16[2,16,32,768]{3,2,1,0:T(8,128)(2,1)S(1)} %pad_maximum_fusion.2), channel_id=1, source_target_pairs={{0,16},{4,20},{8,24},{12,28},{16,0},{20,4},{24,8},{28,12},{1,17},{... | collective-permute-start | bytes 4718600 | tf_op jit(solution)/shard_map/ppermute | solution.py:39
  147.0 40.0 %collective-permute-start.18 = (bf16[2,576,768]{2,1,0:T(8,128)(2,1)S(1)}, bf16[2,576,768]{2,1,0:T(8,128)(2,1)}, u32[]{:S(2)}, u32[]{:S(2)}) collective-permute-start(bf16[2,576,768]{2,1,0:T(8,128)(2,1)S(1)} %pad_maximum_fusion.1.refs_8_), channel_id=1, source_target_pairs={{0,8},{4,12},{8,0},{12,4},{16,24},{20,28},{24,16},{28,20},{1,9},{5... | collective-permute-start | bytes 5308424 | tf_op jit(solution)/shard_map/ppermute | solution.py:39
  150.2 40.2 %collective-permute-start.17 = (bf16[2,576,768]{2,1,0:T(8,128)(2,1)}, bf16[2,576,768]{2,1,0:T(8,128)(2,1)}, u32[]{:S(2)}, u32[]{:S(2)}) collective-permute-start(bf16[2,576,768]{2,1,0:T(8,128)(2,1)} %pad_maximum_fusion.refs_4_), channel_id=1, source_target_pairs={{0,16},{4,20},{8,24},{12,28},{16,0},{20,4},{24,8},{28,12},{1,17},{... | collective-permute-start | bytes 5308424 | tf_op jit(solution)/shard_map/ppermute | solution.py:39
  151.5 28.1 %collective-permute-start.20 = (bf16[256,768]{1,0:T(8,128)(2,1)}, bf16[256,768]{1,0:T(8,128)(2,1)S(1)}, u32[]{:S(2)}, u32[]{:S(2)}) collective-permute-start(bf16[256,768]{1,0:T(8,128)(2,1)} %get-tuple-element.161), channel_id=1, source_target_pairs={{0,2},{1,3},{2,0},{3,1},{4,6},{5,7},{6,4},{7,5},{8,10},{9,11},{10,... | collective-permute-start | bytes 1179656 | tf_op jit(solution)/shard_map/ppermute | solution.py:39
  152.4 27.2 %collective-permute-start.21 = (bf16[256,768]{1,0:T(8,128)(2,1)}, bf16[256,768]{1,0:T(8,128)(2,1)S(1)}, u32[]{:S(2)}, u32[]{:S(2)}) collective-permute-start(bf16[256,768]{1,0:T(8,128)(2,1)} %get-tuple-element.162), channel_id=1, source_target_pairs={{0,3},{1,2},{2,1},{3,0},{4,7},{5,6},{6,5},{7,4},{8,11},{9,10},{10,... | collective-permute-start | bytes 1179656 | tf_op jit(solution)/shard_map/ppermute | solution.py:39
  232.4 28.6 %collective-permute-start.27 = (bf16[256,768]{1,0:T(8,128)(2,1)}, bf16[256,768]{1,0:T(8,128)(2,1)S(1)}, u32[]{:S(2)}, u32[]{:S(2)}) collective-permute-start(bf16[256,768]{1,0:T(8,128)(2,1)} %get-tuple-element.181.refs_2_.refs_1_), channel_id=1, source_target_pairs={{0,2},{1,3},{2,0},{3,1},{4,6},{5,7},{6,4},{7,5},{8,10},{9,11},{10,... | collective-permute-start | bytes 1179656 | tf_op jit(solution)/shard_map/ppermute | solution.py:39
  233.2 27.7 %collective-permute-start.28 = (bf16[256,768]{1,0:T(8,128)(2,1)}, bf16[256,768]{1,0:T(8,128)(2,1)S(1)}, u32[]{:S(2)}, u32[]{:S(2)}) collective-permute-start(bf16[256,768]{1,0:T(8,128)(2,1)} %get-tuple-element.181.refs_2_.refs_1_), channel_id=1, source_target_pairs={{0,3},{1,2},{2,1},{3,0},{4,7},{5,6},{6,5},{7,4},{8,11},{9,10},{10,... | collective-permute-start | bytes 1179656 | tf_op jit(solution)/shard_map/ppermute | solution.py:39
  276.4 47.6 %collective-permute-start.30 = (bf16[2,608,768]{2,1,0:T(8,128)(2,1)}, bf16[2,608,768]{2,1,0:T(8,128)(2,1)S(1)}, u32[]{:S(2)}, u32[]{:S(2)}) collective-permute-start(bf16[2,608,768]{2,1,0:T(8,128)(2,1)} %get-tuple-element.179), channel_id=1, source_target_pairs={{0,8},{4,12},{8,0},{12,4},{16,24},{20,28},{24,16},{28,20},{1,9},{5... | collective-permute-start | bytes 5603336 | tf_op jit(solution)/shard_map/ppermute | solution.py:39
  277.3 46.7 %collective-permute-start.31 = (bf16[2,576,768]{2,1,0:T(8,128)(2,1)}, bf16[2,576,768]{2,1,0:T(8,128)(2,1)}, u32[]{:S(2)}, u32[]{:S(2)}) collective-permute-start(bf16[2,576,768]{2,1,0:T(8,128)(2,1)} %get-tuple-element.180), channel_id=1, source_target_pairs={{0,16},{4,20},{8,24},{12,28},{16,0},{20,4},{24,8},{28,12},{1,17},{... | collective-permute-start | bytes 5308424 | tf_op jit(solution)/shard_map/ppermute | solution.py:39
  278.5 34.9 %collective-permute-start.35 = (bf16[8,4,32,768]{3,2,1,0:T(8,128)(2,1)}, bf16[8,4,32,768]{3,2,1,0:T(8,128)(2,1)}, u32[]{:S(2)}, u32[]{:S(2)}) collective-permute-start(bf16[8,4,32,768]{3,2,1,0:T(8,128)(2,1)} %get-tuple-element.192), channel_id=1, source_target_pairs={{0,4},{4,0},{8,12},{12,8},{16,20},{20,16},{24,28},{28,24},{1,5},{5... | collective-permute-start | bytes 4718600 | tf_op jit(solution)/shard_map/ppermute | solution.py:39
  292.3 26.4 %collective-permute-start.32 = (bf16[8,4,32,768]{3,2,1,0:T(8,128)(2,1)}, bf16[8,4,32,768]{3,2,1,0:T(8,128)(2,1)}, u32[]{:S(2)}, u32[]{:S(2)}) collective-permute-start(bf16[8,4,32,768]{3,2,1,0:T(8,128)(2,1)} %get-tuple-element.186), channel_id=1, source_target_pairs={{0,4},{4,0},{8,12},{12,8},{16,20},{20,16},{24,28},{28,24},{1,5},{5... | collective-permute-start | bytes 4718600 | tf_op jit(solution)/shard_map/ppermute | solution.py:39
  324.0 36.1 %collective-permute-start.36 = (bf16[16,2,32,768]{3,2,1,0:T(8,128)(2,1)}, bf16[16,2,32,768]{3,2,1,0:T(8,128)(2,1)S(1)}, u32[]{:S(2)}, u32[]{:S(2)}) collective-permute-start(bf16[16,2,32,768]{3,2,1,0:T(8,128)(2,1)} %bitcast.191), channel_id=1, source_target_pairs={{0,8},{4,12},{8,0},{12,4},{16,24},{20,28},{24,16},{28,20},{1,9},{5... | collective-permute-start | bytes 4718600 | tf_op jit(solution)/shard_map/ppermute | solution.py:39
  325.3 36.0 %collective-permute-start.37 = (bf16[16,2,32,768]{3,2,1,0:T(8,128)(2,1)}, bf16[16,2,32,768]{3,2,1,0:T(8,128)(2,1)}, u32[]{:S(2)}, u32[]{:S(2)}) collective-permute-start(bf16[16,2,32,768]{3,2,1,0:T(8,128)(2,1)} %bitcast.190), channel_id=1, source_target_pairs={{0,16},{4,20},{8,24},{12,28},{16,0},{20,4},{24,8},{28,12},{1,17},{... | collective-permute-start | bytes 4718600 | tf_op jit(solution)/shard_map/ppermute | solution.py:39
  369.4 50.3 %collective-permute-start.44 = (bf16[1,576,768]{2,1,0:T(8,128)(2,1)S(1)}, bf16[1,576,768]{2,1,0:T(8,128)(2,1)}, u32[]{:S(2)}, u32[]{:S(2)}) collective-permute-start(bf16[1,576,768]{2,1,0:T(8,128)(2,1)S(1)} %constant_dynamic-slice_fusion), channel_id=1, source_target_pairs={{0,8},{4,12},{8,0},{12,4},{16,24},{20,28},{24,16},{28,20},{1,9},{5... | collective-permute-start | bytes 2654216 | tf_op jit(solution)/shard_map/ppermute | solution.py:39
  384.9 36.2 %collective-permute-start.43 = (bf16[1,296,768]{2,1,0:T(8,128)(2,1)}, bf16[1,296,768]{2,1,0:T(8,128)(2,1)S(1)}, u32[]{:S(2)}, u32[]{:S(2)}) collective-permute-start(bf16[1,296,768]{2,1,0:T(8,128)(2,1)} %constant_dynamic-slice_fusion.1), channel_id=1, source_target_pairs={{0,16},{4,20},{8,24},{12,28},{16,0},{20,4},{24,8},{28,12},{1,17},{... | collective-permute-start | bytes 1363976 | tf_op jit(solution)/shard_map/ppermute | solution.py:39
  389.1 32.2 %collective-permute-start.45 = (bf16[8,32,768]{2,1,0:T(8,128)(2,1)}, bf16[8,32,768]{2,1,0:T(8,128)(2,1)}, u32[]{:S(2)}, u32[]{:S(2)}) collective-permute-start(bf16[8,32,768]{2,1,0:T(8,128)(2,1)} %get-tuple-element.259), channel_id=1, source_target_pairs={{0,1},{1,0},{2,3},{3,2},{4,5},{5,4},{6,7},{7,6},{8,9},{9,8},{10,11... | collective-permute-start | bytes 1179656 | tf_op jit(solution)/shard_map/ppermute | solution.py:39
  447.0 38.3 %collective-permute-start.59 = (bf16[1,192,768]{2,1,0:T(8,128)(2,1)S(1)}, bf16[1,192,768]{2,1,0:T(8,128)(2,1)S(1)}, u32[]{:S(2)}, u32[]{:S(2)}) collective-permute-start(bf16[1,192,768]{2,1,0:T(8,128)(2,1)S(1)} %get-tuple-element.271), channel_id=1, source_target_pairs={{0,1},{1,0},{2,3},{3,2},{4,5},{5,4},{6,7},{7,6},{8,9},{9,8},{10,11... | collective-permute-start | bytes 884744 | tf_op jit(solution)/shard_map/ppermute | solution.py:39
  448.4 36.9 %collective-permute-start.60 = (bf16[1,192,768]{2,1,0:T(8,128)(2,1)S(1)}, bf16[1,192,768]{2,1,0:T(8,128)(2,1)S(1)}, u32[]{:S(2)}, u32[]{:S(2)}) collective-permute-start(bf16[1,192,768]{2,1,0:T(8,128)(2,1)S(1)} %get-tuple-element.273), channel_id=1, source_target_pairs={{0,2},{1,3},{2,0},{3,1},{4,6},{5,7},{6,4},{7,5},{8,10},{9,11},{10,... | collective-permute-start | bytes 884744 | tf_op jit(solution)/shard_map/ppermute | solution.py:39
  449.3 36.0 %collective-permute-start.61 = (bf16[1,192,768]{2,1,0:T(8,128)(2,1)S(1)}, bf16[1,192,768]{2,1,0:T(8,128)(2,1)S(1)}, u32[]{:S(2)}, u32[]{:S(2)}) collective-permute-start(bf16[1,192,768]{2,1,0:T(8,128)(2,1)S(1)} %get-tuple-element.272), channel_id=1, source_target_pairs={{0,3},{1,2},{2,1},{3,0},{4,7},{5,6},{6,5},{7,4},{8,11},{9,10},{10,... | collective-permute-start | bytes 884744 | tf_op jit(solution)/shard_map/ppermute | solution.py:39
  (83 other events, 1344.7 us)
where the time goes:
time: 497 us; the launch traced here: 490 us
  Pallas kernels  192 us (39%)
  waiting for transfers between devices  148 us (30%)
  starting transfers between devices  101 us (20%)
  local copies, waits for them, and re-layouts  23.9 us (5%)
  other arithmetic  23.8 us (5%)
    pallas_call x17, Pallas kernels, run_kernel(): pl.pallas_call(whole, in_specs=[pl.BlockSpec(memory_space=pl.ANY)] * coun...  192 us
    ppermute x62, waiting for transfers between devices, swap(): lax.ppermute(values, axis, [(spot, spot ^ step) for spot in range(size)])  148 us
    ppermute x62, starting transfers between devices, swap(): lax.ppermute(values, axis, [(spot, spot ^ step) for spot in range(size)])  101 us
  transfers between devices with their start and end apart: 62, of which 27 were waited for; matrix products, arithmetic and copies ran while one was open for 7% of the time, Pallas kernels for 27%

commit v1 on v0

--- a/solution.py
+++ b/solution.py
@@ -328,14 +328,8 @@
     small_ref = views["small"]
     positions = small_ref.shape[0] - 16
     spots_at = lax.broadcasted_iota(jnp.int32, (positions, row_total), 0)
-    one_hot = jnp.where(spots_at == kept_ref[...], 1.0, 0.0)
-    by_position = lax.dot_general(
-        one_hot,
-        grad_start,
-        (((1,), (0,)), ((), ())),
-        precision=lax.Precision.HIGHEST,
-        preferred_element_type=f32,
-    )
+    one_hot = jnp.where(spots_at == kept_ref[...], 1.0, 0.0).astype(bf16)
+    by_position = dot_nn(one_hot, grad_start.astype(bf16))
     cuts = [bias_grad_ref[:, spot : spot + width] for spot in range(0, hidden, width)]
     cuts.append(jnp.zeros((8 - len(cuts), width), f32))
     small_ref[...] = jnp.concatenate([by_position, sums, *cuts], axis=0).astype(bf16)
@@ -389,7 +383,7 @@
         left_arr,
         right_arr,
         (((left_dim,), (right_dim,)), ((), ())),
-        precision=lax.Precision.HIGHEST,
+        precision=lax.Precision.HIGH,
         preferred_element_type=jnp.float32,
     )
 
@@ -679,7 +673,7 @@
     return min(block.shape[1] for blocks in kernel_groups for _, block in blocks)
 
 
-def piece_specs(kernel_groups, band_step):
+def piece_specs(kernel_groups, band_step, first_group=0):
     group_steps = group_band_count(kernel_groups) // band_step
     specs = []
     arrays = []
@@ -687,10 +681,11 @@
         for keys, block in blocks:
             whole = block.shape[1] > group_steps * band_step
             first = group * group_steps
+            skip = first_group * group_steps
 
             def pick(step, first=first, whole=whole):
                 here = jnp.clip(step - first, 0, group_steps - 1)
-                return (0, here + first if whole else here, 0, 0)
+                return (0, here + first + skip if whole else here, 0, 0)
 
             specs.append(pl.BlockSpec((len(keys), band_step) + block.shape[2:], pick))
             arrays.append(block)
@@ -759,7 +754,7 @@
 def kernel_grad_part(spots, patch_rows, grads, first_band, group_bands, bands_dev, dp_size, after):
     row_total = patch_rows.shape[0]
     width = grads[0].shape[1]
-    band_step = min(2, group_bands // 2)
+    band_step = min(4, group_bands // 2)
     pixels = patch_rows.shape[1] // bands_dev
     depth = band_step * pixels
     offset = first_band // band_step
@@ -804,12 +799,12 @@
         )
 
 
-def patch_grad(spots, grads, kernel_groups, pixels, after):
+def patch_grad(spots, grads, kernel_groups, pixels, first_group, after):
     rows, width = grads[0].shape
     row_total = rows * len(grads)
     band_step = min(4, group_band_count(kernel_groups))
     depth = band_step * pixels
-    specs, arrays, keys_lists, group_steps = piece_specs(kernel_groups, band_step)
+    specs, arrays, keys_lists, group_steps = piece_specs(kernel_groups, band_step, first_group)
     steps = group_steps * len(kernel_groups)
     return run_kernel(
         partial(patch_grad_body, keys_lists, len(grads), group_steps, band_step),
@@ -874,6 +869,16 @@
     out_ref[...] = in_ref[...].reshape(out_ref.shape)
 
 
+def unflatten_body(*refs):
+    *in_refs, out_ref = refs
+    done = 0
+    for in_ref in in_refs:
+        part = in_ref[...]
+        bands = part.shape[1] // out_ref.shape[2]
+        out_ref[:, done : done + bands, :] = part.reshape(-1, bands, out_ref.shape[2])
+        done += bands
+
+
 def flatten_rows(cube, after):
     rows, bands, pixels = cube.shape
     step_rows = 64
@@ -888,17 +893,18 @@
     )
 
 
-def unflatten_rows(flat, bands, after):
-    rows, depth = flat.shape
+def unflatten_rows(flats, bands, after):
+    rows = flats[0].shape[0]
+    pixels = sum(flat.shape[1] for flat in flats) // bands
     step_rows = 64
     return run_kernel(
-        flatten_body,
-        (flat,),
-        [pl.BlockSpec((step_rows, depth), lambda step: (step, 0))],
+        unflatten_body,
+        flats,
+        [pl.BlockSpec((step_rows, flat.shape[1]), lambda step: (step, 0)) for flat in flats],
         after=after,
         grid=(rows // step_rows,),
-        out_shape=jax.ShapeDtypeStruct((rows, bands, depth // bands), flat.dtype),
-        out_specs=pl.BlockSpec((step_rows, bands, depth // bands), lambda step: (step, 0, 0)),
+        out_shape=jax.ShapeDtypeStruct((rows, bands, pixels), flats[0].dtype),
+        out_specs=pl.BlockSpec((step_rows, bands, pixels), lambda step: (step, 0, 0)),
     )
 
 
@@ -972,7 +978,7 @@
     )
 
 
-def weight_grad_body(dp_size, first_steps, hidden, spot_ref, own_ref, other_ref, *refs):
+def weight_grad_body(dp_size, parts, hidden, spot_ref, own_ref, other_ref, *refs):
     *out_refs, turned_ref, hold_ref, feed_ref, small_ref, sems = refs
     width = hold_ref.shape[2]
     row_total = own_ref.shape[0]
@@ -1002,9 +1008,12 @@
             parts.append(turned_ref[pl.ds(pl.multiple_of(first, 16), rows), :])
         return jnp.concatenate(parts, axis=0)
 
-    def send(source_ref, rows, half, first, stride=None):
-        step = first_steps[half] // 2
-        bit = lax.rem(lax.div(spot_ref[0], first_steps[half]), 2)
+    def send(source_ref, rows, number, stride=None):
+        part = [number in numbers for _, numbers in parts].index(True)
+        first_step, numbers = parts[part]
+        first = share * numbers.index(number)
+        step = first_step // 2
+        bit = lax.rem(lax.div(spot_ref[0], first_step), 2)
         for index in range(chips // 2):
             for which in range(2):
                 own_bit = bit if which == 0 else 1 - bit
@@ -1012,7 +1021,7 @@
                 at = chip * (stride or rows)
                 copy = pltpu.make_async_copy(
                     source_ref.at[pl.ds(pl.multiple_of(at, 16), rows), :],
-                    out_refs[half * 2 + which].at[index, pl.ds(first, rows), :],
+                    out_refs[part * 2 + which].at[index, pl.ds(first, rows), :],
                     sems.at[len(copies)],
                 )
                 copy.start()
@@ -1035,7 +1044,7 @@
             turn_rows(left, turned_at[left])
             picked = {left: pick(turned_at[left], share)}
         hold_ref[number] = product(picked[left], right, column).astype(hold_ref.dtype)
-        send(hold_ref.at[number], share, number // 6, number % 6 * share)
+        send(hold_ref.at[number], share, number)
     small = sum(part.astype(jnp.float32) for part in view("small"))
     small_ref[...] = small.astype(small_ref.dtype)
     small_share = row_total // dp_size
@@ -1047,33 +1056,34 @@
         feed_ref[chip * feed_rows : (chip + 1) * feed_rows, :] = product(left, "cot", 0).astype(
             feed_ref.dtype
         )
-    send(feed_ref, feed_rows, 1, (len(blocks) - 6) * share)
+    send(feed_ref, feed_rows, len(blocks))
     own_small = small_ref.at[pl.ds(pl.multiple_of(core * small_share, 16), (dp_size - 1) * small_share), :]
-    send(own_small, small_share, 0, 6 * share, 2 * small_share)
+    send(own_small, small_share, len(blocks) + 1, 2 * small_share)
     for copy in copies:
         copy.wait()
 
 
-def weight_grad(spots, dp_size, first_steps, hidden, own, other):
+def weight_grad(spots, dp_size, parts, hidden, own, other):
     row_total, columns = own.shape
     width = (columns - 2 * hidden) // 9
     bf16 = jnp.bfloat16
     blocks = 4 + hidden // width
     chips = dp_size // 2
     share = width // dp_size
-    rows = [6 * share + row_total // dp_size, (blocks - 6) * share + hidden // dp_size]
+    block_rows = [share] * blocks + [hidden // dp_size, row_total // dp_size]
+    rows = [sum(block_rows[number] for number in numbers) for _, numbers in parts]
     inside = pl.BlockSpec(memory_space=pltpu.VMEM)
     outside = pl.BlockSpec(memory_space=pl.ANY)
     return run_kernel(
-        partial(weight_grad_body, dp_size, first_steps, hidden),
+        partial(weight_grad_body, dp_size, parts, hidden),
         (spots, own, other),
         [pl.BlockSpec(memory_space=pltpu.SMEM), inside, inside],
         out_shape=[
-            jax.ShapeDtypeStruct((chips // 2, rows[half], width), bf16)
-            for half in range(2)
+            jax.ShapeDtypeStruct((chips // 2, part_rows, width), bf16)
+            for part_rows in rows
             for _ in range(2)
         ],
-        out_specs=[outside] * 4,
+        out_specs=[outside] * (2 * len(parts)),
         scratch_shapes=[
             pltpu.VMEM((3 * width + hidden, 2 * row_total), bf16),
             pltpu.VMEM((blocks, chips * share, width), bf16),
@@ -1106,10 +1116,10 @@
     part_outer = outer // len(gots)
     inner_rows = keep.size // (outer * 2 * width)
     rows_step = inner_rows
-    while rows_step > 320 and rows_step % 32 == 0:
+    while rows_step > 512 and rows_step % 32 == 0:
         rows_step //= 2
     outer_step = 1
-    while part_outer % (2 * outer_step) == 0 and 2 * outer_step * rows_step <= 320:
+    while part_outer % (2 * outer_step) == 0 and 2 * outer_step * rows_step <= 512:
         outer_step *= 2
     part_steps = part_outer // outer_step
     block_in = (outer_step, 2, rows_step, width)
@@ -1295,17 +1305,20 @@
         kept_flat[None],
     )
 
+    small_share = row_total // device_count
+    block_rows = weight_rows + [small_share]
+    part_blocks = [[0, 1, 9], [2, 3], [4, 5, 6, 7], [8]]
+    part_orders = [orders[0], orders[1], orders[0], orders[1]]
+    weight_parts = [(order[0], numbers) for order, numbers in zip(part_orders, part_blocks)]
     grads = [grad_embed] + [swap(grad_embed, "band", key) for key in other_bands]
-    first_steps = [order[0] for order in orders]
     weight_split = weight_grad(
-        spots, dp_size, first_steps, hidden, stash, swap(stash, "dp", 1)
+        spots, dp_size, weight_parts, hidden, stash, swap(stash, "dp", 1)
     )
     mixed = together(*grads, *weight_split)
     grads, weight_split = list(mixed[:band_size]), mixed[band_size:]
-
-    weight_got = [
-        swap(weight_split[2 * half + 1], "dp", first_steps[half]) for half in range(2)
-    ]
+    weight_keep, weight_send = list(weight_split[0::2]), list(weight_split[1::2])
+
+    weight_got = [swap(weight_send[part], "dp", part_orders[part][0]) for part in range(2)]
     kernel_split = []
     for group in range(groups):
         *sends, keep = kernel_grad_part(
@@ -1321,21 +1334,17 @@
         core_got = [swap(send, "dp", 1) for send in sends]
         kernel_split += add_split(spots, keep, core_got, 1, orders[group][0], dp_steps)
     weight_got[0], weight_got[1], *kernel_split = together(*weight_got, *kernel_split)
-    weight_sums = [add_low(weight_split[2 * half], weight_got[half]) for half in range(2)]
-    small_share = row_total // device_count
-    half_rows = [weight_rows[:6] + [small_share], weight_rows[6:]]
-    early_blocks = [0, 1, 2, 3, 6]
-    late_blocks = [4, 5]
-
-    def cut_blocks(values, rows_list, numbers):
+
+    def cut_blocks(values, numbers):
         lead = values.shape[0]
-        parts = []
+        cuts = []
+        first = 0
         for number in numbers:
-            rows = rows_list[number]
-            first = sum(rows_list[:number]) * band_size
-            part = values[:, first : first + rows * band_size]
-            parts.append(part.reshape(lead, band_size, rows, model_width))
-        return parts
+            rows = block_rows[number]
+            cut = values[:, first : first + rows * band_size]
+            cuts.append(cut.reshape(lead, band_size, rows, model_width))
+            first += rows * band_size
+        return jnp.concatenate(cuts, axis=2)
 
     def over_band(by_band):
         sent = [
@@ -1347,29 +1356,42 @@
     def total(blocks):
         return sum(block_sum.astype(f32) for block_sum in blocks)
 
-    def over_chips(values, order, first=0):
-        for stage in range(first, len(order)):
-            send, keep = split_half(values, 0, order[stage], order[stage:])
-            values = add_low(keep, swap(send, "dp", order[stage]))
-        return values
-
-    update = patch_grad(spots, grads, kernel_groups, pixel_count, ())
+    def over_chips(sums):
+        cut = [
+            values if isinstance(values, tuple) else split_half(values, 0, order[0], order)
+            for values, order in sums
+        ]
+        got = [None] * len(sums)
+        for step in sorted({order[0] for _, order in sums}):
+            here = [number for number, (_, order) in enumerate(sums) if order[0] == step]
+            flat = [cut[number][0].reshape(-1, model_width) for number in here]
+            moved = swap(jnp.concatenate(flat, axis=0) if len(flat) > 1 else flat[0], "dp", step)
+            first = 0
+            for number, rows in zip(here, flat):
+                part = moved[first : first + rows.shape[0]]
+                got[number] = part.reshape(cut[number][0].shape)
+                first += rows.shape[0]
+        return [
+            (add_low(cut[number][1], got[number]), order[1:])
+            for number, (_, order) in enumerate(sums)
+        ]
+
+    update = patch_grad(spots, grads, kernel_groups, pixel_count, 0, ())
     for stage in range(len(dp_steps)):
         last = stage == len(dp_steps) - 1
         got = [swap(kernel_split[2 * group], "dp", orders[group][stage]) for group in range(groups)]
         if stage == 0:
-            early = cut_blocks(weight_sums[0], half_rows[0], early_blocks)
-            part_got = over_band(jnp.concatenate(early, axis=2))
-            got[0], got[1], update, weight_sums[1], *part_got = together(
-                *got, update, weight_sums[1], *part_got
-            )
+            cuts = [
+                cut_blocks(add_low(weight_keep[part], weight_got[part]), part_blocks[part])
+                for part in range(2)
+            ]
+            part_got = over_band(jnp.concatenate(cuts, axis=2))
+            got[0], got[1], update, *part_got = together(*got, update, *part_got)
             early = total(part_got).astype(bf16)
-            early_rows = early.shape[1]
-            late = cut_blocks(weight_sums[0], half_rows[0], late_blocks)
-            late = [part.reshape(part.shape[0], -1, model_width) for part in late]
-            weight_sums[0] = jnp.concatenate([early, *late], axis=1)
+            early_rows = cuts[0].shape[2]
+            early = [early[:, :early_rows], early[:, early_rows:]]
         else:
-            got[0], got[1], weight_sums[0] = together(*got, weight_sums[0])
+            got[0], got[1], early[0], early[1] = together(*got, *early)
         if not last:
             kernel_split = [
                 part
@@ -1393,28 +1415,40 @@
         for key in range(band_size)
     ]
     pieces = [sent[0]] + [swap(sent[key], "band", key) for key in other_bands]
-    weight_sums = [over_chips(weight_sums[half], orders[half], 1) for half in range(2)]
-    grad_patches = unflatten_rows(update, bands_dev, (sent[0],))
-    weight_sums[0], weight_sums[1], grad_patches, *pieces = together(
-        *weight_sums, grad_patches, *pieces
-    )
+    sums_left = over_chips(
+        [(early[part], part_orders[part][1:]) for part in range(2)]
+        + [
+            ((weight_send[part], weight_keep[part]), part_orders[part])
+            for part in range(2, 4)
+        ]
+    )
+    while any(order for _, order in sums_left[:2]):
+        moved = over_chips([one for one in sums_left[:2] if one[1]])
+        sums_left[:2] = [moved.pop(0) if one[1] else one for one in sums_left[:2]]
+    weight_sums = [values for values, _ in sums_left]
+    grad_patches = unflatten_rows([update], bands_dev, (sent[0],))
+    mixed = together(*weight_sums, grad_patches, *pieces)
+    weight_sums, grad_patches, pieces = list(mixed[:4]), mixed[4], mixed[5:]
     grad_gen_kernel, tail = states_grad(spots, band_states, gen_kernel, pieces, sums)
-    weight_sums[0], weight_sums[1], tail = together(*weight_sums, tail)
-
-    small = weight_sums[0][:, early_rows - small_share : early_rows]
+    mixed = together(*weight_sums, tail)
+    weight_sums, tail = list(mixed[:-1]), mixed[-1]
+
+    small = weight_sums[0][:, -small_share:]
+    late = [(weight_sums[part], part_orders[part][1:]) for part in range(2, 4)]
     small_steps = [("band", step) for step in bit_steps(band_size)]
     small_steps += [("dp", step) for step in turn(bit_steps(dp_size), 1)]
 
     def widen(values, number):
         return jnp.concatenate([values, swap(values, *small_steps[number])], axis=0)
 
+    while any(order for _, order in late):
+        late = over_chips(late)
+    late = [values for values, _ in late]
     tail = total([tail] + [swap(tail, "band", key) for key in other_bands])
     small = widen(small, 0)
-    tail, small, weight_sums[0], weight_sums[1] = together(tail, small, *weight_sums)
-    late_rows = [half_rows[0][number] for number in late_blocks]
-    late = cut_blocks(weight_sums[0][:, early_rows:], late_rows, range(len(late_rows)))
-    late += cut_blocks(weight_sums[1], half_rows[1], range(len(half_rows[1])))
-    last_sum = total(over_band(jnp.concatenate(late, axis=2)))
+    tail, small, late[0], late[1] = together(tail, small, *late)
+    cuts = [cut_blocks(late[part - 2], part_blocks[part]) for part in range(2, 4)]
+    last_sum = total(over_band(jnp.concatenate(cuts, axis=2)))
     for number, step in enumerate(turn(bit_steps(dp_size), 1)):
         got = swap(tail, "dp", step)
         if number + 1 < len(small_steps):
@@ -1424,7 +1458,12 @@
     for number in range(len(bit_steps(dp_size)) + 1, len(small_steps)):
         small = widen(small, number)
     own_grads = jnp.concatenate(
-        [weight_sums[0][0, : early_rows - small_share].astype(f32), last_sum[0]], axis=0
+        [
+            weight_sums[0][0, :-small_share].astype(f32),
+            weight_sums[1][0].astype(f32),
+            last_sum[0],
+        ],
+        axis=0,
     )
     small_order = (jnp.arange(dp_size) ^ spots[0])[:, None] * band_size
     small_order = (small_order + (jnp.arange(band_size) ^ spots[1])[None, :]).reshape(-1)

time: 497 us -> 479 us (0.964)
  Pallas kernels: 192 us -> 183 us
  waiting for transfers between devices: 148 us -> 143 us
    pallas_call x17, Pallas kernels: 192 us -> 183 us  [run_kernel(): pl.pallas_call(whole, in_specs=[pl.BlockSpec(memory_space=pl.ANY)] * coun...]
    ppermute x62 -> x64, waiting for transfers between devices: 148 us -> 143 us  [swap(): lax.ppermute(values, axis, [(spot, spot ^ step) for spot in range(size)])]
    ppermute x62 -> x64, starting transfers between devices: 101 us -> 102 us  [swap(): lax.ppermute(values, axis, [(spot, spot ^ step) for spot in range(size)])]
  transfers between devices with their start and end apart: 62 -> 64, of which waited for: 27 -> 26; matrix products, arithmetic and copies ran while one was open for 7% -> 6% of each run, Pallas kernels for 27% -> 27%
where the time goes in v1:
time: 479 us; the launch traced here: 474 us
  Pallas kernels  183 us (38%)
  waiting for transfers between devices  143 us (30%)
  starting transfers between devices  102 us (21%)
  local copies, waits for them, and re-layouts  23.6 us (5%)
  other arithmetic  20.9 us (4%)
    pallas_call x17, Pallas kernels, run_kernel(): pl.pallas_call(whole, in_specs=[pl.BlockSpec(memory_space=pl.ANY)] * coun...  183 us
    ppermute x64, waiting for transfers between devices, swap(): lax.ppermute(values, axis, [(spot, spot ^ step) for spot in range(size)])  143 us
    ppermute x64, starting transfers between devices, swap(): lax.ppermute(values, axis, [(spot, spot ^ step) for spot in range(size)])  102 us
  transfers between devices with their start and end apart: 64, of which 26 were waited for; matrix products, arithmetic and copies ran while one was open for 6% of the time, Pallas kernels for 27%

profile of v1, /device:TPU:1, one launch (start us, length us, event | category | flops | bytes accessed | tf_op | source)
XLA Modules:
  0.0 473.7 jit_solution(7768842407218768682)
XLA Ops:
  0.7 7.2 %shard_map.323 = (bf16[8,128,768]{2,1,0:T(8,128)(2,1)}, f32[8,768]{1,0:T(8,128)}, bf16[128,128]{1,0:T(8,128)(2,1)}, f32[136,128]{1,0:T(8,128)}, f32[7,136,128]{2...) custom-call(s32[1,128]{1,0:T(1,128)} %bitcast.215, bf16[1,128]{1,0:T(2,128)(2,1)} %bitcast.216, ...), custom_call_target="tpu_custom_call" | custom-call | flops 1000 | bytes 1000 | tf_op jit(solution)/shard_map/pallas_call | solution.py:93
  14.7 18.8 %shard_map.324.refs_1_ = bf16[1024,8192]{1,0:T(8,128)(2,1)} custom-call(bf16[8,128,768]{2,1,0:T(8,128)(2,1)} %get-tuple-element.147.refs_0_, bf16[1024,32,256]{2,1,0:T(8,128)(2,1)} %bitcast.183), custom_call_target="tpu_custom_call" | custom-call | flops 1000 | bytes 1000 | tf_op jit(solution)/shard_map/pallas_call | solution.py:93
  45.7 8.3 %collective-permute-start.6 = (bf16[288,768]{1,0:T(8,128)(2,1)S(1)}, bf16[288,768]{1,0:T(8,128)(2,1)S(1)}, u32[]{:S(2)}, u32[]{:S(2)}) collective-permute-start(bf16[288,768]{1,0:T(8,128)(2,1)S(1)} %copy-done.14), channel_id=1, source_target_pairs={{0,2},{1,3},{2,0},{3,1},{4,6},{5,7},{6,4},{7,5},{8,10},{9,11},{10,... | collective-permute-start | bytes 1327112 | tf_op jit(solution)/shard_map/ppermute | solution.py:39
  54.0 19.0 %collective-permute-done.6.refs_3_ = bf16[288,768]{1,0:T(8,128)(2,1)S(1)} collective-permute-done((bf16[288,768]{1,0:T(8,128)(2,1)S(1)}, bf16[288,768]{1,0:T(8,128)(2,1)S(1)}, u32[]{:S(2)}, u32[]{:S(2)}) %collective-permute-start.6) | collective-permute-done | bytes 442400 | tf_op jit(solution)/shard_map/ppermute | solution.py:39
  79.1 11.0 %collective-permute-done.10.refs_2_ = bf16[288,768]{1,0:T(8,128)(2,1)S(1)} collective-permute-done((bf16[288,768]{1,0:T(8,128)(2,1)S(1)}, bf16[288,768]{1,0:T(8,128)(2,1)S(1)}, u32[]{:S(2)}, u32[]{:S(2)}) %collective-permute-start.10) | collective-permute-done | bytes 442400 | tf_op jit(solution)/shard_map/ppermute | solution.py:39
  90.1 9.0 %collective-permute-done.11.refs_4_ = bf16[288,768]{1,0:T(8,128)(2,1)S(1)} collective-permute-done((bf16[288,768]{1,0:T(8,128)(2,1)S(1)}, bf16[288,768]{1,0:T(8,128)(2,1)S(1)}, u32[]{:S(2)}, u32[]{:S(2)}) %collective-permute-start.11) | collective-permute-done | bytes 442400 | tf_op jit(solution)/shard_map/ppermute | solution.py:39
  99.2 10.3 %collective-permute-done.8.refs_11_.refs_14_ = bf16[2,16,32,768]{3,2,1,0:T(8,128)(2,1)S(1)} collective-permute-done((bf16[2,16,32,768]{3,2,1,0:T(8,128)(2,1)S(1)}, bf16[2,16,32,768]{3,2,1,0:T(8,128)(2,1)S(1)}, u32[]{:S(2)}, u32[]{:S(2)}) %collective-permute-start.8) | collective-permute-done | bytes 1572896 | tf_op jit(solution)/shard_map/ppermute | solution.py:39
  121.5 20.2 %shard_map.327 = (bf16[256,768]{1,0:T(8,128)(2,1)}, bf16[256,768]{1,0:T(8,128)(2,1)}, bf16[256,768]{1,0:T(8,128)(2,1)}, bf16[256,768]{1,0:T(8,128)(2,1)}) custom-call(s32[2]{0:T(128)} %pad_add_fusion.refs_0_.refs_12_.refs_7_, bf16[1024,8192]{1,0:T(8,128)(2,1)} %shard_map.324.refs_1_, bf16[1,32,32,768]{3,2,1,0:T(8,128)(2,1)} %bitcast.175, ...), custom_call_target="tpu_custom_call" | custom-call | flops 1000 | bytes 1000 | tf_op jit(solution)/shard_map/pallas_call | solution.py:93
  151.6 13.4 %collective-permute-done.19.refs_1_ = bf16[256,768]{1,0:T(8,128)(2,1)S(1)} collective-permute-done((bf16[256,768]{1,0:T(8,128)(2,1)}, bf16[256,768]{1,0:T(8,128)(2,1)S(1)}, u32[]{:S(2)}, u32[]{:S(2)}) %collective-permute-start.19) | collective-permute-done | bytes 393248 | tf_op jit(solution)/shard_map/ppermute | solution.py:39
  165.0 10.9 %collective-permute-done.20.refs_2_ = bf16[256,768]{1,0:T(8,128)(2,1)S(1)} collective-permute-done((bf16[256,768]{1,0:T(8,128)(2,1)}, bf16[256,768]{1,0:T(8,128)(2,1)S(1)}, u32[]{:S(2)}, u32[]{:S(2)}) %collective-permute-start.20) | collective-permute-done | bytes 393248 | tf_op jit(solution)/shard_map/ppermute | solution.py:39
  175.9 7.5 %collective-permute-done.18.refs_9_ = bf16[2,576,768]{2,1,0:T(8,128)(2,1)} collective-permute-done((bf16[2,576,768]{2,1,0:T(8,128)(2,1)S(1)}, bf16[2,576,768]{2,1,0:T(8,128)(2,1)}, u32[]{:S(2)}, u32[]{:S(2)}) %collective-permute-start.18) | collective-permute-done | bytes 1769504 | tf_op jit(solution)/shard_map/ppermute | solution.py:39
  199.2 28.1 %shard_map.328 = (bf16[256,768]{1,0:T(8,128)(2,1)}, bf16[256,768]{1,0:T(8,128)(2,1)}, bf16[256,13056]{1,0:T(8,128)(2,1)}, f32[8,768]{1,0:T(8,128)}) custom-call(bf16[256,768]{1,0:T(8,128)(2,1)} %get-tuple-element.175.refs_0_, bf16[256,768]{1,0:T(8,128)(2,1)} %copy-done.32, bf16[256,768]{1,0:T(8,128)(2,1)} %copy-done.33, bf16[256,768]{1,0:T(8,128)(2,1)} %copy-done.34, ...), custom_call_target="tpu_custom_call" | custom-call | flops 1000 | bytes 1000 | tf_op jit(solution)/shard_map/pallas_call | solution.py:93
  231.4 7.1 %collective-permute-done.29.refs_2_ = bf16[256,13056]{1,0:T(8,128)(2,1)} collective-permute-done((bf16[256,13056]{1,0:T(8,128)(2,1)}, bf16[256,13056]{1,0:T(8,128)(2,1)}, u32[]{:S(2)}, u32[]{:S(2)}) %collective-permute-start.29) | collective-permute-done | bytes 6684704 | tf_op jit(solution)/shard_map/ppermute | solution.py:39
  238.5 11.1 %shard_map.329 = (bf16[2,224,768]{2,1,0:T(8,128)(2,1)}, bf16[2,224,768]{2,1,0:T(8,128)(2,1)}, bf16[2,192,768]{2,1,0:T(8,128)(2,1)}, bf16[2,192,768]{2,1,0:T(8,12...) custom-call(s32[2]{0:T(128)} %pad_add_fusion.refs_0_.refs_12_.refs_7, ...), custom_call_target="tpu_custom_call" | custom-call | flops 1000 | bytes 1000 | tf_op jit(solution)/shard_map/pallas_call | solution.py:93
  257.3 12.2 %shard_map.332 = (bf16[8,4,32,768]{3,2,1,0:T(8,128)(2,1)}, bf16[8,4,32,768]{3,2,1,0:T(8,128)(2,1)}, bf16[16,4,32,768]{3,2,1,0:T(8,128)(2,1)}) custom-call(s32[2]{0:T(128)} %pad_add_fusion.refs_0_.refs_12_.refs_7_, bf16[1024,8192]{1,0:T(8,128)(2,1)} %shard_map.324.refs_1_, bf16[256,768]{1,0:T(8,128)(2,1)} %get-tuple-element.197.refs_2_.refs_1_, ...), custom_call_target="tpu_custom_call" | custom-call | flops 1000 | bytes 1000 | tf_op jit(solution)/shard_map/pallas_call | solution.py:93
  271.0 12.2 %shard_map.330 = (bf16[8,4,32,768]{3,2,1,0:T(8,128)(2,1)}, bf16[8,4,32,768]{3,2,1,0:T(8,128)(2,1)}, bf16[16,4,32,768]{3,2,1,0:T(8,128)(2,1)}) custom-call(s32[2]{0:T(128)} %pad_add_fusion.refs_0_.refs_12_.refs_7_, bf16[1024,8192]{1,0:T(8,128)(2,1)} %shard_map.324.refs_1_, bf16[256,768]{1,0:T(8,128)(2,1)} %get-tuple-element.197.refs_2_.refs_1_, ...), custom_call_target="tpu_custom_call" | custom-call | flops 1000 | bytes 1000 | tf_op jit(solution)/shard_map/pallas_call | solution.py:93
  305.6 8.0 %collective-permute-start.38 = (bf16[2,104,768]{2,1,0:T(8,128)(2,1)}, bf16[2,104,768]{2,1,0:T(8,128)(2,1)S(1)}, u32[]{:S(2)}, u32[]{:S(2)}) collective-permute-start(bf16[2,104,768]{2,1,0:T(8,128)(2,1)} %get-tuple-element.289), channel_id=1, source_target_pairs={{0,1},{1,0},{2,3},{3,2},{4,5},{5,4},{6,7},{7,6},{8,9},{9,8},{10,11... | collective-permute-start | bytes 958472 | tf_op jit(solution)/shard_map/ppermute | solution.py:39
  315.7 20.5 %shard_map.334.refs_1_ = bf16[1024,8192]{1,0:T(8,128)(2,1)} custom-call(s32[2]{0:T(128)} %pad_add_fusion.refs_0_.refs_12_.refs_7_, bf16[256,768]{1,0:T(8,128)(2,1)} %get-tuple-element.197.refs_2_.refs_1_, bf16[256,768]{1,0:T(8,128)(2,1)} %copy-done.9, bf16[256,768]{1,0:T(8,128)(2,1)} %copy-done.10, bf16[256,768]{1,0:T(8,128)(2,1)} %copy-done.11, ...), custom_call_target="tpu_custom_call" | custom-call | flops 1000 | bytes 1000 | tf_op jit(solution)/shard_map/pallas_call | solution.py:93
  349.1 9.4 %collective-permute-done.42 = bf16[16,1,32,768]{3,2,0,1:T(8,128)(2,1)} collective-permute-done((bf16[16,1,32,768]{3,2,0,1:T(8,128)(2,1)}, bf16[16,1,32,768]{3,2,0,1:T(8,128)(2,1)}, u32[]{:S(2)}, u32[]{:S(2)}) %collective-permute-start.42) | collective-permute-done | bytes 786464 | tf_op jit(solution)/shard_map/ppermute | solution.py:39
  371.3 7.9 %collective-permute-start.45 = (bf16[8,32,768]{2,1,0:T(8,128)(2,1)}, bf16[8,32,768]{2,1,0:T(8,128)(2,1)}, u32[]{:S(2)}, u32[]{:S(2)}) collective-permute-start(bf16[8,32,768]{2,1,0:T(8,128)(2,1)} %get-tuple-element.279), channel_id=1, source_target_pairs={{0,1},{1,0},{2,3},{3,2},{4,5},{5,4},{6,7},{7,6},{8,9},{9,8},{10,11... | collective-permute-start | bytes 1179656 | tf_op jit(solution)/shard_map/ppermute | solution.py:39
  381.3 18.8 %shard_map.337 = bf16[1024,32,256]{2,1,0:T(8,128)(2,1)} custom-call(bf16[8,32,768]{2,1,0:T(8,128)(2,1)} %get-tuple-element.244.refs_0_.refs_2_, bf16[1024,8192]{1,0:T(8,128)(2,1)} %shard_map.334.refs_1_), custom_call_target="tpu_custom_call" | custom-call | flops 1000 | bytes 1000 | tf_op jit(solution)/shard_map/pallas_call | solution.py:93
  409.0 9.0 %collective-permute-start.48 = (f32[136,128]{1,0:T(8,128)}, f32[136,128]{1,0:T(8,128)S(1)}, u32[]{:S(2)}, u32[]{:S(2)}) collective-permute-start(f32[136,128]{1,0:T(8,128)} %get-tuple-element.250), channel_id=1, source_target_pairs={{0,1},{1,0},{2,3},{3,2},{4,5},{5,4},{6,7},{7,6},{8,9},{9,8},{10,11... | collective-permute-start | bytes 208904 | tf_op jit(solution)/shard_map/ppermute | solution.py:39
  446.1 10.7 %collective-permute-start.58 = (f32[136,128]{1,0:T(8,128)S(1)}, f32[136,128]{1,0:T(8,128)S(1)}, u32[]{:S(2)}, u32[]{:S(2)}) collective-permute-start(f32[136,128]{1,0:T(8,128)S(1)} %add.255), channel_id=1, source_target_pairs={{0,4},{4,0},{8,12},{12,8},{16,20},{20,16},{24,28},{28,24},{1,5},{5... | collective-permute-start | bytes 208904 | tf_op jit(solution)/shard_map/ppermute | solution.py:39
  460.8 8.1 %shard_map.339 = (f32[1,128]{1,0:T(1,128)}, f32[4,128,128]{2,1,0:T(8,128)}, f32[2,128]{1,0:T(2,128)}, f32[128,2048]{1,0:T(8,128)}, f32[2048,128]{1,0:T(8,128)}, /*index=5*/f32[128,768]{1,0:T(8,128)}) custom-call(f32[136,128]{1,0:T(8,128)} %add.256.refs_0_, bf16[4,128,128]{2,1,0:T(8,128)(2,1)} %refs_1_.5, bf16[2,128]{1,0:T(2,128)(2,1)} %refs_2_.5, ...), custom_call_target="tpu_custom_call" | custom-call | flops 1000 | bytes 1000 | tf_op jit(solution)/shard_map/pallas_call | solution.py:93
  (317 shorter events, 173.0 us)
Async XLA Ops:
  9.6 26.2 %collective-permute-start = (bf16[32,8,768]{2,1,0:T(8,128)(2,1)S(1)}, bf16[32,8,768]{2,1,0:T(8,128)(2,1)S(1)}, u32[]{:S(2)}, u32[]{:S(2)}) collective-permute-start(bf16[32,8,768]{2,1,0:T(8,128)(2,1)S(1)} %bitcast.210), channel_id=1, source_target_pairs={{0,1},{1,0},{2,3},{3,2},{4,5},{5,4},{6,7},{7,6},{8,9},{9,8},{10,11... | collective-permute-start | bytes 1179656 | tf_op jit(solution)/shard_map/ppermute | solution.py:39
  39.6 34.2 %collective-permute-start.5 = (bf16[32,32,768]{2,1,0:T(8,128)(2,1)S(1)}, bf16[32,32,768]{2,1,0:T(8,128)(2,1)S(1)}, u32[]{:S(2)}, u32[]{:S(2)}) collective-permute-start(bf16[32,32,768]{2,1,0:T(8,128)(2,1)S(1)} %bitcast.174), channel_id=1, source_target_pairs={{0,4},{4,0},{8,12},{12,8},{16,20},{20,16},{24,28},{28,24},{1,5},{5... | collective-permute-start | bytes 4718600 | tf_op jit(solution)/shard_map/ppermute | solution.py:39
  43.2 29.8 %collective-permute-start.3 = (bf16[1,16,32,768]{3,2,1,0:T(8,128)(2,1)S(1)}, bf16[1,16,32,768]{3,2,1,0:T(8,128)(2,1)S(1)}, u32[]{:S(2)}, u32[]{:S(2)}) collective-permute-start(bf16[1,16,32,768]{3,2,1,0:T(8,128)(2,1)S(1)} %get-tuple-element.282), channel_id=1, source_target_pairs={{0,8},{4,12},{8,0},{12,4},{16,24},{20,28},{24,16},{28,20},{1,9},{5... | collective-permute-start | bytes 2359304 | tf_op jit(solution)/shard_map/ppermute | solution.py:39
  44.5 28.5 %collective-permute-start.4 = (bf16[1,16,32,768]{3,2,1,0:T(8,128)(2,1)S(1)}, bf16[1,16,32,768]{3,2,1,0:T(8,128)(2,1)S(1)}, u32[]{:S(2)}, u32[]{:S(2)}) collective-permute-start(bf16[1,16,32,768]{3,2,1,0:T(8,128)(2,1)S(1)} %get-tuple-element.281), channel_id=1, source_target_pairs={{0,16},{4,20},{8,24},{12,28},{16,0},{20,4},{24,8},{28,12},{1,17},{... | collective-permute-start | bytes 2359304 | tf_op jit(solution)/shard_map/ppermute | solution.py:39
  45.7 27.2 %collective-permute-start.6 = (bf16[288,768]{1,0:T(8,128)(2,1)S(1)}, bf16[288,768]{1,0:T(8,128)(2,1)S(1)}, u32[]{:S(2)}, u32[]{:S(2)}) collective-permute-start(bf16[288,768]{1,0:T(8,128)(2,1)S(1)} %copy-done.14), channel_id=1, source_target_pairs={{0,2},{1,3},{2,0},{3,1},{4,6},{5,7},{6,4},{7,5},{8,10},{9,11},{10,... | collective-permute-start | bytes 1327112 | tf_op jit(solution)/shard_map/ppermute | solution.py:39
  75.1 34.4 %collective-permute-start.8 = (bf16[2,16,32,768]{3,2,1,0:T(8,128)(2,1)S(1)}, bf16[2,16,32,768]{3,2,1,0:T(8,128)(2,1)S(1)}, u32[]{:S(2)}, u32[]{:S(2)}) collective-permute-start(bf16[2,16,32,768]{3,2,1,0:T(8,128)(2,1)S(1)} %pad_maximum_fusion.3), channel_id=1, source_target_pairs={{0,8},{4,12},{8,0},{12,4},{16,24},{20,28},{24,16},{28,20},{1,9},{5... | collective-permute-start | bytes 4718600 | tf_op jit(solution)/shard_map/ppermute | solution.py:39
  75.6 34.1 %collective-permute-start.7 = (bf16[2,16,32,768]{3,2,1,0:T(8,128)(2,1)S(1)}, bf16[2,16,32,768]{3,2,1,0:T(8,128)(2,1)}, u32[]{:S(2)}, u32[]{:S(2)}) collective-permute-start(bf16[2,16,32,768]{3,2,1,0:T(8,128)(2,1)S(1)} %pad_maximum_fusion.2), channel_id=1, source_target_pairs={{0,16},{4,20},{8,24},{12,28},{16,0},{20,4},{24,8},{28,12},{1,17},{... | collective-permute-start | bytes 4718600 | tf_op jit(solution)/shard_map/ppermute | solution.py:39
  116.2 25.5 %collective-permute-start.15 = (bf16[576,768]{1,0:T(8,128)(2,1)}, bf16[576,768]{1,0:T(8,128)(2,1)}, u32[]{:S(2)}, u32[]{:S(2)}) collective-permute-start(bf16[576,768]{1,0:T(8,128)(2,1)} %get-tuple-element.158), channel_id=1, source_target_pairs={{0,8},{4,12},{8,0},{12,4},{16,24},{20,28},{24,16},{28,20},{1,9},{5... | collective-permute-start | bytes 2654216 | tf_op jit(solution)/shard_map/ppermute | solution.py:39
  143.4 40.0 %collective-permute-start.18 = (bf16[2,576,768]{2,1,0:T(8,128)(2,1)S(1)}, bf16[2,576,768]{2,1,0:T(8,128)(2,1)}, u32[]{:S(2)}, u32[]{:S(2)}) collective-permute-start(bf16[2,576,768]{2,1,0:T(8,128)(2,1)S(1)} %pad_maximum_fusion.1.refs_8_), channel_id=1, source_target_pairs={{0,8},{4,12},{8,0},{12,4},{16,24},{20,28},{24,16},{28,20},{1,9},{5... | collective-permute-start | bytes 5308424 | tf_op jit(solution)/shard_map/ppermute | solution.py:39
  146.7 40.2 %collective-permute-start.17 = (bf16[2,576,768]{2,1,0:T(8,128)(2,1)}, bf16[2,576,768]{2,1,0:T(8,128)(2,1)}, u32[]{:S(2)}, u32[]{:S(2)}) collective-permute-start(bf16[2,576,768]{2,1,0:T(8,128)(2,1)} %pad_maximum_fusion.refs_4_), channel_id=1, source_target_pairs={{0,16},{4,20},{8,24},{12,28},{16,0},{20,4},{24,8},{28,12},{1,17},{... | collective-permute-start | bytes 5308424 | tf_op jit(solution)/shard_map/ppermute | solution.py:39
  147.9 28.0 %collective-permute-start.20 = (bf16[256,768]{1,0:T(8,128)(2,1)}, bf16[256,768]{1,0:T(8,128)(2,1)S(1)}, u32[]{:S(2)}, u32[]{:S(2)}) collective-permute-start(bf16[256,768]{1,0:T(8,128)(2,1)} %get-tuple-element.173), channel_id=1, source_target_pairs={{0,2},{1,3},{2,0},{3,1},{4,6},{5,7},{6,4},{7,5},{8,10},{9,11},{10,... | collective-permute-start | bytes 1179656 | tf_op jit(solution)/shard_map/ppermute | solution.py:39
  148.8 27.2 %collective-permute-start.21 = (bf16[256,768]{1,0:T(8,128)(2,1)}, bf16[256,768]{1,0:T(8,128)(2,1)S(1)}, u32[]{:S(2)}, u32[]{:S(2)}) collective-permute-start(bf16[256,768]{1,0:T(8,128)(2,1)} %get-tuple-element.174), channel_id=1, source_target_pairs={{0,3},{1,2},{2,1},{3,0},{4,7},{5,6},{6,5},{7,4},{8,11},{9,10},{10,... | collective-permute-start | bytes 1179656 | tf_op jit(solution)/shard_map/ppermute | solution.py:39
  227.8 28.6 %collective-permute-start.27 = (bf16[256,768]{1,0:T(8,128)(2,1)}, bf16[256,768]{1,0:T(8,128)(2,1)S(1)}, u32[]{:S(2)}, u32[]{:S(2)}) collective-permute-start(bf16[256,768]{1,0:T(8,128)(2,1)} %get-tuple-element.197.refs_2_.refs_1_), channel_id=1, source_target_pairs={{0,2},{1,3},{2,0},{3,1},{4,6},{5,7},{6,4},{7,5},{8,10},{9,11},{10,... | collective-permute-start | bytes 1179656 | tf_op jit(solution)/shard_map/ppermute | solution.py:39
  228.7 27.7 %collective-permute-start.28 = (bf16[256,768]{1,0:T(8,128)(2,1)}, bf16[256,768]{1,0:T(8,128)(2,1)S(1)}, u32[]{:S(2)}, u32[]{:S(2)}) collective-permute-start(bf16[256,768]{1,0:T(8,128)(2,1)} %get-tuple-element.197.refs_2_.refs_1_), channel_id=1, source_target_pairs={{0,3},{1,2},{2,1},{3,0},{4,7},{5,6},{6,5},{7,4},{8,11},{9,10},{10,... | collective-permute-start | bytes 1179656 | tf_op jit(solution)/shard_map/ppermute | solution.py:39
  302.1 35.1 %collective-permute-start.36 = (bf16[16,2,32,768]{3,2,1,0:T(8,128)(2,1)}, bf16[16,2,32,768]{3,2,1,0:T(8,128)(2,1)S(1)}, u32[]{:S(2)}, u32[]{:S(2)}) collective-permute-start(bf16[16,2,32,768]{3,2,1,0:T(8,128)(2,1)} %bitcast.34), channel_id=1, source_target_pairs={{0,8},{4,12},{8,0},{12,4},{16,24},{20,28},{24,16},{28,20},{1,9},{5... | collective-permute-start | bytes 4718600 | tf_op jit(solution)/shard_map/ppermute | solution.py:39
  303.1 34.8 %collective-permute-start.37 = (bf16[16,2,32,768]{3,2,1,0:T(8,128)(2,1)}, bf16[16,2,32,768]{3,2,1,0:T(8,128)(2,1)S(1)}, u32[]{:S(2)}, u32[]{:S(2)}) collective-permute-start(bf16[16,2,32,768]{3,2,1,0:T(8,128)(2,1)} %bitcast.39), channel_id=1, source_target_pairs={{0,16},{4,20},{8,24},{12,28},{16,0},{20,4},{24,8},{28,12},{1,17},{... | collective-permute-start | bytes 4718600 | tf_op jit(solution)/shard_map/ppermute | solution.py:39
  305.6 30.6 %collective-permute-start.38 = (bf16[2,104,768]{2,1,0:T(8,128)(2,1)}, bf16[2,104,768]{2,1,0:T(8,128)(2,1)S(1)}, u32[]{:S(2)}, u32[]{:S(2)}) collective-permute-start(bf16[2,104,768]{2,1,0:T(8,128)(2,1)} %get-tuple-element.289), channel_id=1, source_target_pairs={{0,1},{1,0},{2,3},{3,2},{4,5},{5,4},{6,7},{7,6},{8,9},{9,8},{10,11... | collective-permute-start | bytes 958472 | tf_op jit(solution)/shard_map/ppermute | solution.py:39
  363.6 36.5 %collective-permute-start.44 = (bf16[816,768]{1,0:T(8,128)(2,1)}, bf16[816,768]{1,0:T(8,128)(2,1)}, u32[]{:S(2)}, u32[]{:S(2)}) collective-permute-start(bf16[816,768]{1,0:T(8,128)(2,1)} %pad_maximum_fusion.6), channel_id=1, source_target_pairs={{0,8},{4,12},{8,0},{12,4},{16,24},{20,28},{24,16},{28,20},{1,9},{5... | collective-permute-start | bytes 3760136 | tf_op jit(solution)/shard_map/ppermute | solution.py:39
  364.6 38.2 %collective-permute-start.43 = (bf16[824,768]{1,0:T(8,128)(2,1)S(1)}, bf16[824,768]{1,0:T(8,128)(2,1)S(1)}, u32[]{:S(2)}, u32[]{:S(2)}) collective-permute-start(bf16[824,768]{1,0:T(8,128)(2,1)S(1)} %pad_maximum_fusion.5), channel_id=1, source_target_pairs={{0,16},{4,20},{8,24},{12,28},{16,0},{20,4},{24,8},{28,12},{1,17},{... | collective-permute-start | bytes 3797000 | tf_op jit(solution)/shard_map/ppermute | solution.py:39
  371.3 33.0 %collective-permute-start.45 = (bf16[8,32,768]{2,1,0:T(8,128)(2,1)}, bf16[8,32,768]{2,1,0:T(8,128)(2,1)}, u32[]{:S(2)}, u32[]{:S(2)}) collective-permute-start(bf16[8,32,768]{2,1,0:T(8,128)(2,1)} %get-tuple-element.279), channel_id=1, source_target_pairs={{0,1},{1,0},{2,3},{3,2},{4,5},{5,4},{6,7},{7,6},{8,9},{9,8},{10,11... | collective-permute-start | bytes 1179656 | tf_op jit(solution)/shard_map/ppermute | solution.py:39
  379.2 25.2 %collective-permute-start.47 = (bf16[8,32,768]{2,1,0:T(8,128)(2,1)}, bf16[8,32,768]{2,1,0:T(8,128)(2,1)}, u32[]{:S(2)}, u32[]{:S(2)}) collective-permute-start(bf16[8,32,768]{2,1,0:T(8,128)(2,1)} %get-tuple-element.277), channel_id=1, source_target_pairs={{0,3},{1,2},{2,1},{3,0},{4,7},{5,6},{6,5},{7,4},{8,11},{9,10},{10,... | collective-permute-start | bytes 1179656 | tf_op jit(solution)/shard_map/ppermute | solution.py:39
  438.3 30.6 %collective-permute-start.61 = (bf16[1,192,768]{2,1,0:T(8,128)(2,1)S(1)}, bf16[1,192,768]{2,1,0:T(8,128)(2,1)S(1)}, u32[]{:S(2)}, u32[]{:S(2)}) collective-permute-start(bf16[1,192,768]{2,1,0:T(8,128)(2,1)S(1)} %get-tuple-element.291), channel_id=1, source_target_pairs={{0,1},{1,0},{2,3},{3,2},{4,5},{5,4},{6,7},{7,6},{8,9},{9,8},{10,11... | collective-permute-start | bytes 884744 | tf_op jit(solution)/shard_map/ppermute | solution.py:39
  439.8 29.2 %collective-permute-start.62 = (bf16[1,192,768]{2,1,0:T(8,128)(2,1)S(1)}, bf16[1,192,768]{2,1,0:T(8,128)(2,1)S(1)}, u32[]{:S(2)}, u32[]{:S(2)}) collective-permute-start(bf16[1,192,768]{2,1,0:T(8,128)(2,1)S(1)} %get-tuple-element.293), channel_id=1, source_target_pairs={{0,2},{1,3},{2,0},{3,1},{4,6},{5,7},{6,4},{7,5},{8,10},{9,11},{10,... | collective-permute-start | bytes 884744 | tf_op jit(solution)/shard_map/ppermute | solution.py:39
  440.6 28.3 %collective-permute-start.63 = (bf16[1,192,768]{2,1,0:T(8,128)(2,1)S(1)}, bf16[1,192,768]{2,1,0:T(8,128)(2,1)S(1)}, u32[]{:S(2)}, u32[]{:S(2)}) collective-permute-start(bf16[1,192,768]{2,1,0:T(8,128)(2,1)S(1)} %get-tuple-element.292), channel_id=1, source_target_pairs={{0,3},{1,2},{2,1},{3,0},{4,7},{5,6},{6,5},{7,4},{8,11},{9,10},{10,... | collective-permute-start | bytes 884744 | tf_op jit(solution)/shard_map/ppermute | solution.py:39
  (81 other events, 1194.2 us)

commit v2 on v1

--- a/solution.py
+++ b/solution.py
@@ -1148,6 +1148,46 @@
     return outs[0].reshape(rest), outs[1].reshape(rest)
 
 
+def owners_body(groups, spot_ref, *refs):
+    keep_refs = refs[:groups]
+    got_refs = refs[groups : 2 * groups]
+    *out_refs, hold_ref = refs[2 * groups :]
+    pixels = out_refs[0].shape[0]
+    for group, (keep_ref, got_ref) in enumerate(zip(keep_refs, got_refs)):
+        bands = keep_ref.shape[0]
+        hold_ref[...] = keep_ref[...].astype(jnp.float32) + got_ref[...].astype(jnp.float32)
+        for key, out_ref in enumerate(out_refs):
+            first = pl.multiple_of(jnp.bitwise_xor(spot_ref[1], key) * pixels, pixels)
+            part = hold_ref[:, pl.ds(first, pixels), :]
+            out_ref[:, group * bands : (group + 1) * bands, :] = jnp.swapaxes(part, 0, 1).astype(
+                out_ref.dtype
+            )
+
+
+def by_owner(spots, keeps, gots, band_size):
+    bands, share, width = keeps[0].shape
+    pixels = share // band_size
+    if pixels % 8:
+        whole = jnp.concatenate([add_low(keep, got) for keep, got in zip(keeps, gots)], axis=0)
+        whole = whole.reshape(-1, band_size, pixels, width).transpose(1, 2, 0, 3)
+        return [
+            lax.dynamic_index_in_dim(whole, spots[1] ^ key, 0, keepdims=False)
+            for key in range(band_size)
+        ]
+    inside = pl.BlockSpec(memory_space=pltpu.VMEM)
+    return run_kernel(
+        partial(owners_body, len(keeps)),
+        (spots, *keeps, *gots),
+        [pl.BlockSpec(memory_space=pltpu.SMEM)] + [inside] * (2 * len(keeps)),
+        out_shape=[
+            jax.ShapeDtypeStruct((pixels, bands * len(keeps), width), keeps[0].dtype)
+        ]
+        * band_size,
+        out_specs=[inside] * band_size,
+        scratch_shapes=[pltpu.VMEM((bands, share, width), jnp.float32)],
+    )
+
+
 def shards(
     patches,
     bias_token,
@@ -1307,8 +1347,8 @@
 
     small_share = row_total // device_count
     block_rows = weight_rows + [small_share]
-    part_blocks = [[0, 1, 9], [2, 3], [4, 5, 6, 7], [8]]
-    part_orders = [orders[0], orders[1], orders[0], orders[1]]
+    part_blocks = [[0, 9], [1], [2], [3], [4, 5, 6, 7], [8]]
+    part_orders = [orders[0], orders[1], orders[1], orders[0], orders[0], orders[1]]
     weight_parts = [(order[0], numbers) for order, numbers in zip(part_orders, part_blocks)]
     grads = [grad_embed] + [swap(grad_embed, "band", key) for key in other_bands]
     weight_split = weight_grad(
@@ -1380,18 +1420,31 @@
     for stage in range(len(dp_steps)):
         last = stage == len(dp_steps) - 1
         got = [swap(kernel_split[2 * group], "dp", orders[group][stage]) for group in range(groups)]
+        part = 2 + stage
+        cuts = [
+            cut_blocks(weight_keep[part], part_blocks[part]),
+            cut_blocks(weight_send[part], part_blocks[part]),
+        ]
         if stage == 0:
-            cuts = [
-                cut_blocks(add_low(weight_keep[part], weight_got[part]), part_blocks[part])
-                for part in range(2)
+            cuts += [
+                cut_blocks(add_low(weight_keep[early], weight_got[early]), part_blocks[early])
+                for early in range(2)
             ]
+        part_got = [None]
+        if stage < 2:
             part_got = over_band(jnp.concatenate(cuts, axis=2))
+        if stage == 0:
             got[0], got[1], update, *part_got = together(*got, update, *part_got)
-            early = total(part_got).astype(bf16)
-            early_rows = cuts[0].shape[2]
-            early = [early[:, :early_rows], early[:, early_rows:]]
         else:
-            got[0], got[1], early[0], early[1] = together(*got, *early)
+            got[0], got[1], *part_got = together(*got, *part_got)
+        if stage < 2:
+            summed = total(part_got).astype(bf16)
+            rows = [cut.shape[2] for cut in cuts]
+            spots_in = [sum(rows[:number]) for number in range(len(rows))]
+            summed = [summed[:, first : first + size] for first, size in zip(spots_in, rows)]
+            weight_keep[part], weight_send[part] = summed[:2]
+            if stage == 0:
+                early = summed[2:]
         if not last:
             kernel_split = [
                 part
@@ -1405,21 +1458,21 @@
                     orders[group][stage + 1 :],
                 )
             ]
-    kernel_sums = [add_low(kernel_split[2 * group + 1], got[group]) for group in range(groups)]
-
-    own_part = jnp.concatenate(kernel_sums, axis=0)
-    own_part = own_part.reshape(bands_dev, band_size, own_pixels, model_width)
-    own_part = own_part.transpose(1, 2, 0, 3)
-    sent = [
-        lax.dynamic_index_in_dim(own_part, spot ^ key, 0, keepdims=False)
-        for key in range(band_size)
-    ]
+    sent = by_owner(
+        spots,
+        [
+            kernel_split[2 * group + 1].reshape(group_bands, share, model_width)
+            for group in range(groups)
+        ],
+        [got[group].reshape(group_bands, share, model_width) for group in range(groups)],
+        band_size,
+    )
     pieces = [sent[0]] + [swap(sent[key], "band", key) for key in other_bands]
     sums_left = over_chips(
         [(early[part], part_orders[part][1:]) for part in range(2)]
         + [
             ((weight_send[part], weight_keep[part]), part_orders[part])
-            for part in range(2, 4)
+            for part in range(2, len(part_blocks))
         ]
     )
     while any(order for _, order in sums_left[:2]):
@@ -1428,13 +1481,14 @@
     weight_sums = [values for values, _ in sums_left]
     grad_patches = unflatten_rows([update], bands_dev, (sent[0],))
     mixed = together(*weight_sums, grad_patches, *pieces)
-    weight_sums, grad_patches, pieces = list(mixed[:4]), mixed[4], mixed[5:]
+    count = len(part_blocks)
+    weight_sums, grad_patches, pieces = list(mixed[:count]), mixed[count], mixed[count + 1 :]
     grad_gen_kernel, tail = states_grad(spots, band_states, gen_kernel, pieces, sums)
     mixed = together(*weight_sums, tail)
     weight_sums, tail = list(mixed[:-1]), mixed[-1]
 
     small = weight_sums[0][:, -small_share:]
-    late = [(weight_sums[part], part_orders[part][1:]) for part in range(2, 4)]
+    late = [(weight_sums[part], part_orders[part][1:]) for part in range(2, count)]
     small_steps = [("band", step) for step in bit_steps(band_size)]
     small_steps += [("dp", step) for step in turn(bit_steps(dp_size), 1)]
 
@@ -1445,22 +1499,25 @@
         late = over_chips(late)
     late = [values for values, _ in late]
     tail = total([tail] + [swap(tail, "band", key) for key in other_bands])
+    tail_steps = bit_steps(dp_size)
+    tail = tail + swap(tail, "dp", tail_steps[0])
+    tail, *late = together(tail, *late)
+    cuts = [cut_blocks(late[part - 2], part_blocks[part]) for part in range(4, count)]
+    last_sum = total(over_band(jnp.concatenate(cuts, axis=2)))
     small = widen(small, 0)
-    tail, small, late[0], late[1] = together(tail, small, *late)
-    cuts = [cut_blocks(late[part - 2], part_blocks[part]) for part in range(2, 4)]
-    last_sum = total(over_band(jnp.concatenate(cuts, axis=2)))
-    for number, step in enumerate(turn(bit_steps(dp_size), 1)):
+    for number, step in enumerate(tail_steps[1:]):
         got = swap(tail, "dp", step)
-        if number + 1 < len(small_steps):
-            small = widen(small, number + 1)
+        small = widen(small, number + 1)
         got, small = together(got, small)
         tail = tail + got
-    for number in range(len(bit_steps(dp_size)) + 1, len(small_steps)):
+    for number in range(len(tail_steps), len(small_steps)):
         small = widen(small, number)
     own_grads = jnp.concatenate(
         [
             weight_sums[0][0, :-small_share].astype(f32),
             weight_sums[1][0].astype(f32),
+            late[0][0].astype(f32),
+            late[1][0].astype(f32),
             last_sum[0],
         ],
         axis=0,

time: 479 us -> 470 us (0.981)
  waiting for transfers between devices: 143 us -> 120 us
  starting transfers between devices: 102 us -> 108 us
    ppermute x64 -> x67, waiting for transfers between devices: 143 us -> 120 us  [swap(): lax.ppermute(values, axis, [(spot, spot ^ step) for spot in range(size)])]
    ppermute x64 -> x67, starting transfers between devices: 102 us -> 108 us  [swap(): lax.ppermute(values, axis, [(spot, spot ^ step) for spot in range(size)])]
    pallas_call x17 -> x18, Pallas kernels: 183 us -> 187 us  [run_kernel(): pl.pallas_call(whole, in_specs=[pl.BlockSpec(memory_space=pl.ANY)] * coun...]
    unnamed x90 -> x96, local copies, waits for them, and re-layouts: 7.48 us -> 11.2 us
  transfers between devices with their start and end apart: 64 -> 67, of which waited for: 26 -> 22; matrix products, arithmetic and copies ran while one was open for 6% -> 7% of each run, Pallas kernels for 27% -> 29%
where the time goes in v2:
time: 470 us; the launch traced here: 465 us
  Pallas kernels  187 us (40%)
  waiting for transfers between devices  120 us (26%)
  starting transfers between devices  108 us (23%)
  local copies, waits for them, and re-layouts  25.5 us (5%)
  other arithmetic  22.9 us (5%)
    pallas_call x18, Pallas kernels, run_kernel(): pl.pallas_call(whole, in_specs=[pl.BlockSpec(memory_space=pl.ANY)] * coun...  187 us
    ppermute x67, waiting for transfers between devices, swap(): lax.ppermute(values, axis, [(spot, spot ^ step) for spot in range(size)])  120 us
    ppermute x67, starting transfers between devices, swap(): lax.ppermute(values, axis, [(spot, spot ^ step) for spot in range(size)])  108 us
    unnamed x96, local copies, waits for them, and re-layouts  11.2 us
  transfers between devices with their start and end apart: 67, of which 22 were waited for; matrix products, arithmetic and copies ran while one was open for 7% of the time, Pallas kernels for 29%

profile of v2, /device:TPU:1, one launch (start us, length us, event | category | flops | bytes accessed | tf_op | source)
XLA Modules:
  0.0 464.9 jit_solution(8321168638064931109)
XLA Ops:
  0.7 7.2 %shard_map.323 = (bf16[8,128,768]{2,1,0:T(8,128)(2,1)}, f32[8,768]{1,0:T(8,128)}, bf16[128,128]{1,0:T(8,128)(2,1)}, f32[136,128]{1,0:T(8,128)}, f32[7,136,128]{2...) custom-call(s32[1,128]{1,0:T(1,128)} %bitcast.250, bf16[1,128]{1,0:T(2,128)(2,1)} %bitcast.251, ...), custom_call_target="tpu_custom_call" | custom-call | flops 1000 | bytes 1000 | tf_op jit(solution)/shard_map/pallas_call | solution.py:93
  14.7 18.8 %shard_map.324.refs_1_ = bf16[1024,8192]{1,0:T(8,128)(2,1)} custom-call(bf16[8,128,768]{2,1,0:T(8,128)(2,1)} %get-tuple-element.164.refs_0_, bf16[1024,32,256]{2,1,0:T(8,128)(2,1)} %bitcast.211), custom_call_target="tpu_custom_call" | custom-call | flops 1000 | bytes 1000 | tf_op jit(solution)/shard_map/pallas_call | solution.py:93
  45.7 8.3 %collective-permute-start.6 = (bf16[288,768]{1,0:T(8,128)(2,1)S(1)}, bf16[288,768]{1,0:T(8,128)(2,1)S(1)}, u32[]{:S(2)}, u32[]{:S(2)}) collective-permute-start(bf16[288,768]{1,0:T(8,128)(2,1)S(1)} %copy-done.14), channel_id=1, source_target_pairs={{0,2},{1,3},{2,0},{3,1},{4,6},{5,7},{6,4},{7,5},{8,10},{9,11},{10,... | collective-permute-start | bytes 1327112 | tf_op jit(solution)/shard_map/ppermute | solution.py:39
  54.0 19.0 %collective-permute-done.6.refs_3_ = bf16[288,768]{1,0:T(8,128)(2,1)S(1)} collective-permute-done((bf16[288,768]{1,0:T(8,128)(2,1)S(1)}, bf16[288,768]{1,0:T(8,128)(2,1)S(1)}, u32[]{:S(2)}, u32[]{:S(2)}) %collective-permute-start.6) | collective-permute-done | bytes 442400 | tf_op jit(solution)/shard_map/ppermute | solution.py:39
  79.2 11.0 %collective-permute-done.10.refs_2_ = bf16[288,768]{1,0:T(8,128)(2,1)S(1)} collective-permute-done((bf16[288,768]{1,0:T(8,128)(2,1)S(1)}, bf16[288,768]{1,0:T(8,128)(2,1)S(1)}, u32[]{:S(2)}, u32[]{:S(2)}) %collective-permute-start.10) | collective-permute-done | bytes 442400 | tf_op jit(solution)/shard_map/ppermute | solution.py:39
  90.2 9.0 %collective-permute-done.11.refs_4_ = bf16[288,768]{1,0:T(8,128)(2,1)S(1)} collective-permute-done((bf16[288,768]{1,0:T(8,128)(2,1)S(1)}, bf16[288,768]{1,0:T(8,128)(2,1)S(1)}, u32[]{:S(2)}, u32[]{:S(2)}) %collective-permute-start.11) | collective-permute-done | bytes 442400 | tf_op jit(solution)/shard_map/ppermute | solution.py:39
  99.2 10.3 %collective-permute-done.8.refs_11_.refs_14_ = bf16[2,16,32,768]{3,2,1,0:T(8,128)(2,1)S(1)} collective-permute-done((bf16[2,16,32,768]{3,2,1,0:T(8,128)(2,1)S(1)}, bf16[2,16,32,768]{3,2,1,0:T(8,128)(2,1)S(1)}, u32[]{:S(2)}, u32[]{:S(2)}) %collective-permute-start.8) | collective-permute-done | bytes 1572896 | tf_op jit(solution)/shard_map/ppermute | solution.py:39
  121.5 20.3 %shard_map.327 = (bf16[256,768]{1,0:T(8,128)(2,1)}, bf16[256,768]{1,0:T(8,128)(2,1)}, bf16[256,768]{1,0:T(8,128)(2,1)}, bf16[256,768]{1,0:T(8,128)(2,1)}) custom-call(s32[2]{0:T(128)} %pad_add_fusion.refs_0_.refs_12_.refs_7_, bf16[1024,8192]{1,0:T(8,128)(2,1)} %shard_map.324.refs_1_, bf16[1,32,32,768]{3,2,1,0:T(8,128)(2,1)} %bitcast.203, ...), custom_call_target="tpu_custom_call" | custom-call | flops 1000 | bytes 1000 | tf_op jit(solution)/shard_map/pallas_call | solution.py:93
  151.5 13.4 %collective-permute-done.19.refs_1_ = bf16[256,768]{1,0:T(8,128)(2,1)S(1)} collective-permute-done((bf16[256,768]{1,0:T(8,128)(2,1)}, bf16[256,768]{1,0:T(8,128)(2,1)S(1)}, u32[]{:S(2)}, u32[]{:S(2)}) %collective-permute-start.19) | collective-permute-done | bytes 393248 | tf_op jit(solution)/shard_map/ppermute | solution.py:39
  164.9 10.9 %collective-permute-done.20.refs_2_ = bf16[256,768]{1,0:T(8,128)(2,1)S(1)} collective-permute-done((bf16[256,768]{1,0:T(8,128)(2,1)}, bf16[256,768]{1,0:T(8,128)(2,1)S(1)}, u32[]{:S(2)}, u32[]{:S(2)}) %collective-permute-start.20) | collective-permute-done | bytes 393248 | tf_op jit(solution)/shard_map/ppermute | solution.py:39
  175.8 7.5 %collective-permute-done.18.refs_9_ = bf16[2,576,768]{2,1,0:T(8,128)(2,1)} collective-permute-done((bf16[2,576,768]{2,1,0:T(8,128)(2,1)S(1)}, bf16[2,576,768]{2,1,0:T(8,128)(2,1)}, u32[]{:S(2)}, u32[]{:S(2)}) %collective-permute-start.18) | collective-permute-done | bytes 1769504 | tf_op jit(solution)/shard_map/ppermute | solution.py:39
  199.2 28.2 %shard_map.328 = (bf16[256,768]{1,0:T(8,128)(2,1)}, bf16[256,768]{1,0:T(8,128)(2,1)}, bf16[256,13056]{1,0:T(8,128)(2,1)}, f32[8,768]{1,0:T(8,128)}) custom-call(bf16[256,768]{1,0:T(8,128)(2,1)} %get-tuple-element.192.refs_0_, bf16[256,768]{1,0:T(8,128)(2,1)} %copy-done.30, bf16[256,768]{1,0:T(8,128)(2,1)} %copy-done.31, bf16[256,768]{1,0:T(8,128)(2,1)} %copy-done.32, ...), custom_call_target="tpu_custom_call" | custom-call | flops 1000 | bytes 1000 | tf_op jit(solution)/shard_map/pallas_call | solution.py:93
  231.3 7.1 %collective-permute-done.29.refs_2_ = bf16[256,13056]{1,0:T(8,128)(2,1)} collective-permute-done((bf16[256,13056]{1,0:T(8,128)(2,1)}, bf16[256,13056]{1,0:T(8,128)(2,1)}, u32[]{:S(2)}, u32[]{:S(2)}) %collective-permute-start.29) | collective-permute-done | bytes 6684704 | tf_op jit(solution)/shard_map/ppermute | solution.py:39
  238.5 11.2 %shard_map.329 = (bf16[2,128,768]{2,1,0:T(8,128)(2,1)}, bf16[2,128,768]{2,1,0:T(8,128)(2,1)}, bf16[2,96,768]{2,1,0:T(8,128)(2,1)}, bf16[2,96,768]{2,1,0:T(8,128)...) custom-call(s32[2]{0:T(128)} %pad_add_fusion.refs_0_.refs_12_.refs_7, ...), custom_call_target="tpu_custom_call" | custom-call | flops 1000 | bytes 1000 | tf_op jit(solution)/shard_map/pallas_call | solution.py:93
  249.7 6.7 %collective-permute-done.27.refs_4_.refs_3_ = bf16[256,768]{1,0:T(8,128)(2,1)S(1)} collective-permute-done((bf16[256,768]{1,0:T(8,128)(2,1)}, bf16[256,768]{1,0:T(8,128)(2,1)S(1)}, u32[]{:S(2)}, u32[]{:S(2)}) %collective-permute-start.27) | collective-permute-done | bytes 393248 | tf_op jit(solution)/shard_map/ppermute | solution.py:39
  257.2 12.3 %shard_map.332 = (bf16[8,4,32,768]{3,2,1,0:T(8,128)(2,1)}, bf16[8,4,32,768]{3,2,1,0:T(8,128)(2,1)}, bf16[16,4,32,768]{3,2,1,0:T(8,128)(2,1)}) custom-call(s32[2]{0:T(128)} %pad_add_fusion.refs_0_.refs_12_.refs_7_, bf16[1024,8192]{1,0:T(8,128)(2,1)} %shard_map.324.refs_1_, bf16[256,768]{1,0:T(8,128)(2,1)} %get-tuple-element.218.refs_2_.refs_1_, ...), custom_call_target="tpu_custom_call" | custom-call | flops 1000 | bytes 1000 | tf_op jit(solution)/shard_map/pallas_call | solution.py:93
  271.0 12.2 %shard_map.330 = (bf16[8,4,32,768]{3,2,1,0:T(8,128)(2,1)}, bf16[8,4,32,768]{3,2,1,0:T(8,128)(2,1)}, bf16[16,4,32,768]{3,2,1,0:T(8,128)(2,1)}) custom-call(s32[2]{0:T(128)} %pad_add_fusion.refs_0_.refs_12_.refs_7_, bf16[1024,8192]{1,0:T(8,128)(2,1)} %shard_map.324.refs_1_, bf16[256,768]{1,0:T(8,128)(2,1)} %get-tuple-element.218.refs_2_.refs_1_, ...), custom_call_target="tpu_custom_call" | custom-call | flops 1000 | bytes 1000 | tf_op jit(solution)/shard_map/pallas_call | solution.py:93
  304.1 8.0 %collective-permute-start.38 = (bf16[2,104,768]{2,1,0:T(8,128)(2,1)}, bf16[2,104,768]{2,1,0:T(8,128)(2,1)}, u32[]{:S(2)}, u32[]{:S(2)}) collective-permute-start(bf16[2,104,768]{2,1,0:T(8,128)(2,1)} %get-tuple-element.319), channel_id=1, source_target_pairs={{0,1},{1,0},{2,3},{3,2},{4,5},{5,4},{6,7},{7,6},{8,9},{9,8},{10,11... | collective-permute-start | bytes 958472 | tf_op jit(solution)/shard_map/ppermute | solution.py:39
  314.2 20.4 %shard_map.334.refs_1_ = bf16[1024,8192]{1,0:T(8,128)(2,1)} custom-call(s32[2]{0:T(128)} %pad_add_fusion.refs_0_.refs_12_.refs_7_, bf16[256,768]{1,0:T(8,128)(2,1)} %get-tuple-element.218.refs_2_.refs_1_, bf16[256,768]{1,0:T(8,128)(2,1)} %copy-done.9, bf16[256,768]{1,0:T(8,128)(2,1)} %copy-done.10, bf16[256,768]{1,0:T(8,128)(2,1)} %copy-done.11, ...), custom_call_target="tpu_custom_call" | custom-call | flops 1000 | bytes 1000 | tf_op jit(solution)/shard_map/pallas_call | solution.py:93
  377.6 18.8 %shard_map.338 = bf16[1024,32,256]{2,1,0:T(8,128)(2,1)} custom-call(bf16[8,32,768]{2,1,0:T(8,128)(2,1)} %get-tuple-element.277.refs_0_.refs_2_, bf16[1024,8192]{1,0:T(8,128)(2,1)} %shard_map.334.refs_1_), custom_call_target="tpu_custom_call" | custom-call | flops 1000 | bytes 1000 | tf_op jit(solution)/shard_map/pallas_call | solution.py:93
  406.1 8.2 %collective-permute-start.51 = (f32[136,128]{1,0:T(8,128)}, f32[136,128]{1,0:T(8,128)S(1)}, u32[]{:S(2)}, u32[]{:S(2)}) collective-permute-start(f32[136,128]{1,0:T(8,128)} %get-tuple-element.283), channel_id=1, source_target_pairs={{0,1},{1,0},{2,3},{3,2},{4,5},{5,4},{6,7},{7,6},{8,9},{9,8},{10,11... | collective-permute-start | bytes 208904 | tf_op jit(solution)/shard_map/ppermute | solution.py:39
  421.3 6.9 %collective-permute-start.54 = (f32[136,128]{1,0:T(8,128)S(1)}, f32[136,128]{1,0:T(8,128)S(1)}, u32[]{:S(2)}, u32[]{:S(2)}) collective-permute-start(f32[136,128]{1,0:T(8,128)S(1)} %add_add_fusion), channel_id=1, source_target_pairs={{0,4},{4,0},{8,12},{12,8},{16,20},{20,16},{24,28},{28,24},{1,5},{5... | collective-permute-start | bytes 208904 | tf_op jit(solution)/shard_map/ppermute | solution.py:39
  441.6 8.1 %shard_map.340 = (f32[1,128]{1,0:T(1,128)}, f32[4,128,128]{2,1,0:T(8,128)}, f32[2,128]{1,0:T(2,128)}, f32[128,2048]{1,0:T(8,128)}, f32[2048,128]{1,0:T(8,128)}, /*index=5*/f32[128,768]{1,0:T(8,128)}) custom-call(f32[136,128]{1,0:T(8,128)} %add.282.refs_0_, bf16[4,128,128]{2,1,0:T(8,128)(2,1)} %refs_1_.5, bf16[2,128]{1,0:T(2,128)(2,1)} %refs_2_.5, ...), custom_call_target="tpu_custom_call" | custom-call | flops 1000 | bytes 1000 | tf_op jit(solution)/shard_map/pallas_call | solution.py:93
  449.7 10.4 %collective-permute-start.63 = (bf16[16,8,768]{2,1,0:T(8,128)(2,1)S(1)}, bf16[16,8,768]{2,1,0:T(8,128)(2,1)S(1)}, u32[]{:S(2)}, u32[]{:S(2)}) collective-permute-start(bf16[16,8,768]{2,1,0:T(8,128)(2,1)S(1)} %pad_maximum_fusion.10), channel_id=1, source_target_pairs={{0,4},{4,0},{8,12},{12,8},{16,20},{20,16},{24,28},{28,24},{1,5},{5... | collective-permute-start | bytes 589832 | tf_op jit(solution)/shard_map/ppermute | solution.py:39
  (336 shorter events, 168.8 us)
Async XLA Ops:
  9.6 26.2 %collective-permute-start = (bf16[32,8,768]{2,1,0:T(8,128)(2,1)S(1)}, bf16[32,8,768]{2,1,0:T(8,128)(2,1)S(1)}, u32[]{:S(2)}, u32[]{:S(2)}) collective-permute-start(bf16[32,8,768]{2,1,0:T(8,128)(2,1)S(1)} %bitcast.235), channel_id=1, source_target_pairs={{0,1},{1,0},{2,3},{3,2},{4,5},{5,4},{6,7},{7,6},{8,9},{9,8},{10,11... | collective-permute-start | bytes 1179656 | tf_op jit(solution)/shard_map/ppermute | solution.py:39
  39.6 34.1 %collective-permute-start.5 = (bf16[32,32,768]{2,1,0:T(8,128)(2,1)S(1)}, bf16[32,32,768]{2,1,0:T(8,128)(2,1)S(1)}, u32[]{:S(2)}, u32[]{:S(2)}) collective-permute-start(bf16[32,32,768]{2,1,0:T(8,128)(2,1)S(1)} %bitcast.202), channel_id=1, source_target_pairs={{0,4},{4,0},{8,12},{12,8},{16,20},{20,16},{24,28},{28,24},{1,5},{5... | collective-permute-start | bytes 4718600 | tf_op jit(solution)/shard_map/ppermute | solution.py:39
  43.2 29.8 %collective-permute-start.3 = (bf16[1,16,32,768]{3,2,1,0:T(8,128)(2,1)S(1)}, bf16[1,16,32,768]{3,2,1,0:T(8,128)(2,1)S(1)}, u32[]{:S(2)}, u32[]{:S(2)}) collective-permute-start(bf16[1,16,32,768]{3,2,1,0:T(8,128)(2,1)S(1)} %get-tuple-element.312), channel_id=1, source_target_pairs={{0,8},{4,12},{8,0},{12,4},{16,24},{20,28},{24,16},{28,20},{1,9},{5... | collective-permute-start | bytes 2359304 | tf_op jit(solution)/shard_map/ppermute | solution.py:39
  44.5 28.5 %collective-permute-start.4 = (bf16[1,16,32,768]{3,2,1,0:T(8,128)(2,1)S(1)}, bf16[1,16,32,768]{3,2,1,0:T(8,128)(2,1)S(1)}, u32[]{:S(2)}, u32[]{:S(2)}) collective-permute-start(bf16[1,16,32,768]{3,2,1,0:T(8,128)(2,1)S(1)} %get-tuple-element.311), channel_id=1, source_target_pairs={{0,16},{4,20},{8,24},{12,28},{16,0},{20,4},{24,8},{28,12},{1,17},{... | collective-permute-start | bytes 2359304 | tf_op jit(solution)/shard_map/ppermute | solution.py:39
  45.7 27.2 %collective-permute-start.6 = (bf16[288,768]{1,0:T(8,128)(2,1)S(1)}, bf16[288,768]{1,0:T(8,128)(2,1)S(1)}, u32[]{:S(2)}, u32[]{:S(2)}) collective-permute-start(bf16[288,768]{1,0:T(8,128)(2,1)S(1)} %copy-done.14), channel_id=1, source_target_pairs={{0,2},{1,3},{2,0},{3,1},{4,6},{5,7},{6,4},{7,5},{8,10},{9,11},{10,... | collective-permute-start | bytes 1327112 | tf_op jit(solution)/shard_map/ppermute | solution.py:39
  75.2 34.4 %collective-permute-start.8 = (bf16[2,16,32,768]{3,2,1,0:T(8,128)(2,1)S(1)}, bf16[2,16,32,768]{3,2,1,0:T(8,128)(2,1)S(1)}, u32[]{:S(2)}, u32[]{:S(2)}) collective-permute-start(bf16[2,16,32,768]{3,2,1,0:T(8,128)(2,1)S(1)} %pad_maximum_fusion.3), channel_id=1, source_target_pairs={{0,8},{4,12},{8,0},{12,4},{16,24},{20,28},{24,16},{28,20},{1,9},{5... | collective-permute-start | bytes 4718600 | tf_op jit(solution)/shard_map/ppermute | solution.py:39
  75.6 34.1 %collective-permute-start.7 = (bf16[2,16,32,768]{3,2,1,0:T(8,128)(2,1)S(1)}, bf16[2,16,32,768]{3,2,1,0:T(8,128)(2,1)}, u32[]{:S(2)}, u32[]{:S(2)}) collective-permute-start(bf16[2,16,32,768]{3,2,1,0:T(8,128)(2,1)S(1)} %pad_maximum_fusion.2), channel_id=1, source_target_pairs={{0,16},{4,20},{8,24},{12,28},{16,0},{20,4},{24,8},{28,12},{1,17},{... | collective-permute-start | bytes 4718600 | tf_op jit(solution)/shard_map/ppermute | solution.py:39
  143.3 40.0 %collective-permute-start.18 = (bf16[2,576,768]{2,1,0:T(8,128)(2,1)S(1)}, bf16[2,576,768]{2,1,0:T(8,128)(2,1)}, u32[]{:S(2)}, u32[]{:S(2)}) collective-permute-start(bf16[2,576,768]{2,1,0:T(8,128)(2,1)S(1)} %pad_maximum_fusion.1.refs_8_), channel_id=1, source_target_pairs={{0,8},{4,12},{8,0},{12,4},{16,24},{20,28},{24,16},{28,20},{1,9},{5... | collective-permute-start | bytes 5308424 | tf_op jit(solution)/shard_map/ppermute | solution.py:39
  146.6 40.2 %collective-permute-start.17 = (bf16[2,576,768]{2,1,0:T(8,128)(2,1)}, bf16[2,576,768]{2,1,0:T(8,128)(2,1)}, u32[]{:S(2)}, u32[]{:S(2)}) collective-permute-start(bf16[2,576,768]{2,1,0:T(8,128)(2,1)} %pad_maximum_fusion.refs_4_), channel_id=1, source_target_pairs={{0,16},{4,20},{8,24},{12,28},{16,0},{20,4},{24,8},{28,12},{1,17},{... | collective-permute-start | bytes 5308424 | tf_op jit(solution)/shard_map/ppermute | solution.py:39
  147.8 28.0 %collective-permute-start.20 = (bf16[256,768]{1,0:T(8,128)(2,1)}, bf16[256,768]{1,0:T(8,128)(2,1)S(1)}, u32[]{:S(2)}, u32[]{:S(2)}) collective-permute-start(bf16[256,768]{1,0:T(8,128)(2,1)} %get-tuple-element.190), channel_id=1, source_target_pairs={{0,2},{1,3},{2,0},{3,1},{4,6},{5,7},{6,4},{7,5},{8,10},{9,11},{10,... | collective-permute-start | bytes 1179656 | tf_op jit(solution)/shard_map/ppermute | solution.py:39
  148.7 27.2 %collective-permute-start.21 = (bf16[256,768]{1,0:T(8,128)(2,1)}, bf16[256,768]{1,0:T(8,128)(2,1)S(1)}, u32[]{:S(2)}, u32[]{:S(2)}) collective-permute-start(bf16[256,768]{1,0:T(8,128)(2,1)} %get-tuple-element.191), channel_id=1, source_target_pairs={{0,3},{1,2},{2,1},{3,0},{4,7},{5,6},{6,5},{7,4},{8,11},{9,10},{10,... | collective-permute-start | bytes 1179656 | tf_op jit(solution)/shard_map/ppermute | solution.py:39
  227.8 28.6 %collective-permute-start.27 = (bf16[256,768]{1,0:T(8,128)(2,1)}, bf16[256,768]{1,0:T(8,128)(2,1)S(1)}, u32[]{:S(2)}, u32[]{:S(2)}) collective-permute-start(bf16[256,768]{1,0:T(8,128)(2,1)} %get-tuple-element.218.refs_2_.refs_1_), channel_id=1, source_target_pairs={{0,2},{1,3},{2,0},{3,1},{4,6},{5,7},{6,4},{7,5},{8,10},{9,11},{10,... | collective-permute-start | bytes 1179656 | tf_op jit(solution)/shard_map/ppermute | solution.py:39
  228.6 27.7 %collective-permute-start.28 = (bf16[256,768]{1,0:T(8,128)(2,1)}, bf16[256,768]{1,0:T(8,128)(2,1)S(1)}, u32[]{:S(2)}, u32[]{:S(2)}) collective-permute-start(bf16[256,768]{1,0:T(8,128)(2,1)} %get-tuple-element.218.refs_2_.refs_1_), channel_id=1, source_target_pairs={{0,3},{1,2},{2,1},{3,0},{4,7},{5,6},{6,5},{7,4},{8,11},{9,10},{10,... | collective-permute-start | bytes 1179656 | tf_op jit(solution)/shard_map/ppermute | solution.py:39
  297.0 40.0 %collective-permute-start.36 = (bf16[16,2,32,768]{3,2,1,0:T(8,128)(2,1)}, bf16[16,2,32,768]{3,2,1,0:T(8,128)(2,1)S(1)}, u32[]{:S(2)}, u32[]{:S(2)}) collective-permute-start(bf16[16,2,32,768]{3,2,1,0:T(8,128)(2,1)} %bitcast.253), channel_id=1, source_target_pairs={{0,8},{4,12},{8,0},{12,4},{16,24},{20,28},{24,16},{28,20},{1,9},{5... | collective-permute-start | bytes 4718600 | tf_op jit(solution)/shard_map/ppermute | solution.py:39
  297.6 39.4 %collective-permute-start.37 = (bf16[16,2,32,768]{3,2,1,0:T(8,128)(2,1)}, bf16[16,2,32,768]{3,2,1,0:T(8,128)(2,1)S(1)}, u32[]{:S(2)}, u32[]{:S(2)}) collective-permute-start(bf16[16,2,32,768]{3,2,1,0:T(8,128)(2,1)} %bitcast.252), channel_id=1, source_target_pairs={{0,16},{4,20},{8,24},{12,28},{16,0},{20,4},{24,8},{28,12},{1,17},{... | collective-permute-start | bytes 4718600 | tf_op jit(solution)/shard_map/ppermute | solution.py:39
  304.1 32.3 %collective-permute-start.38 = (bf16[2,104,768]{2,1,0:T(8,128)(2,1)}, bf16[2,104,768]{2,1,0:T(8,128)(2,1)}, u32[]{:S(2)}, u32[]{:S(2)}) collective-permute-start(bf16[2,104,768]{2,1,0:T(8,128)(2,1)} %get-tuple-element.319), channel_id=1, source_target_pairs={{0,1},{1,0},{2,3},{3,2},{4,5},{5,4},{6,7},{7,6},{8,9},{9,8},{10,11... | collective-permute-start | bytes 958472 | tf_op jit(solution)/shard_map/ppermute | solution.py:39
  347.7 48.7 %collective-permute-start.41 = (bf16[848,768]{1,0:T(8,128)(2,1)S(1)}, bf16[848,768]{1,0:T(8,128)(2,1)S(1)}, u32[]{:S(2)}, u32[]{:S(2)}) collective-permute-start(bf16[848,768]{1,0:T(8,128)(2,1)S(1)} %pad_maximum_fusion.4), channel_id=1, source_target_pairs={{0,16},{4,20},{8,24},{12,28},{16,0},{20,4},{24,8},{28,12},{1,17},{... | collective-permute-start | bytes 3907592 | tf_op jit(solution)/shard_map/ppermute | solution.py:39
  366.1 31.9 %collective-permute-start.47 = (bf16[840,768]{1,0:T(8,128)(2,1)}, bf16[840,768]{1,0:T(8,128)(2,1)}, u32[]{:S(2)}, u32[]{:S(2)}) collective-permute-start(bf16[840,768]{1,0:T(8,128)(2,1)} %pad_maximum_fusion.5), channel_id=1, source_target_pairs={{0,8},{4,12},{8,0},{12,4},{16,24},{20,28},{24,16},{28,20},{1,9},{5... | collective-permute-start | bytes 3870728 | tf_op jit(solution)/shard_map/ppermute | solution.py:39
  370.7 30.7 %collective-permute-start.48 = (bf16[8,32,768]{2,1,0:T(8,128)(2,1)}, bf16[8,32,768]{2,1,0:T(8,128)(2,1)}, u32[]{:S(2)}, u32[]{:S(2)}) collective-permute-start(bf16[8,32,768]{2,1,0:T(8,128)(2,1)} %get-tuple-element.266), channel_id=1, source_target_pairs={{0,1},{1,0},{2,3},{3,2},{4,5},{5,4},{6,7},{7,6},{8,9},{9,8},{10,11... | collective-permute-start | bytes 1179656 | tf_op jit(solution)/shard_map/ppermute | solution.py:39
  375.5 26.0 %collective-permute-start.49 = (bf16[8,32,768]{2,1,0:T(8,128)(2,1)}, bf16[8,32,768]{2,1,0:T(8,128)(2,1)}, u32[]{:S(2)}, u32[]{:S(2)}) collective-permute-start(bf16[8,32,768]{2,1,0:T(8,128)(2,1)} %get-tuple-element.267), channel_id=1, source_target_pairs={{0,2},{1,3},{2,0},{3,1},{4,6},{5,7},{6,4},{7,5},{8,10},{9,11},{10,... | collective-permute-start | bytes 1179656 | tf_op jit(solution)/shard_map/ppermute | solution.py:39
  375.6 25.9 %collective-permute-start.50 = (bf16[8,32,768]{2,1,0:T(8,128)(2,1)}, bf16[8,32,768]{2,1,0:T(8,128)(2,1)}, u32[]{:S(2)}, u32[]{:S(2)}) collective-permute-start(bf16[8,32,768]{2,1,0:T(8,128)(2,1)} %get-tuple-element.268), channel_id=1, source_target_pairs={{0,3},{1,2},{2,1},{3,0},{4,7},{5,6},{6,5},{7,4},{8,11},{9,10},{10,... | collective-permute-start | bytes 1179656 | tf_op jit(solution)/shard_map/ppermute | solution.py:39
  431.7 28.4 %collective-permute-start.64 = (bf16[1,192,768]{2,1,0:T(8,128)(2,1)S(1)}, bf16[1,192,768]{2,1,0:T(8,128)(2,1)S(1)}, u32[]{:S(2)}, u32[]{:S(2)}) collective-permute-start(bf16[1,192,768]{2,1,0:T(8,128)(2,1)S(1)} %get-tuple-element.321), channel_id=1, source_target_pairs={{0,1},{1,0},{2,3},{3,2},{4,5},{5,4},{6,7},{7,6},{8,9},{9,8},{10,11... | collective-permute-start | bytes 884744 | tf_op jit(solution)/shard_map/ppermute | solution.py:39
  431.8 28.3 %collective-permute-start.65 = (bf16[1,192,768]{2,1,0:T(8,128)(2,1)S(1)}, bf16[1,192,768]{2,1,0:T(8,128)(2,1)S(1)}, u32[]{:S(2)}, u32[]{:S(2)}) collective-permute-start(bf16[1,192,768]{2,1,0:T(8,128)(2,1)S(1)} %get-tuple-element.323), channel_id=1, source_target_pairs={{0,2},{1,3},{2,0},{3,1},{4,6},{5,7},{6,4},{7,5},{8,10},{9,11},{10,... | collective-permute-start | bytes 884744 | tf_op jit(solution)/shard_map/ppermute | solution.py:39
  432.8 27.4 %collective-permute-start.66 = (bf16[1,192,768]{2,1,0:T(8,128)(2,1)S(1)}, bf16[1,192,768]{2,1,0:T(8,128)(2,1)S(1)}, u32[]{:S(2)}, u32[]{:S(2)}) collective-permute-start(bf16[1,192,768]{2,1,0:T(8,128)(2,1)S(1)} %get-tuple-element.322), channel_id=1, source_target_pairs={{0,3},{1,2},{2,1},{3,0},{4,7},{5,6},{6,5},{7,4},{8,11},{9,10},{10,... | collective-permute-start | bytes 884744 | tf_op jit(solution)/shard_map/ppermute | solution.py:39
  (87 other events, 1229.5 us)

commit v3 on v2

--- a/solution.py
+++ b/solution.py
@@ -84,7 +84,7 @@
     return [matrix[:, spot : spot + width] for spot in range(0, matrix.shape[1], width)]
 
 
-def run_kernel(body, args, in_specs, after=(), **options):
+def run_kernel(body, args, in_specs, after=(), limit=60, **options):
     count = len(after)
 
     def whole(*refs):
@@ -93,7 +93,7 @@
     return pl.pallas_call(
         whole,
         in_specs=[pl.BlockSpec(memory_space=pl.ANY)] * count + in_specs,
-        compiler_params=pltpu.CompilerParams(vmem_limit_bytes=60 * 1024 * 1024),
+        compiler_params=pltpu.CompilerParams(vmem_limit_bytes=limit * 1024 * 1024),
         cost_estimate=pl.CostEstimate(flops=1000, bytes_accessed=1000, transcendentals=0),
         **options,
     )(*after, *args)
@@ -723,7 +723,7 @@
 
 def kernel_grad_body(dp_size, band_step, *refs):
     spot_ref, patch_ref = refs[:2]
-    *grad_refs, first_ref, last_ref, keep_ref, hold_ref = refs[2:]
+    *grad_refs, send_ref, keep_ref, hold_ref = refs[2:]
     rows = grad_refs[0].shape[0]
     total = 0.0
     for key, grad_ref in enumerate(grad_refs):
@@ -738,23 +738,14 @@
             base = band * pixels + chip * 2 * share
             kept = pl.multiple_of(base + core * share, share)
             keep_ref[band, chip] = hold_ref[pl.ds(kept, share), :]
-
-    half = pl.num_programs(0) // 2
-    for number, send_ref in enumerate((first_ref, last_ref)):
-
-        @pl.when(pl.program_id(0) // half == number)
-        def _(send_ref=send_ref):
-            for band in range(band_step):
-                for chip in range(dp_size // 2):
-                    base = band * pixels + chip * 2 * share
-                    sent = pl.multiple_of(base + (1 - core) * share, share)
-                    send_ref[band, chip] = hold_ref[pl.ds(sent, share), :]
+            sent = pl.multiple_of(base + (1 - core) * share, share)
+            send_ref[band, chip] = hold_ref[pl.ds(sent, share), :]
 
 
 def kernel_grad_part(spots, patch_rows, grads, first_band, group_bands, bands_dev, dp_size, after):
     row_total = patch_rows.shape[0]
     width = grads[0].shape[1]
-    band_step = min(4, group_bands // 2)
+    band_step = min(4, group_bands)
     pixels = patch_rows.shape[1] // bands_dev
     depth = band_step * pixels
     offset = first_band // band_step
@@ -766,10 +757,11 @@
         partial(kernel_grad_body, dp_size, band_step),
         (spots, patch_rows, *grads),
         after=after,
+        limit=63,
         grid=(steps,),
         out_shape=[
             jax.ShapeDtypeStruct((bands,) + chips, jnp.bfloat16)
-            for bands in (group_bands // 2, group_bands // 2, group_bands)
+            for bands in (group_bands, group_bands)
         ],
         in_specs=[
             pl.BlockSpec(memory_space=pltpu.SMEM),
@@ -777,8 +769,7 @@
         ]
         + [pl.BlockSpec(grad.shape, lambda step: (0, 0)) for grad in grads],
         out_specs=[
-            pl.BlockSpec(block, lambda step: (jnp.minimum(step, steps // 2 - 1), 0, 0, 0)),
-            pl.BlockSpec(block, lambda step: (jnp.maximum(step - steps // 2, 0), 0, 0, 0)),
+            pl.BlockSpec(block, lambda step: (step, 0, 0, 0)),
             pl.BlockSpec(block, lambda step: (step, 0, 0, 0)),
         ],
         scratch_shapes=[pltpu.VMEM((depth, width), jnp.bfloat16)],
@@ -813,6 +804,7 @@
         + [pl.BlockSpec(grad.shape, lambda step: (0, 0)) for grad in grads]
         + specs,
         after=after,
+        limit=63,
         grid=(steps,),
         out_shape=jax.ShapeDtypeStruct((row_total, steps * depth), jnp.bfloat16),
         out_specs=pl.BlockSpec((row_total, depth), lambda step: (0, step)),
@@ -902,6 +894,7 @@
         flats,
         [pl.BlockSpec((step_rows, flat.shape[1]), lambda step: (step, 0)) for flat in flats],
         after=after,
+        limit=63,
         grid=(rows // step_rows,),
         out_shape=jax.ShapeDtypeStruct((rows, bands, pixels), flats[0].dtype),
         out_specs=pl.BlockSpec((step_rows, bands, pixels), lambda step: (step, 0, 0)),
@@ -1078,6 +1071,7 @@
         partial(weight_grad_body, dp_size, parts, hidden),
         (spots, own, other),
         [pl.BlockSpec(memory_space=pltpu.SMEM), inside, inside],
+        limit=63,
         out_shape=[
             jax.ShapeDtypeStruct((chips // 2, part_rows, width), bf16)
             for part_rows in rows
@@ -1140,6 +1134,7 @@
             pl.BlockSpec(block_in, lambda first, rows: (first, 0, rows, 0)),
         ]
         + [part_spec(number) for number in range(len(gots))],
+        limit=63,
         grid=(outer // outer_step, inner_rows // rows_step),
         out_shape=[jax.ShapeDtypeStruct((outer, inner_rows, width), keep.dtype)] * 2,
         out_specs=[block_out] * 2,
@@ -1179,6 +1174,7 @@
         partial(owners_body, len(keeps)),
         (spots, *keeps, *gots),
         [pl.BlockSpec(memory_space=pltpu.SMEM)] + [inside] * (2 * len(keeps)),
+        limit=63,
         out_shape=[
             jax.ShapeDtypeStruct((pixels, bands * len(keeps), width), keeps[0].dtype)
         ]

time: 470 us -> 465 us (0.989)
    unnamed x96 -> x82, local copies, waits for them, and re-layouts: 11.2 us -> 5.54 us
    ppermute x67 -> x65, waiting for transfers between devices: 120 us -> 119 us  [swap(): lax.ppermute(values, axis, [(spot, spot ^ step) for spot in range(size)])]
    ppermute x67 -> x65, starting transfers between devices: 108 us -> 108 us  [swap(): lax.ppermute(values, axis, [(spot, spot ^ step) for spot in range(size)])]
  transfers between devices with their start and end apart: 67 -> 65, of which waited for: 22 -> 22; matrix products, arithmetic and copies ran while one was open for 7% -> 7% of each run, Pallas kernels for 29% -> 29%
where the time goes in v3:
time: 465 us; the launch traced here: 460 us
  Pallas kernels  187 us (40%)
  waiting for transfers between devices  119 us (26%)
  starting transfers between devices  108 us (23%)
  other arithmetic  22.5 us (5%)
  local copies, waits for them, and re-layouts  21.9 us (5%)
    pallas_call x18, Pallas kernels, run_kernel(): pl.pallas_call(whole, in_specs=[pl.BlockSpec(memory_space=pl.ANY)] * coun...  187 us
    ppermute x65, waiting for transfers between devices, swap(): lax.ppermute(values, axis, [(spot, spot ^ step) for spot in range(size)])  119 us
    ppermute x65, starting transfers between devices, swap(): lax.ppermute(values, axis, [(spot, spot ^ step) for spot in range(size)])  108 us
  transfers between devices with their start and end apart: 65, of which 22 were waited for; matrix products, arithmetic and copies ran while one was open for 7% of the time, Pallas kernels for 29%

profile of v3, /device:TPU:1, one launch (start us, length us, event | category | flops | bytes accessed | tf_op | source)
XLA Modules:
  0.0 460.0 jit_solution(11422941318235816141)
XLA Ops:
  0.7 7.2 %shard_map.323 = (bf16[8,128,768]{2,1,0:T(8,128)(2,1)}, f32[8,768]{1,0:T(8,128)}, bf16[128,128]{1,0:T(8,128)(2,1)}, f32[136,128]{1,0:T(8,128)}, f32[7,136,128]{2...) custom-call(s32[1,128]{1,0:T(1,128)} %bitcast.242, bf16[1,128]{1,0:T(2,128)(2,1)} %bitcast.243, ...), custom_call_target="tpu_custom_call" | custom-call | flops 1000 | bytes 1000 | tf_op jit(solution)/shard_map/pallas_call | solution.py:93
  14.6 18.8 %shard_map.324.refs_1_ = bf16[1024,8192]{1,0:T(8,128)(2,1)} custom-call(bf16[8,128,768]{2,1,0:T(8,128)(2,1)} %get-tuple-element.162.refs_0_, bf16[1024,32,256]{2,1,0:T(8,128)(2,1)} %bitcast.205), custom_call_target="tpu_custom_call" | custom-call | flops 1000 | bytes 1000 | tf_op jit(solution)/shard_map/pallas_call | solution.py:93
  45.7 8.3 %collective-permute-start.6 = (bf16[288,768]{1,0:T(8,128)(2,1)S(1)}, bf16[288,768]{1,0:T(8,128)(2,1)S(1)}, u32[]{:S(2)}, u32[]{:S(2)}) collective-permute-start(bf16[288,768]{1,0:T(8,128)(2,1)S(1)} %copy-done.11), channel_id=1, source_target_pairs={{0,2},{1,3},{2,0},{3,1},{4,6},{5,7},{6,4},{7,5},{8,10},{9,11},{10,... | collective-permute-start | bytes 1327112 | tf_op jit(solution)/shard_map/ppermute | solution.py:39
  53.9 19.0 %collective-permute-done.6.refs_3_ = bf16[288,768]{1,0:T(8,128)(2,1)S(1)} collective-permute-done((bf16[288,768]{1,0:T(8,128)(2,1)S(1)}, bf16[288,768]{1,0:T(8,128)(2,1)S(1)}, u32[]{:S(2)}, u32[]{:S(2)}) %collective-permute-start.6) | collective-permute-done | bytes 442400 | tf_op jit(solution)/shard_map/ppermute | solution.py:39
  78.6 11.0 %collective-permute-done.10.refs_2_ = bf16[288,768]{1,0:T(8,128)(2,1)S(1)} collective-permute-done((bf16[288,768]{1,0:T(8,128)(2,1)S(1)}, bf16[288,768]{1,0:T(8,128)(2,1)S(1)}, u32[]{:S(2)}, u32[]{:S(2)}) %collective-permute-start.10) | collective-permute-done | bytes 442400 | tf_op jit(solution)/shard_map/ppermute | solution.py:39
  89.6 9.0 %collective-permute-done.11.refs_4_ = bf16[288,768]{1,0:T(8,128)(2,1)S(1)} collective-permute-done((bf16[288,768]{1,0:T(8,128)(2,1)S(1)}, bf16[288,768]{1,0:T(8,128)(2,1)S(1)}, u32[]{:S(2)}, u32[]{:S(2)}) %collective-permute-start.11) | collective-permute-done | bytes 442400 | tf_op jit(solution)/shard_map/ppermute | solution.py:39
  98.7 10.3 %collective-permute-done.8.refs_11_.refs_14_ = bf16[2,16,32,768]{3,2,1,0:T(8,128)(2,1)S(1)} collective-permute-done((bf16[2,16,32,768]{3,2,1,0:T(8,128)(2,1)S(1)}, bf16[2,16,32,768]{3,2,1,0:T(8,128)(2,1)S(1)}, u32[]{:S(2)}, u32[]{:S(2)}) %collective-permute-start.8) | collective-permute-done | bytes 1572896 | tf_op jit(solution)/shard_map/ppermute | solution.py:39
  120.9 20.3 %shard_map.327 = (bf16[256,768]{1,0:T(8,128)(2,1)}, bf16[256,768]{1,0:T(8,128)(2,1)}, bf16[256,768]{1,0:T(8,128)(2,1)}, bf16[256,768]{1,0:T(8,128)(2,1)}) custom-call(s32[2]{0:T(128)} %pad_add_fusion.refs_0_.refs_12_.refs_7_, bf16[1024,8192]{1,0:T(8,128)(2,1)} %shard_map.324.refs_1_, bf16[1,32,32,768]{3,2,1,0:T(8,128)(2,1)} %bitcast.201, ...), custom_call_target="tpu_custom_call" | custom-call | flops 1000 | bytes 1000 | tf_op jit(solution)/shard_map/pallas_call | solution.py:93
  150.9 13.4 %collective-permute-done.19.refs_1_ = bf16[256,768]{1,0:T(8,128)(2,1)S(1)} collective-permute-done((bf16[256,768]{1,0:T(8,128)(2,1)}, bf16[256,768]{1,0:T(8,128)(2,1)S(1)}, u32[]{:S(2)}, u32[]{:S(2)}) %collective-permute-start.19) | collective-permute-done | bytes 393248 | tf_op jit(solution)/shard_map/ppermute | solution.py:39
  164.3 10.9 %collective-permute-done.20.refs_2_ = bf16[256,768]{1,0:T(8,128)(2,1)S(1)} collective-permute-done((bf16[256,768]{1,0:T(8,128)(2,1)}, bf16[256,768]{1,0:T(8,128)(2,1)S(1)}, u32[]{:S(2)}, u32[]{:S(2)}) %collective-permute-start.20) | collective-permute-done | bytes 393248 | tf_op jit(solution)/shard_map/ppermute | solution.py:39
  175.2 7.5 %collective-permute-done.18.refs_9_ = bf16[2,576,768]{2,1,0:T(8,128)(2,1)} collective-permute-done((bf16[2,576,768]{2,1,0:T(8,128)(2,1)S(1)}, bf16[2,576,768]{2,1,0:T(8,128)(2,1)}, u32[]{:S(2)}, u32[]{:S(2)}) %collective-permute-start.18) | collective-permute-done | bytes 1769504 | tf_op jit(solution)/shard_map/ppermute | solution.py:39
  198.6 28.1 %shard_map.328 = (bf16[256,768]{1,0:T(8,128)(2,1)}, bf16[256,768]{1,0:T(8,128)(2,1)}, bf16[256,13056]{1,0:T(8,128)(2,1)}, f32[8,768]{1,0:T(8,128)}) custom-call(bf16[256,768]{1,0:T(8,128)(2,1)} %get-tuple-element.190.refs_0_, bf16[256,768]{1,0:T(8,128)(2,1)} %copy-done.23, bf16[256,768]{1,0:T(8,128)(2,1)} %copy-done.24, bf16[256,768]{1,0:T(8,128)(2,1)} %copy-done.25, ...), custom_call_target="tpu_custom_call" | custom-call | flops 1000 | bytes 1000 | tf_op jit(solution)/shard_map/pallas_call | solution.py:93
  230.6 7.1 %collective-permute-done.29.refs_2_ = bf16[256,13056]{1,0:T(8,128)(2,1)} collective-permute-done((bf16[256,13056]{1,0:T(8,128)(2,1)}, bf16[256,13056]{1,0:T(8,128)(2,1)}, u32[]{:S(2)}, u32[]{:S(2)}) %collective-permute-start.29) | collective-permute-done | bytes 6684704 | tf_op jit(solution)/shard_map/ppermute | solution.py:39
  237.8 11.1 %shard_map.329 = (bf16[2,128,768]{2,1,0:T(8,128)(2,1)}, bf16[2,128,768]{2,1,0:T(8,128)(2,1)}, bf16[2,96,768]{2,1,0:T(8,128)(2,1)}, bf16[2,96,768]{2,1,0:T(8,128)...) custom-call(s32[2]{0:T(128)} %pad_add_fusion.refs_0_.refs_12_.refs_7, ...), custom_call_target="tpu_custom_call" | custom-call | flops 1000 | bytes 1000 | tf_op jit(solution)/shard_map/pallas_call | solution.py:93
  248.9 6.8 %collective-permute-done.27.refs_4_.refs_3_ = bf16[256,768]{1,0:T(8,128)(2,1)} collective-permute-done((bf16[256,768]{1,0:T(8,128)(2,1)}, bf16[256,768]{1,0:T(8,128)(2,1)}, u32[]{:S(2)}, u32[]{:S(2)}) %collective-permute-start.27) | collective-permute-done | bytes 393248 | tf_op jit(solution)/shard_map/ppermute | solution.py:39
  255.8 12.8 %shard_map.332 = (bf16[16,4,32,768]{3,2,1,0:T(8,128)(2,1)}, bf16[16,4,32,768]{3,2,1,0:T(8,128)(2,1)}) custom-call(s32[2]{0:T(128)} %pad_add_fusion.refs_0_.refs_12_.refs_7_, bf16[1024,8192]{1,0:T(8,128)(2,1)} %shard_map.324.refs_1_, bf16[256,768]{1,0:T(8,128)(2,1)} %get-tuple-element.216.refs_2_.refs_1_, bf16[256,768]{1,0:T(8,128)(2,1)} %copy-done.8, ...), custom_call_target="tpu_custom_call" | custom-call | flops 1000 | bytes 1000 | tf_op jit(solution)/shard_map/pallas_call | solution.py:93
  270.0 12.7 %shard_map.330 = (bf16[16,4,32,768]{3,2,1,0:T(8,128)(2,1)}, bf16[16,4,32,768]{3,2,1,0:T(8,128)(2,1)}) custom-call(s32[2]{0:T(128)} %pad_add_fusion.refs_0_.refs_12_.refs_7_, bf16[1024,8192]{1,0:T(8,128)(2,1)} %shard_map.324.refs_1_, bf16[256,768]{1,0:T(8,128)(2,1)} %get-tuple-element.216.refs_2_.refs_1_, bf16[256,768]{1,0:T(8,128)(2,1)} %copy-done.8, ...), custom_call_target="tpu_custom_call" | custom-call | flops 1000 | bytes 1000 | tf_op jit(solution)/shard_map/pallas_call | solution.py:93
  299.9 8.1 %collective-permute-start.36 = (bf16[2,104,768]{2,1,0:T(8,128)(2,1)}, bf16[2,104,768]{2,1,0:T(8,128)(2,1)S(1)}, u32[]{:S(2)}, u32[]{:S(2)}) collective-permute-start(bf16[2,104,768]{2,1,0:T(8,128)(2,1)} %get-tuple-element.315), channel_id=1, source_target_pairs={{0,1},{1,0},{2,3},{3,2},{4,5},{5,4},{6,7},{7,6},{8,9},{9,8},{10,11... | collective-permute-start | bytes 958472 | tf_op jit(solution)/shard_map/ppermute | solution.py:39
  310.1 20.4 %shard_map.334.refs_1_ = bf16[1024,8192]{1,0:T(8,128)(2,1)} custom-call(s32[2]{0:T(128)} %pad_add_fusion.refs_0_.refs_12_.refs_7_, bf16[256,768]{1,0:T(8,128)(2,1)} %get-tuple-element.216.refs_2_.refs_1_, bf16[256,768]{1,0:T(8,128)(2,1)} %copy-done.8, bf16[256,768]{1,0:T(8,128)(2,1)} %collective-permute-done.27.refs_4_.refs_3_, ...), custom_call_target="tpu_custom_call" | custom-call | flops 1000 | bytes 1000 | tf_op jit(solution)/shard_map/pallas_call | solution.py:93
  371.3 18.8 %shard_map.338 = bf16[1024,32,256]{2,1,0:T(8,128)(2,1)} custom-call(bf16[8,32,768]{2,1,0:T(8,128)(2,1)} %get-tuple-element.273.refs_0_.refs_2_, bf16[1024,8192]{1,0:T(8,128)(2,1)} %shard_map.334.refs_1_), custom_call_target="tpu_custom_call" | custom-call | flops 1000 | bytes 1000 | tf_op jit(solution)/shard_map/pallas_call | solution.py:93
  401.7 5.9 %collective-permute-start.49 = (f32[136,128]{1,0:T(8,128)}, f32[136,128]{1,0:T(8,128)S(1)}, u32[]{:S(2)}, u32[]{:S(2)}) collective-permute-start(f32[136,128]{1,0:T(8,128)} %get-tuple-element.279), channel_id=1, source_target_pairs={{0,1},{1,0},{2,3},{3,2},{4,5},{5,4},{6,7},{7,6},{8,9},{9,8},{10,11... | collective-permute-start | bytes 208904 | tf_op jit(solution)/shard_map/ppermute | solution.py:39
  416.6 6.6 %collective-permute-start.52 = (f32[136,128]{1,0:T(8,128)S(1)}, f32[136,128]{1,0:T(8,128)S(1)}, u32[]{:S(2)}, u32[]{:S(2)}) collective-permute-start(f32[136,128]{1,0:T(8,128)S(1)} %add_add_fusion), channel_id=1, source_target_pairs={{0,4},{4,0},{8,12},{12,8},{16,20},{20,16},{24,28},{28,24},{1,5},{5... | collective-permute-start | bytes 208904 | tf_op jit(solution)/shard_map/ppermute | solution.py:39
  438.2 8.1 %shard_map.340 = (f32[1,128]{1,0:T(1,128)}, f32[4,128,128]{2,1,0:T(8,128)}, f32[2,128]{1,0:T(2,128)}, f32[128,2048]{1,0:T(8,128)}, f32[2048,128]{1,0:T(8,128)}, /*index=5*/f32[128,768]{1,0:T(8,128)}) custom-call(f32[136,128]{1,0:T(8,128)} %add.282.refs_0_, bf16[4,128,128]{2,1,0:T(8,128)(2,1)} %refs_1_.5, bf16[2,128]{1,0:T(2,128)(2,1)} %refs_2_.5, ...), custom_call_target="tpu_custom_call" | custom-call | flops 1000 | bytes 1000 | tf_op jit(solution)/shard_map/pallas_call | solution.py:93
  446.3 8.9 %collective-permute-start.61 = (bf16[16,8,768]{2,1,0:T(8,128)(2,1)S(1)}, bf16[16,8,768]{2,1,0:T(8,128)(2,1)S(1)}, u32[]{:S(2)}, u32[]{:S(2)}) collective-permute-start(bf16[16,8,768]{2,1,0:T(8,128)(2,1)S(1)} %pad_maximum_fusion.10), channel_id=1, source_target_pairs={{0,4},{4,0},{8,12},{12,8},{16,20},{20,16},{24,28},{28,24},{1,5},{5... | collective-permute-start | bytes 589832 | tf_op jit(solution)/shard_map/ppermute | solution.py:39
  (318 shorter events, 167.0 us)
Async XLA Ops:
  9.6 26.2 %collective-permute-start = (bf16[32,8,768]{2,1,0:T(8,128)(2,1)S(1)}, bf16[32,8,768]{2,1,0:T(8,128)(2,1)S(1)}, u32[]{:S(2)}, u32[]{:S(2)}) collective-permute-start(bf16[32,8,768]{2,1,0:T(8,128)(2,1)S(1)} %bitcast.227), channel_id=1, source_target_pairs={{0,1},{1,0},{2,3},{3,2},{4,5},{5,4},{6,7},{7,6},{8,9},{9,8},{10,11... | collective-permute-start | bytes 1179656 | tf_op jit(solution)/shard_map/ppermute | solution.py:39
  39.5 34.2 %collective-permute-start.5 = (bf16[32,32,768]{2,1,0:T(8,128)(2,1)S(1)}, bf16[32,32,768]{2,1,0:T(8,128)(2,1)}, u32[]{:S(2)}, u32[]{:S(2)}) collective-permute-start(bf16[32,32,768]{2,1,0:T(8,128)(2,1)S(1)} %bitcast.200), channel_id=1, source_target_pairs={{0,4},{4,0},{8,12},{12,8},{16,20},{20,16},{24,28},{28,24},{1,5},{5... | collective-permute-start | bytes 4718600 | tf_op jit(solution)/shard_map/ppermute | solution.py:39
  43.1 29.8 %collective-permute-start.3 = (bf16[1,16,32,768]{3,2,1,0:T(8,128)(2,1)S(1)}, bf16[1,16,32,768]{3,2,1,0:T(8,128)(2,1)S(1)}, u32[]{:S(2)}, u32[]{:S(2)}) collective-permute-start(bf16[1,16,32,768]{3,2,1,0:T(8,128)(2,1)S(1)} %get-tuple-element.308), channel_id=1, source_target_pairs={{0,8},{4,12},{8,0},{12,4},{16,24},{20,28},{24,16},{28,20},{1,9},{5... | collective-permute-start | bytes 2359304 | tf_op jit(solution)/shard_map/ppermute | solution.py:39
  44.4 28.5 %collective-permute-start.4 = (bf16[1,16,32,768]{3,2,1,0:T(8,128)(2,1)S(1)}, bf16[1,16,32,768]{3,2,1,0:T(8,128)(2,1)S(1)}, u32[]{:S(2)}, u32[]{:S(2)}) collective-permute-start(bf16[1,16,32,768]{3,2,1,0:T(8,128)(2,1)S(1)} %get-tuple-element.307), channel_id=1, source_target_pairs={{0,16},{4,20},{8,24},{12,28},{16,0},{20,4},{24,8},{28,12},{1,17},{... | collective-permute-start | bytes 2359304 | tf_op jit(solution)/shard_map/ppermute | solution.py:39
  45.7 27.2 %collective-permute-start.6 = (bf16[288,768]{1,0:T(8,128)(2,1)S(1)}, bf16[288,768]{1,0:T(8,128)(2,1)S(1)}, u32[]{:S(2)}, u32[]{:S(2)}) collective-permute-start(bf16[288,768]{1,0:T(8,128)(2,1)S(1)} %copy-done.11), channel_id=1, source_target_pairs={{0,2},{1,3},{2,0},{3,1},{4,6},{5,7},{6,4},{7,5},{8,10},{9,11},{10,... | collective-permute-start | bytes 1327112 | tf_op jit(solution)/shard_map/ppermute | solution.py:39
  74.6 34.4 %collective-permute-start.8 = (bf16[2,16,32,768]{3,2,1,0:T(8,128)(2,1)S(1)}, bf16[2,16,32,768]{3,2,1,0:T(8,128)(2,1)S(1)}, u32[]{:S(2)}, u32[]{:S(2)}) collective-permute-start(bf16[2,16,32,768]{3,2,1,0:T(8,128)(2,1)S(1)} %pad_maximum_fusion.3), channel_id=1, source_target_pairs={{0,8},{4,12},{8,0},{12,4},{16,24},{20,28},{24,16},{28,20},{1,9},{5... | collective-permute-start | bytes 4718600 | tf_op jit(solution)/shard_map/ppermute | solution.py:39
  75.0 34.1 %collective-permute-start.7 = (bf16[2,16,32,768]{3,2,1,0:T(8,128)(2,1)S(1)}, bf16[2,16,32,768]{3,2,1,0:T(8,128)(2,1)}, u32[]{:S(2)}, u32[]{:S(2)}) collective-permute-start(bf16[2,16,32,768]{3,2,1,0:T(8,128)(2,1)S(1)} %pad_maximum_fusion.2), channel_id=1, source_target_pairs={{0,16},{4,20},{8,24},{12,28},{16,0},{20,4},{24,8},{28,12},{1,17},{... | collective-permute-start | bytes 4718600 | tf_op jit(solution)/shard_map/ppermute | solution.py:39
  142.7 40.0 %collective-permute-start.18 = (bf16[2,576,768]{2,1,0:T(8,128)(2,1)S(1)}, bf16[2,576,768]{2,1,0:T(8,128)(2,1)}, u32[]{:S(2)}, u32[]{:S(2)}) collective-permute-start(bf16[2,576,768]{2,1,0:T(8,128)(2,1)S(1)} %pad_maximum_fusion.1.refs_8_), channel_id=1, source_target_pairs={{0,8},{4,12},{8,0},{12,4},{16,24},{20,28},{24,16},{28,20},{1,9},{5... | collective-permute-start | bytes 5308424 | tf_op jit(solution)/shard_map/ppermute | solution.py:39
  146.0 40.2 %collective-permute-start.17 = (bf16[2,576,768]{2,1,0:T(8,128)(2,1)}, bf16[2,576,768]{2,1,0:T(8,128)(2,1)}, u32[]{:S(2)}, u32[]{:S(2)}) collective-permute-start(bf16[2,576,768]{2,1,0:T(8,128)(2,1)} %pad_maximum_fusion.refs_4_), channel_id=1, source_target_pairs={{0,16},{4,20},{8,24},{12,28},{16,0},{20,4},{24,8},{28,12},{1,17},{... | collective-permute-start | bytes 5308424 | tf_op jit(solution)/shard_map/ppermute | solution.py:39
  147.2 28.0 %collective-permute-start.20 = (bf16[256,768]{1,0:T(8,128)(2,1)}, bf16[256,768]{1,0:T(8,128)(2,1)S(1)}, u32[]{:S(2)}, u32[]{:S(2)}) collective-permute-start(bf16[256,768]{1,0:T(8,128)(2,1)} %get-tuple-element.188), channel_id=1, source_target_pairs={{0,2},{1,3},{2,0},{3,1},{4,6},{5,7},{6,4},{7,5},{8,10},{9,11},{10,... | collective-permute-start | bytes 1179656 | tf_op jit(solution)/shard_map/ppermute | solution.py:39
  148.1 27.2 %collective-permute-start.21 = (bf16[256,768]{1,0:T(8,128)(2,1)}, bf16[256,768]{1,0:T(8,128)(2,1)S(1)}, u32[]{:S(2)}, u32[]{:S(2)}) collective-permute-start(bf16[256,768]{1,0:T(8,128)(2,1)} %get-tuple-element.189), channel_id=1, source_target_pairs={{0,3},{1,2},{2,1},{3,0},{4,7},{5,6},{6,5},{7,4},{8,11},{9,10},{10,... | collective-permute-start | bytes 1179656 | tf_op jit(solution)/shard_map/ppermute | solution.py:39
  227.1 28.7 %collective-permute-start.27 = (bf16[256,768]{1,0:T(8,128)(2,1)}, bf16[256,768]{1,0:T(8,128)(2,1)}, u32[]{:S(2)}, u32[]{:S(2)}) collective-permute-start(bf16[256,768]{1,0:T(8,128)(2,1)} %get-tuple-element.216.refs_2_.refs_1_), channel_id=1, source_target_pairs={{0,2},{1,3},{2,0},{3,1},{4,6},{5,7},{6,4},{7,5},{8,10},{9,11},{10,... | collective-permute-start | bytes 1179656 | tf_op jit(solution)/shard_map/ppermute | solution.py:39
  227.9 27.8 %collective-permute-start.28 = (bf16[256,768]{1,0:T(8,128)(2,1)}, bf16[256,768]{1,0:T(8,128)(2,1)}, u32[]{:S(2)}, u32[]{:S(2)}) collective-permute-start(bf16[256,768]{1,0:T(8,128)(2,1)} %get-tuple-element.216.refs_2_.refs_1_), channel_id=1, source_target_pairs={{0,3},{1,2},{2,1},{3,0},{4,7},{5,6},{6,5},{7,4},{8,11},{9,10},{10,... | collective-permute-start | bytes 1179656 | tf_op jit(solution)/shard_map/ppermute | solution.py:39
  294.1 38.9 %collective-permute-start.34 = (bf16[16,2,32,768]{3,2,1,0:T(8,128)(2,1)}, bf16[16,2,32,768]{3,2,1,0:T(8,128)(2,1)}, u32[]{:S(2)}, u32[]{:S(2)}) collective-permute-start(bf16[16,2,32,768]{3,2,1,0:T(8,128)(2,1)} %bitcast.245), channel_id=1, source_target_pairs={{0,8},{4,12},{8,0},{12,4},{16,24},{20,28},{24,16},{28,20},{1,9},{5... | collective-permute-start | bytes 4718600 | tf_op jit(solution)/shard_map/ppermute | solution.py:39
  294.7 38.3 %collective-permute-start.35 = (bf16[16,2,32,768]{3,2,1,0:T(8,128)(2,1)}, bf16[16,2,32,768]{3,2,1,0:T(8,128)(2,1)}, u32[]{:S(2)}, u32[]{:S(2)}) collective-permute-start(bf16[16,2,32,768]{3,2,1,0:T(8,128)(2,1)} %bitcast.244), channel_id=1, source_target_pairs={{0,16},{4,20},{8,24},{12,28},{16,0},{20,4},{24,8},{28,12},{1,17},{... | collective-permute-start | bytes 4718600 | tf_op jit(solution)/shard_map/ppermute | solution.py:39
  299.9 32.5 %collective-permute-start.36 = (bf16[2,104,768]{2,1,0:T(8,128)(2,1)}, bf16[2,104,768]{2,1,0:T(8,128)(2,1)S(1)}, u32[]{:S(2)}, u32[]{:S(2)}) collective-permute-start(bf16[2,104,768]{2,1,0:T(8,128)(2,1)} %get-tuple-element.315), channel_id=1, source_target_pairs={{0,1},{1,0},{2,3},{3,2},{4,5},{5,4},{6,7},{7,6},{8,9},{9,8},{10,11... | collective-permute-start | bytes 958472 | tf_op jit(solution)/shard_map/ppermute | solution.py:39
  343.7 46.4 %collective-permute-start.39 = (bf16[848,768]{1,0:T(8,128)(2,1)}, bf16[848,768]{1,0:T(8,128)(2,1)}, u32[]{:S(2)}, u32[]{:S(2)}) collective-permute-start(bf16[848,768]{1,0:T(8,128)(2,1)} %pad_maximum_fusion.4), channel_id=1, source_target_pairs={{0,16},{4,20},{8,24},{12,28},{16,0},{20,4},{24,8},{28,12},{1,17},{... | collective-permute-start | bytes 3907592 | tf_op jit(solution)/shard_map/ppermute | solution.py:39
  358.9 34.7 %collective-permute-start.45 = (bf16[840,768]{1,0:T(8,128)(2,1)}, bf16[840,768]{1,0:T(8,128)(2,1)}, u32[]{:S(2)}, u32[]{:S(2)}) collective-permute-start(bf16[840,768]{1,0:T(8,128)(2,1)} %pad_maximum_fusion.5), channel_id=1, source_target_pairs={{0,8},{4,12},{8,0},{12,4},{16,24},{20,28},{24,16},{28,20},{1,9},{5... | collective-permute-start | bytes 3870728 | tf_op jit(solution)/shard_map/ppermute | solution.py:39
  364.0 33.1 %collective-permute-start.46 = (bf16[8,32,768]{2,1,0:T(8,128)(2,1)}, bf16[8,32,768]{2,1,0:T(8,128)(2,1)}, u32[]{:S(2)}, u32[]{:S(2)}) collective-permute-start(bf16[8,32,768]{2,1,0:T(8,128)(2,1)} %get-tuple-element.262), channel_id=1, source_target_pairs={{0,1},{1,0},{2,3},{3,2},{4,5},{5,4},{6,7},{7,6},{8,9},{9,8},{10,11... | collective-permute-start | bytes 1179656 | tf_op jit(solution)/shard_map/ppermute | solution.py:39
  369.0 28.1 %collective-permute-start.47 = (bf16[8,32,768]{2,1,0:T(8,128)(2,1)}, bf16[8,32,768]{2,1,0:T(8,128)(2,1)}, u32[]{:S(2)}, u32[]{:S(2)}) collective-permute-start(bf16[8,32,768]{2,1,0:T(8,128)(2,1)} %get-tuple-element.263), channel_id=1, source_target_pairs={{0,2},{1,3},{2,0},{3,1},{4,6},{5,7},{6,4},{7,5},{8,10},{9,11},{10,... | collective-permute-start | bytes 1179656 | tf_op jit(solution)/shard_map/ppermute | solution.py:39
  370.1 27.0 %collective-permute-start.48 = (bf16[8,32,768]{2,1,0:T(8,128)(2,1)}, bf16[8,32,768]{2,1,0:T(8,128)(2,1)}, u32[]{:S(2)}, u32[]{:S(2)}) collective-permute-start(bf16[8,32,768]{2,1,0:T(8,128)(2,1)} %get-tuple-element.264), channel_id=1, source_target_pairs={{0,3},{1,2},{2,1},{3,0},{4,7},{5,6},{6,5},{7,4},{8,11},{9,10},{10,... | collective-permute-start | bytes 1179656 | tf_op jit(solution)/shard_map/ppermute | solution.py:39
  427.6 27.6 %collective-permute-start.62 = (bf16[1,192,768]{2,1,0:T(8,128)(2,1)S(1)}, bf16[1,192,768]{2,1,0:T(8,128)(2,1)S(1)}, u32[]{:S(2)}, u32[]{:S(2)}) collective-permute-start(bf16[1,192,768]{2,1,0:T(8,128)(2,1)S(1)} %get-tuple-element.317), channel_id=1, source_target_pairs={{0,1},{1,0},{2,3},{3,2},{4,5},{5,4},{6,7},{7,6},{8,9},{9,8},{10,11... | collective-permute-start | bytes 884744 | tf_op jit(solution)/shard_map/ppermute | solution.py:39
  427.7 27.5 %collective-permute-start.63 = (bf16[1,192,768]{2,1,0:T(8,128)(2,1)S(1)}, bf16[1,192,768]{2,1,0:T(8,128)(2,1)S(1)}, u32[]{:S(2)}, u32[]{:S(2)}) collective-permute-start(bf16[1,192,768]{2,1,0:T(8,128)(2,1)S(1)} %get-tuple-element.319), channel_id=1, source_target_pairs={{0,2},{1,3},{2,0},{3,1},{4,6},{5,7},{6,4},{7,5},{8,10},{9,11},{10,... | collective-permute-start | bytes 884744 | tf_op jit(solution)/shard_map/ppermute | solution.py:39
  428.8 26.4 %collective-permute-start.64 = (bf16[1,192,768]{2,1,0:T(8,128)(2,1)S(1)}, bf16[1,192,768]{2,1,0:T(8,128)(2,1)S(1)}, u32[]{:S(2)}, u32[]{:S(2)}) collective-permute-start(bf16[1,192,768]{2,1,0:T(8,128)(2,1)S(1)} %get-tuple-element.318), channel_id=1, source_target_pairs={{0,3},{1,2},{2,1},{3,0},{4,7},{5,6},{6,5},{7,4},{8,11},{9,10},{10,... | collective-permute-start | bytes 884744 | tf_op jit(solution)/shard_map/ppermute | solution.py:39
  (78 other events, 1193.5 us)

commit v4 on v3

--- a/solution.py
+++ b/solution.py
@@ -158,7 +158,7 @@
         kept_ref,
         result_ref,
         embed_grad_ref,
-        stash_ref,
+        stash_hbm,
         sums_ref,
         qkv_w,
         out_w,
@@ -170,7 +170,9 @@
         back_ref,
         mixed_grad_ref,
         bias_grad_ref,
+        stash_ref,
         sems,
+        stash_sems,
     ) = refs[part_count + weight_count :]
     bf16 = jnp.bfloat16
     f32 = jnp.float32
@@ -186,6 +188,18 @@
     branch_ref = views["branch"]
     pre_grad_ref = views["pre_grad"]
     views["cot"][...] = cot_ref[...]
+    leaving = []
+
+    def leave(*names):
+        for name in names:
+            cols = pl.ds(*spans[name])
+            copy = pltpu.make_async_copy(
+                stash_ref.at[:, cols], stash_hbm.at[:, cols], stash_sems.at[len(leaving)]
+            )
+            copy.start()
+            leaving.append(copy)
+
+    leave("cot")
     share = width // sum(len(keys) for keys in keys_lists[0])
     targets = (
         [(qkv_w, column, share) for column in range(3)]
@@ -256,7 +270,8 @@
             mixed_ref[rows, cols[0]] = mixed.astype(bf16)
         return carry
 
-    lax.fori_loop(0, head_pairs, attend, 0)
+    lax.fori_loop(0, head_pairs, attend, 0, unroll=3)
+    leave("normed", "mixed")
     arrive(out_w)
     middle = start + dot_nn(mixed_ref[...], out_w[...])
     unit_two, scale_two = norm_stats(middle)
@@ -283,6 +298,7 @@
         return carry
 
     lax.fori_loop(0, fc_in_w.shape[1] // ff_step, feed, 0)
+    leave("normed_two", "act", "pre_grad")
     result_ref[...] = (total_ref[...] * keep_ref[...]).astype(bf16)
     grad_norm, gain_two, shift_two = norm_back(unit_two, scale_two, gain_ref[1:2], back_ref[...])
     grad_middle = cot_ref[...].astype(f32) + grad_norm
@@ -311,7 +327,8 @@
                 qkv_grad_ref[rows, cols[which]] = (grads[which] * factor).astype(bf16)
         return carry
 
-    lax.fori_loop(0, head_pairs, attend_back, 0)
+    lax.fori_loop(0, head_pairs, attend_back, 0, unroll=3)
+    leave("branch", "qkv_grad")
     back = jnp.zeros((row_total, width), f32)
     for spot in range(3):
         cols = slice(spot * width, (spot + 1) * width)
@@ -333,6 +350,9 @@
     cuts = [bias_grad_ref[:, spot : spot + width] for spot in range(0, hidden, width)]
     cuts.append(jnp.zeros((8 - len(cuts), width), f32))
     small_ref[...] = jnp.concatenate([by_position, sums, *cuts], axis=0).astype(bf16)
+    leave("small")
+    for copy in leaving:
+        copy.wait()
 
 
 def block(parts, weight_halves, spots, base, cot, keep, mask, gains, shifts, bias, kept):
@@ -354,14 +374,14 @@
         ((8, width), f32),
     ]
     return run_kernel(
-        partial(block_body, len(parts), tile_rows, 512, keys_lists),
+        partial(block_body, len(parts), tile_rows, width, keys_lists),
         (*parts, *weight_args, spots, base, cot, keep, mask, gains, shifts, bias, kept),
         [inside] * len(parts)
         + [outside] * len(weight_args)
         + [pl.BlockSpec(memory_space=pltpu.SMEM)]
         + [inside] * 8,
         out_shape=[jax.ShapeDtypeStruct(shape, kind) for shape, kind in shapes],
-        out_specs=[inside] * len(shapes),
+        out_specs=[inside, inside, outside, inside],
         scratch_shapes=[
             pltpu.VMEM((width, 3 * width), bf16),
             pltpu.VMEM((width, width), bf16),
@@ -373,7 +393,9 @@
             pltpu.VMEM(rows, f32),
             pltpu.VMEM(rows, bf16),
             pltpu.VMEM((1, hidden), f32),
+            pltpu.VMEM((row_total, sum(stash_spans(width, hidden)["small"])), bf16),
             pltpu.SemaphoreType.DMA(((5 + hidden // width) * pieces,)),
+            pltpu.SemaphoreType.DMA((len(stash_spans(width, hidden)),)),
         ],
     )
 
@@ -404,22 +426,10 @@
     ff_out_hbm,
     bias_w_hbm,
     columns_hbm,
-    kernel_ref,
-    embed_bias_ref,
-    low_ref,
-    states_ref,
-    rows_ref,
-    weights_ref,
-    pre_ref,
-    scales_ref,
-    attn_ref,
-    gain_ref,
-    ff_in_ref,
-    ff_out_ref,
-    bias_w_ref,
-    columns_ref,
-    sems,
+    *refs,
 ):
+    *kernel_refs, embed_bias_ref, low_ref, states_ref, rows_ref, weights_ref, pre_ref, scales_ref = refs[:-8]
+    attn_ref, gain_ref, ff_in_ref, ff_out_ref, bias_w_ref, columns_ref, hold_ref, sems = refs[-8:]
     f32 = jnp.float32
     copies = [
         pltpu.make_async_copy(source, target, sems.at[number])
@@ -488,17 +498,24 @@
     scales_ref[1] = jnp.broadcast_to(scale_two, (padded, width))
     low = states[:bands].astype(jnp.bfloat16)
     low_ref[...] = low
-    features = kernel_ref.shape[2]
+    features = hold_ref.shape[2]
+    part_bands = kernel_refs[0].shape[1]
     copies[4].wait()
-    for pixel in range(kernel_ref.shape[0]):
+    for pixel in range(hold_ref.shape[0]):
         cols = slice(pixel * features, (pixel + 1) * features)
-        kernel_ref[pixel] = dot_nn(low, columns_ref[:, cols]).astype(jnp.bfloat16)
+        hold_ref[pixel] = dot_nn(low, columns_ref[:, cols]).astype(jnp.bfloat16)
+        for key, kernel_ref in enumerate(kernel_refs):
+            first = 0
+            if len(kernel_refs) > 1:
+                first = jnp.bitwise_xor(lax.axis_index("band"), key) * part_bands
+                first = pl.multiple_of(first, part_bands)
+            kernel_ref[pixel] = hold_ref[pixel, pl.ds(first, part_bands), :]
     copies[5].wait()
     token_state = states[bands : bands + 8]
     embed_bias_ref[...] = dot_full(token_state, bias_w_ref[...].astype(f32))
 
 
-def generate_fast(wavelengths, token, gen_attn, gen_gain, ff_in, ff_out, gen_bias, columns):
+def generate_fast(parts, wavelengths, token, gen_attn, gen_gain, ff_in, ff_out, gen_bias, columns):
     f32 = jnp.float32
     bf16 = jnp.bfloat16
     bands = wavelengths.shape[0]
@@ -506,7 +523,6 @@
     padded = -(-(bands + 1) // 8) * 8
     features = gen_bias.shape[1]
     shapes = [
-        ((columns.shape[1] // features, bands, features), bf16),
         ((8, features), f32),
         ((bands, width), bf16),
         ((padded, width), f32),
@@ -515,6 +531,8 @@
         ((padded, ff_in.shape[1]), f32),
         ((2, padded, width), f32),
     ]
+    pixels = columns.shape[1] // features
+    shapes = [((pixels, bands // parts, features), bf16)] * parts + shapes
     inside = pl.BlockSpec(memory_space=pltpu.VMEM)
     outside = pl.BlockSpec(memory_space=pl.ANY)
     weights = (gen_attn, gen_gain, ff_in, ff_out, gen_bias, columns)
@@ -525,7 +543,10 @@
         in_specs=[inside] * 2 + [outside] * 6,
         out_specs=[inside] * len(shapes),
         scratch_shapes=[pltpu.VMEM(weight.shape, bf16) for weight in weights]
-        + [pltpu.SemaphoreType.DMA((6,))],
+        + [
+            pltpu.VMEM((pixels, bands, features), bf16),
+            pltpu.SemaphoreType.DMA((6,)),
+        ],
     )
 
 
@@ -711,6 +732,7 @@
             pl.BlockSpec((row_total, depth), lambda step: (0, step)),
         ]
         + specs,
+        limit=63,
         grid=(group_steps * len(kernel_groups),),
         out_shape=[jax.ShapeDtypeStruct((rows, width), jnp.bfloat16)] * owners,
         out_specs=[pl.BlockSpec((rows, width), lambda step: (0, 0))] * owners,
@@ -1222,7 +1244,9 @@
     spot = lax.axis_index("band")
     spots = jnp.stack([lax.axis_index("dp"), spot]).astype(jnp.int32)
 
-    own_kernel, embed_bias, band_states, *gen_kept = generate_fast(
+    parts = band_size if bands_dev % 16 == 0 else 1
+    outs = generate_fast(
+        parts,
         wavelengths,
         bias_token,
         gen_attn,
@@ -1232,21 +1256,25 @@
         gen_bias,
         gen_kernel,
     )
+    own_kernel = outs[:parts]
+    embed_bias, band_states, *gen_kept = outs[parts:]
     hidden = w_fc1.shape[1]
     weight_rows = [w_qkv.shape[0]] * (4 + hidden // model_width) + [w_fc2.shape[0]]
     stack = stack_weights((w_qkv, w_out, w_fc1, w_fc2))
     patch_rows = flatten_rows(
-        patches.reshape(group_size * slot_count, bands_dev, pixel_count), (own_kernel,)
-    )
-    own_kernel = own_kernel.reshape(own_pixels, band_size, bands_dev, model_width)
+        patches.reshape(group_size * slot_count, bands_dev, pixel_count), (band_states,)
+    )
     other_bands = range(1, band_size)
     dp_steps = bit_steps(dp_size)[1:]
     orders = [turn(dp_steps, group) for group in range(groups)]
 
-    sent = [
-        lax.dynamic_index_in_dim(own_kernel, spot ^ key, 1, keepdims=False).transpose(1, 0, 2)
-        for key in range(band_size)
-    ]
+    if parts == 1:
+        whole = own_kernel[0].reshape(own_pixels, band_size, bands_dev, model_width)
+        own_kernel = [
+            lax.dynamic_index_in_dim(whole, spot ^ key, 1, keepdims=False)
+            for key in range(band_size)
+        ]
+    sent = [part.transpose(1, 0, 2) for part in own_kernel]
     got = [swap(sent[key], "band", key) for key in other_bands]
     *got, patch_rows, stack = together(*got, patch_rows, stack)
     piece = place(

time: 465 us -> 460 us (0.989)
  transfers between devices with their start and end apart: 65 -> 65, of which waited for: 22 -> 22; matrix products, arithmetic and copies ran while one was open for 7% -> 7% of each run, Pallas kernels for 29% -> 30%
where the time goes in v4:
time: 460 us; the launch traced here: 455 us
  Pallas kernels  185 us (40%)
  waiting for transfers between devices  121 us (26%)
  starting transfers between devices  105 us (23%)
  other arithmetic  22.7 us (5%)
  local copies, waits for them, and re-layouts  19.7 us (4%)
    pallas_call x18, Pallas kernels, run_kernel(): pl.pallas_call(whole, in_specs=[pl.BlockSpec(memory_space=pl.ANY)] * coun...  185 us
    ppermute x65, waiting for transfers between devices, swap(): lax.ppermute(values, axis, [(spot, spot ^ step) for spot in range(size)])  121 us
    ppermute x65, starting transfers between devices, swap(): lax.ppermute(values, axis, [(spot, spot ^ step) for spot in range(size)])  105 us
  transfers between devices with their start and end apart: 65, of which 22 were waited for; matrix products, arithmetic and copies ran while one was open for 7% of the time, Pallas kernels for 30%

profile of v4, /device:TPU:1, one launch (start us, length us, event | category | flops | bytes accessed | tf_op | source)
XLA Modules:
  0.0 454.9 jit_solution(15440634415341613767)
XLA Ops:
  0.7 7.2 %shard_map.323 = (bf16[8,32,768]{2,1,0:T(8,128)(2,1)}, bf16[8,32,768]{2,1,0:T(8,128)(2,1)}, bf16[8,32,768]{2,1,0:T(8,128)(2,1)}, bf16[8,32,768]{2,1,0:T(8,128)(2...) custom-call(s32[1,128]{1,0:T(1,128)} %bitcast.223, ...), custom_call_target="tpu_custom_call" | custom-call | flops 1000 | bytes 1000 | tf_op jit(solution)/shard_map/pallas_call | solution.py:93
  12.4 18.8 %shard_map.324.refs_1_ = bf16[1024,8192]{1,0:T(8,128)(2,1)} custom-call(bf16[128,128]{1,0:T(8,128)(2,1)} %get-tuple-element.168.refs_0_, bf16[1024,32,256]{2,1,0:T(8,128)(2,1)} %bitcast.186), custom_call_target="tpu_custom_call" | custom-call | flops 1000 | bytes 1000 | tf_op jit(solution)/shard_map/pallas_call | solution.py:93
  44.5 8.3 %collective-permute-start.6 = (bf16[288,768]{1,0:T(8,128)(2,1)S(1)}, bf16[288,768]{1,0:T(8,128)(2,1)S(1)}, u32[]{:S(2)}, u32[]{:S(2)}) collective-permute-start(bf16[288,768]{1,0:T(8,128)(2,1)S(1)} %copy-done.11), channel_id=1, source_target_pairs={{0,2},{1,3},{2,0},{3,1},{4,6},{5,7},{6,4},{7,5},{8,10},{9,11},{10,... | collective-permute-start | bytes 1327112 | tf_op jit(solution)/shard_map/ppermute | solution.py:39
  52.8 19.0 %collective-permute-done.6.refs_3_ = bf16[288,768]{1,0:T(8,128)(2,1)S(1)} collective-permute-done((bf16[288,768]{1,0:T(8,128)(2,1)S(1)}, bf16[288,768]{1,0:T(8,128)(2,1)S(1)}, u32[]{:S(2)}, u32[]{:S(2)}) %collective-permute-start.6) | collective-permute-done | bytes 442400 | tf_op jit(solution)/shard_map/ppermute | solution.py:39
  76.8 11.0 %collective-permute-done.10.refs_2_ = bf16[288,768]{1,0:T(8,128)(2,1)S(1)} collective-permute-done((bf16[288,768]{1,0:T(8,128)(2,1)S(1)}, bf16[288,768]{1,0:T(8,128)(2,1)S(1)}, u32[]{:S(2)}, u32[]{:S(2)}) %collective-permute-start.10) | collective-permute-done | bytes 442400 | tf_op jit(solution)/shard_map/ppermute | solution.py:39
  87.8 9.1 %collective-permute-done.11.refs_4_ = bf16[288,768]{1,0:T(8,128)(2,1)S(1)} collective-permute-done((bf16[288,768]{1,0:T(8,128)(2,1)S(1)}, bf16[288,768]{1,0:T(8,128)(2,1)S(1)}, u32[]{:S(2)}, u32[]{:S(2)}) %collective-permute-start.11) | collective-permute-done | bytes 442400 | tf_op jit(solution)/shard_map/ppermute | solution.py:39
  96.9 10.3 %collective-permute-done.8.refs_11_.refs_14_ = bf16[2,16,32,768]{3,2,1,0:T(8,128)(2,1)S(1)} collective-permute-done((bf16[2,16,32,768]{3,2,1,0:T(8,128)(2,1)S(1)}, bf16[2,16,32,768]{3,2,1,0:T(8,128)(2,1)S(1)}, u32[]{:S(2)}, u32[]{:S(2)}) %collective-permute-start.8) | collective-permute-done | bytes 1572896 | tf_op jit(solution)/shard_map/ppermute | solution.py:39
  119.1 20.2 %shard_map.327 = (bf16[256,768]{1,0:T(8,128)(2,1)}, bf16[256,768]{1,0:T(8,128)(2,1)}, bf16[256,768]{1,0:T(8,128)(2,1)}, bf16[256,768]{1,0:T(8,128)(2,1)}) custom-call(s32[2]{0:T(128)} %pad_add_fusion.refs_0_.refs_12_.refs_7_, bf16[1024,8192]{1,0:T(8,128)(2,1)} %shard_map.324.refs_1_, bf16[1,32,32,768]{3,2,1,0:T(8,128)(2,1)} %bitcast.182, ...), custom_call_target="tpu_custom_call" | custom-call | flops 1000 | bytes 1000 | tf_op jit(solution)/shard_map/pallas_call | solution.py:93
  149.3 13.4 %collective-permute-done.19.refs_1_ = bf16[256,768]{1,0:T(8,128)(2,1)S(1)} collective-permute-done((bf16[256,768]{1,0:T(8,128)(2,1)}, bf16[256,768]{1,0:T(8,128)(2,1)S(1)}, u32[]{:S(2)}, u32[]{:S(2)}) %collective-permute-start.19) | collective-permute-done | bytes 393248 | tf_op jit(solution)/shard_map/ppermute | solution.py:39
  162.7 10.9 %collective-permute-done.20.refs_2_ = bf16[256,768]{1,0:T(8,128)(2,1)S(1)} collective-permute-done((bf16[256,768]{1,0:T(8,128)(2,1)}, bf16[256,768]{1,0:T(8,128)(2,1)S(1)}, u32[]{:S(2)}, u32[]{:S(2)}) %collective-permute-start.20) | collective-permute-done | bytes 393248 | tf_op jit(solution)/shard_map/ppermute | solution.py:39
  173.7 7.5 %collective-permute-done.18.refs_9_ = bf16[2,576,768]{2,1,0:T(8,128)(2,1)} collective-permute-done((bf16[2,576,768]{2,1,0:T(8,128)(2,1)S(1)}, bf16[2,576,768]{2,1,0:T(8,128)(2,1)}, u32[]{:S(2)}, u32[]{:S(2)}) %collective-permute-start.18) | collective-permute-done | bytes 1769504 | tf_op jit(solution)/shard_map/ppermute | solution.py:39
  196.9 25.6 %shard_map.328 = (bf16[256,768]{1,0:T(8,128)(2,1)}, bf16[256,768]{1,0:T(8,128)(2,1)}, bf16[256,13056]{1,0:T(8,128)(2,1)}, f32[8,768]{1,0:T(8,128)}) custom-call(bf16[256,768]{1,0:T(8,128)(2,1)} %get-tuple-element.197.refs_0_, bf16[256,768]{1,0:T(8,128)(2,1)} %copy-done.23, bf16[256,768]{1,0:T(8,128)(2,1)} %copy-done.24, bf16[256,768]{1,0:T(8,128)(2,1)} %copy-done.25, ...), custom_call_target="tpu_custom_call" | custom-call | flops 1000 | bytes 1000 | tf_op jit(solution)/shard_map/pallas_call | solution.py:93
  226.5 7.1 %collective-permute-done.29.refs_2_ = bf16[256,13056]{1,0:T(8,128)(2,1)} collective-permute-done((bf16[256,13056]{1,0:T(8,128)(2,1)}, bf16[256,13056]{1,0:T(8,128)(2,1)}, u32[]{:S(2)}, u32[]{:S(2)}) %collective-permute-start.29) | collective-permute-done | bytes 6684704 | tf_op jit(solution)/shard_map/ppermute | solution.py:39
  233.7 11.1 %shard_map.329 = (bf16[2,128,768]{2,1,0:T(8,128)(2,1)}, bf16[2,128,768]{2,1,0:T(8,128)(2,1)}, bf16[2,96,768]{2,1,0:T(8,128)(2,1)}, bf16[2,96,768]{2,1,0:T(8,128)...) custom-call(s32[2]{0:T(128)} %pad_add_fusion.refs_0_.refs_12_.refs_7, ...), custom_call_target="tpu_custom_call" | custom-call | flops 1000 | bytes 1000 | tf_op jit(solution)/shard_map/pallas_call | solution.py:93
  244.8 6.8 %collective-permute-done.27.refs_4_.refs_3_ = bf16[256,768]{1,0:T(8,128)(2,1)} collective-permute-done((bf16[256,768]{1,0:T(8,128)(2,1)}, bf16[256,768]{1,0:T(8,128)(2,1)}, u32[]{:S(2)}, u32[]{:S(2)}) %collective-permute-start.27) | collective-permute-done | bytes 393248 | tf_op jit(solution)/shard_map/ppermute | solution.py:39
  251.7 12.8 %shard_map.332 = (bf16[16,4,32,768]{3,2,1,0:T(8,128)(2,1)}, bf16[16,4,32,768]{3,2,1,0:T(8,128)(2,1)}) custom-call(s32[2]{0:T(128)} %pad_add_fusion.refs_0_.refs_12_.refs_7_, bf16[1024,8192]{1,0:T(8,128)(2,1)} %shard_map.324.refs_1_, bf16[256,768]{1,0:T(8,128)(2,1)} %get-tuple-element.223.refs_2_.refs_1_, bf16[256,768]{1,0:T(8,128)(2,1)} %copy-done.8, ...), custom_call_target="tpu_custom_call" | custom-call | flops 1000 | bytes 1000 | tf_op jit(solution)/shard_map/pallas_call | solution.py:93
  265.9 13.1 %shard_map.330 = (bf16[16,4,32,768]{3,2,1,0:T(8,128)(2,1)}, bf16[16,4,32,768]{3,2,1,0:T(8,128)(2,1)}) custom-call(s32[2]{0:T(128)} %pad_add_fusion.refs_0_.refs_12_.refs_7_, bf16[1024,8192]{1,0:T(8,128)(2,1)} %shard_map.324.refs_1_, bf16[256,768]{1,0:T(8,128)(2,1)} %get-tuple-element.223.refs_2_.refs_1_, bf16[256,768]{1,0:T(8,128)(2,1)} %copy-done.8, ...), custom_call_target="tpu_custom_call" | custom-call | flops 1000 | bytes 1000 | tf_op jit(solution)/shard_map/pallas_call | solution.py:93
  295.8 8.1 %collective-permute-start.36 = (bf16[2,104,768]{2,1,0:T(8,128)(2,1)}, bf16[2,104,768]{2,1,0:T(8,128)(2,1)S(1)}, u32[]{:S(2)}, u32[]{:S(2)}) collective-permute-start(bf16[2,104,768]{2,1,0:T(8,128)(2,1)} %get-tuple-element.317), channel_id=1, source_target_pairs={{0,1},{1,0},{2,3},{3,2},{4,5},{5,4},{6,7},{7,6},{8,9},{9,8},{10,11... | collective-permute-start | bytes 958472 | tf_op jit(solution)/shard_map/ppermute | solution.py:39
  306.1 20.4 %shard_map.334.refs_1_ = bf16[1024,8192]{1,0:T(8,128)(2,1)} custom-call(s32[2]{0:T(128)} %pad_add_fusion.refs_0_.refs_12_.refs_7_, bf16[256,768]{1,0:T(8,128)(2,1)} %get-tuple-element.223.refs_2_.refs_1_, bf16[256,768]{1,0:T(8,128)(2,1)} %copy-done.8, bf16[256,768]{1,0:T(8,128)(2,1)} %collective-permute-done.27.refs_4_.refs_3_, ...), custom_call_target="tpu_custom_call" | custom-call | flops 1000 | bytes 1000 | tf_op jit(solution)/shard_map/pallas_call | solution.py:93
  367.1 18.8 %shard_map.338 = bf16[1024,32,256]{2,1,0:T(8,128)(2,1)} custom-call(bf16[8,32,768]{2,1,0:T(8,128)(2,1)} %get-tuple-element.279.refs_0_.refs_2_, bf16[1024,8192]{1,0:T(8,128)(2,1)} %shard_map.334.refs_1_), custom_call_target="tpu_custom_call" | custom-call | flops 1000 | bytes 1000 | tf_op jit(solution)/shard_map/pallas_call | solution.py:93
  397.5 6.1 %collective-permute-start.49 = (f32[136,128]{1,0:T(8,128)}, f32[136,128]{1,0:T(8,128)S(1)}, u32[]{:S(2)}, u32[]{:S(2)}) collective-permute-start(f32[136,128]{1,0:T(8,128)} %get-tuple-element.285), channel_id=1, source_target_pairs={{0,1},{1,0},{2,3},{3,2},{4,5},{5,4},{6,7},{7,6},{8,9},{9,8},{10,11... | collective-permute-start | bytes 208904 | tf_op jit(solution)/shard_map/ppermute | solution.py:39
  412.5 6.3 %collective-permute-start.52 = (f32[136,128]{1,0:T(8,128)S(1)}, f32[136,128]{1,0:T(8,128)S(1)}, u32[]{:S(2)}, u32[]{:S(2)}) collective-permute-start(f32[136,128]{1,0:T(8,128)S(1)} %add_add_fusion), channel_id=1, source_target_pairs={{0,4},{4,0},{8,12},{12,8},{16,20},{20,16},{24,28},{28,24},{1,5},{5... | collective-permute-start | bytes 208904 | tf_op jit(solution)/shard_map/ppermute | solution.py:39
  433.2 8.1 %shard_map.340 = (f32[1,128]{1,0:T(1,128)}, f32[4,128,128]{2,1,0:T(8,128)}, f32[2,128]{1,0:T(2,128)}, f32[128,2048]{1,0:T(8,128)}, f32[2048,128]{1,0:T(8,128)}, /*index=5*/f32[128,768]{1,0:T(8,128)}) custom-call(f32[136,128]{1,0:T(8,128)} %add.277.refs_0_, bf16[4,128,128]{2,1,0:T(8,128)(2,1)} %refs_1_.5, bf16[2,128]{1,0:T(2,128)(2,1)} %refs_2_.5, ...), custom_call_target="tpu_custom_call" | custom-call | flops 1000 | bytes 1000 | tf_op jit(solution)/shard_map/pallas_call | solution.py:93
  441.3 8.8 %collective-permute-start.61 = (bf16[16,8,768]{2,1,0:T(8,128)(2,1)S(1)}, bf16[16,8,768]{2,1,0:T(8,128)(2,1)S(1)}, u32[]{:S(2)}, u32[]{:S(2)}) collective-permute-start(bf16[16,8,768]{2,1,0:T(8,128)(2,1)S(1)} %pad_maximum_fusion.10), channel_id=1, source_target_pairs={{0,4},{4,0},{8,12},{12,8},{16,20},{20,16},{24,28},{28,24},{1,5},{5... | collective-permute-start | bytes 589832 | tf_op jit(solution)/shard_map/ppermute | solution.py:39
  (314 shorter events, 164.3 us)
Async XLA Ops:
  7.9 25.7 %collective-permute-start = (bf16[32,8,768]{2,0,1:T(8,128)(2,1)}, bf16[32,8,768]{2,0,1:T(8,128)(2,1)S(1)}, u32[]{:S(2)}, u32[]{:S(2)}) collective-permute-start(bf16[32,8,768]{2,0,1:T(8,128)(2,1)} %bitcast.232), channel_id=1, source_target_pairs={{0,1},{1,0},{2,3},{3,2},{4,5},{5,4},{6,7},{7,6},{8,9},{9,8},{10,11... | collective-permute-start | bytes 1179656 | tf_op jit(solution)/shard_map/ppermute | solution.py:39
  38.6 33.1 %collective-permute-start.5 = (bf16[32,32,768]{2,1,0:T(8,128)(2,1)S(1)}, bf16[32,32,768]{2,1,0:T(8,128)(2,1)}, u32[]{:S(2)}, u32[]{:S(2)}) collective-permute-start(bf16[32,32,768]{2,1,0:T(8,128)(2,1)S(1)} %bitcast.181), channel_id=1, source_target_pairs={{0,4},{4,0},{8,12},{12,8},{16,20},{20,16},{24,28},{28,24},{1,5},{5... | collective-permute-start | bytes 4718600 | tf_op jit(solution)/shard_map/ppermute | solution.py:39
  42.0 29.8 %collective-permute-start.3 = (bf16[1,16,32,768]{3,2,1,0:T(8,128)(2,1)S(1)}, bf16[1,16,32,768]{3,2,1,0:T(8,128)(2,1)S(1)}, u32[]{:S(2)}, u32[]{:S(2)}) collective-permute-start(bf16[1,16,32,768]{3,2,1,0:T(8,128)(2,1)S(1)} %get-tuple-element.314), channel_id=1, source_target_pairs={{0,8},{4,12},{8,0},{12,4},{16,24},{20,28},{24,16},{28,20},{1,9},{5... | collective-permute-start | bytes 2359304 | tf_op jit(solution)/shard_map/ppermute | solution.py:39
  43.2 28.5 %collective-permute-start.4 = (bf16[1,16,32,768]{3,2,1,0:T(8,128)(2,1)S(1)}, bf16[1,16,32,768]{3,2,1,0:T(8,128)(2,1)S(1)}, u32[]{:S(2)}, u32[]{:S(2)}) collective-permute-start(bf16[1,16,32,768]{3,2,1,0:T(8,128)(2,1)S(1)} %get-tuple-element.313), channel_id=1, source_target_pairs={{0,16},{4,20},{8,24},{12,28},{16,0},{20,4},{24,8},{28,12},{1,17},{... | collective-permute-start | bytes 2359304 | tf_op jit(solution)/shard_map/ppermute | solution.py:39
  44.5 27.3 %collective-permute-start.6 = (bf16[288,768]{1,0:T(8,128)(2,1)S(1)}, bf16[288,768]{1,0:T(8,128)(2,1)S(1)}, u32[]{:S(2)}, u32[]{:S(2)}) collective-permute-start(bf16[288,768]{1,0:T(8,128)(2,1)S(1)} %copy-done.11), channel_id=1, source_target_pairs={{0,2},{1,3},{2,0},{3,1},{4,6},{5,7},{6,4},{7,5},{8,10},{9,11},{10,... | collective-permute-start | bytes 1327112 | tf_op jit(solution)/shard_map/ppermute | solution.py:39
  72.8 34.4 %collective-permute-start.8 = (bf16[2,16,32,768]{3,2,1,0:T(8,128)(2,1)S(1)}, bf16[2,16,32,768]{3,2,1,0:T(8,128)(2,1)S(1)}, u32[]{:S(2)}, u32[]{:S(2)}) collective-permute-start(bf16[2,16,32,768]{3,2,1,0:T(8,128)(2,1)S(1)} %pad_maximum_fusion.3), channel_id=1, source_target_pairs={{0,8},{4,12},{8,0},{12,4},{16,24},{20,28},{24,16},{28,20},{1,9},{5... | collective-permute-start | bytes 4718600 | tf_op jit(solution)/shard_map/ppermute | solution.py:39
  73.3 34.2 %collective-permute-start.7 = (bf16[2,16,32,768]{3,2,1,0:T(8,128)(2,1)S(1)}, bf16[2,16,32,768]{3,2,1,0:T(8,128)(2,1)}, u32[]{:S(2)}, u32[]{:S(2)}) collective-permute-start(bf16[2,16,32,768]{3,2,1,0:T(8,128)(2,1)S(1)} %pad_maximum_fusion.2), channel_id=1, source_target_pairs={{0,16},{4,20},{8,24},{12,28},{16,0},{20,4},{24,8},{28,12},{1,17},{... | collective-permute-start | bytes 4718600 | tf_op jit(solution)/shard_map/ppermute | solution.py:39
  113.8 25.6 %collective-permute-start.15 = (bf16[576,768]{1,0:T(8,128)(2,1)}, bf16[576,768]{1,0:T(8,128)(2,1)}, u32[]{:S(2)}, u32[]{:S(2)}) collective-permute-start(bf16[576,768]{1,0:T(8,128)(2,1)} %get-tuple-element.180), channel_id=1, source_target_pairs={{0,8},{4,12},{8,0},{12,4},{16,24},{20,28},{24,16},{28,20},{1,9},{5... | collective-permute-start | bytes 2654216 | tf_op jit(solution)/shard_map/ppermute | solution.py:39
  141.1 40.0 %collective-permute-start.18 = (bf16[2,576,768]{2,1,0:T(8,128)(2,1)S(1)}, bf16[2,576,768]{2,1,0:T(8,128)(2,1)}, u32[]{:S(2)}, u32[]{:S(2)}) collective-permute-start(bf16[2,576,768]{2,1,0:T(8,128)(2,1)S(1)} %pad_maximum_fusion.1.refs_8_), channel_id=1, source_target_pairs={{0,8},{4,12},{8,0},{12,4},{16,24},{20,28},{24,16},{28,20},{1,9},{5... | collective-permute-start | bytes 5308424 | tf_op jit(solution)/shard_map/ppermute | solution.py:39
  144.4 40.2 %collective-permute-start.17 = (bf16[2,576,768]{2,1,0:T(8,128)(2,1)}, bf16[2,576,768]{2,1,0:T(8,128)(2,1)}, u32[]{:S(2)}, u32[]{:S(2)}) collective-permute-start(bf16[2,576,768]{2,1,0:T(8,128)(2,1)} %pad_maximum_fusion.refs_4_), channel_id=1, source_target_pairs={{0,16},{4,20},{8,24},{12,28},{16,0},{20,4},{24,8},{28,12},{1,17},{... | collective-permute-start | bytes 5308424 | tf_op jit(solution)/shard_map/ppermute | solution.py:39
  145.6 28.0 %collective-permute-start.20 = (bf16[256,768]{1,0:T(8,128)(2,1)}, bf16[256,768]{1,0:T(8,128)(2,1)S(1)}, u32[]{:S(2)}, u32[]{:S(2)}) collective-permute-start(bf16[256,768]{1,0:T(8,128)(2,1)} %get-tuple-element.195), channel_id=1, source_target_pairs={{0,2},{1,3},{2,0},{3,1},{4,6},{5,7},{6,4},{7,5},{8,10},{9,11},{10,... | collective-permute-start | bytes 1179656 | tf_op jit(solution)/shard_map/ppermute | solution.py:39
  146.5 27.2 %collective-permute-start.21 = (bf16[256,768]{1,0:T(8,128)(2,1)}, bf16[256,768]{1,0:T(8,128)(2,1)S(1)}, u32[]{:S(2)}, u32[]{:S(2)}) collective-permute-start(bf16[256,768]{1,0:T(8,128)(2,1)} %get-tuple-element.196), channel_id=1, source_target_pairs={{0,3},{1,2},{2,1},{3,0},{4,7},{5,6},{6,5},{7,4},{8,11},{9,10},{10,... | collective-permute-start | bytes 1179656 | tf_op jit(solution)/shard_map/ppermute | solution.py:39
  223.0 28.7 %collective-permute-start.27 = (bf16[256,768]{1,0:T(8,128)(2,1)}, bf16[256,768]{1,0:T(8,128)(2,1)}, u32[]{:S(2)}, u32[]{:S(2)}) collective-permute-start(bf16[256,768]{1,0:T(8,128)(2,1)} %get-tuple-element.223.refs_2_.refs_1_), channel_id=1, source_target_pairs={{0,2},{1,3},{2,0},{3,1},{4,6},{5,7},{6,4},{7,5},{8,10},{9,11},{10,... | collective-permute-start | bytes 1179656 | tf_op jit(solution)/shard_map/ppermute | solution.py:39
  223.8 27.8 %collective-permute-start.28 = (bf16[256,768]{1,0:T(8,128)(2,1)}, bf16[256,768]{1,0:T(8,128)(2,1)}, u32[]{:S(2)}, u32[]{:S(2)}) collective-permute-start(bf16[256,768]{1,0:T(8,128)(2,1)} %get-tuple-element.223.refs_2_.refs_1_), channel_id=1, source_target_pairs={{0,3},{1,2},{2,1},{3,0},{4,7},{5,6},{6,5},{7,4},{8,11},{9,10},{10,... | collective-permute-start | bytes 1179656 | tf_op jit(solution)/shard_map/ppermute | solution.py:39
  290.0 39.0 %collective-permute-start.34 = (bf16[16,2,32,768]{3,2,1,0:T(8,128)(2,1)}, bf16[16,2,32,768]{3,2,1,0:T(8,128)(2,1)}, u32[]{:S(2)}, u32[]{:S(2)}) collective-permute-start(bf16[16,2,32,768]{3,2,1,0:T(8,128)(2,1)} %bitcast.226), channel_id=1, source_target_pairs={{0,8},{4,12},{8,0},{12,4},{16,24},{20,28},{24,16},{28,20},{1,9},{5... | collective-permute-start | bytes 4718600 | tf_op jit(solution)/shard_map/ppermute | solution.py:39
  290.6 38.4 %collective-permute-start.35 = (bf16[16,2,32,768]{3,2,1,0:T(8,128)(2,1)}, bf16[16,2,32,768]{3,2,1,0:T(8,128)(2,1)}, u32[]{:S(2)}, u32[]{:S(2)}) collective-permute-start(bf16[16,2,32,768]{3,2,1,0:T(8,128)(2,1)} %bitcast.225), channel_id=1, source_target_pairs={{0,16},{4,20},{8,24},{12,28},{16,0},{20,4},{24,8},{28,12},{1,17},{... | collective-permute-start | bytes 4718600 | tf_op jit(solution)/shard_map/ppermute | solution.py:39
  295.8 32.5 %collective-permute-start.36 = (bf16[2,104,768]{2,1,0:T(8,128)(2,1)}, bf16[2,104,768]{2,1,0:T(8,128)(2,1)S(1)}, u32[]{:S(2)}, u32[]{:S(2)}) collective-permute-start(bf16[2,104,768]{2,1,0:T(8,128)(2,1)} %get-tuple-element.317), channel_id=1, source_target_pairs={{0,1},{1,0},{2,3},{3,2},{4,5},{5,4},{6,7},{7,6},{8,9},{9,8},{10,11... | collective-permute-start | bytes 958472 | tf_op jit(solution)/shard_map/ppermute | solution.py:39
  339.6 46.3 %collective-permute-start.39 = (bf16[848,768]{1,0:T(8,128)(2,1)}, bf16[848,768]{1,0:T(8,128)(2,1)}, u32[]{:S(2)}, u32[]{:S(2)}) collective-permute-start(bf16[848,768]{1,0:T(8,128)(2,1)} %pad_maximum_fusion.4), channel_id=1, source_target_pairs={{0,16},{4,20},{8,24},{12,28},{16,0},{20,4},{24,8},{28,12},{1,17},{... | collective-permute-start | bytes 3907592 | tf_op jit(solution)/shard_map/ppermute | solution.py:39
  354.5 34.9 %collective-permute-start.45 = (bf16[840,768]{1,0:T(8,128)(2,1)}, bf16[840,768]{1,0:T(8,128)(2,1)}, u32[]{:S(2)}, u32[]{:S(2)}) collective-permute-start(bf16[840,768]{1,0:T(8,128)(2,1)} %pad_maximum_fusion.5), channel_id=1, source_target_pairs={{0,8},{4,12},{8,0},{12,4},{16,24},{20,28},{24,16},{28,20},{1,9},{5... | collective-permute-start | bytes 3870728 | tf_op jit(solution)/shard_map/ppermute | solution.py:39
  359.6 33.3 %collective-permute-start.46 = (bf16[8,32,768]{2,1,0:T(8,128)(2,1)}, bf16[8,32,768]{2,1,0:T(8,128)(2,1)}, u32[]{:S(2)}, u32[]{:S(2)}) collective-permute-start(bf16[8,32,768]{2,1,0:T(8,128)(2,1)} %get-tuple-element.269), channel_id=1, source_target_pairs={{0,1},{1,0},{2,3},{3,2},{4,5},{5,4},{6,7},{7,6},{8,9},{9,8},{10,11... | collective-permute-start | bytes 1179656 | tf_op jit(solution)/shard_map/ppermute | solution.py:39
  364.6 28.3 %collective-permute-start.47 = (bf16[8,32,768]{2,1,0:T(8,128)(2,1)}, bf16[8,32,768]{2,1,0:T(8,128)(2,1)}, u32[]{:S(2)}, u32[]{:S(2)}) collective-permute-start(bf16[8,32,768]{2,1,0:T(8,128)(2,1)} %get-tuple-element.270), channel_id=1, source_target_pairs={{0,2},{1,3},{2,0},{3,1},{4,6},{5,7},{6,4},{7,5},{8,10},{9,11},{10,... | collective-permute-start | bytes 1179656 | tf_op jit(solution)/shard_map/ppermute | solution.py:39
  365.9 27.0 %collective-permute-start.48 = (bf16[8,32,768]{2,1,0:T(8,128)(2,1)}, bf16[8,32,768]{2,1,0:T(8,128)(2,1)}, u32[]{:S(2)}, u32[]{:S(2)}) collective-permute-start(bf16[8,32,768]{2,1,0:T(8,128)(2,1)} %get-tuple-element.271), channel_id=1, source_target_pairs={{0,3},{1,2},{2,1},{3,0},{4,7},{5,6},{6,5},{7,4},{8,11},{9,10},{10,... | collective-permute-start | bytes 1179656 | tf_op jit(solution)/shard_map/ppermute | solution.py:39
  423.6 26.5 %collective-permute-start.62 = (bf16[1,192,768]{2,1,0:T(8,128)(2,1)S(1)}, bf16[1,192,768]{2,1,0:T(8,128)(2,1)S(1)}, u32[]{:S(2)}, u32[]{:S(2)}) collective-permute-start(bf16[1,192,768]{2,1,0:T(8,128)(2,1)S(1)} %get-tuple-element.319), channel_id=1, source_target_pairs={{0,1},{1,0},{2,3},{3,2},{4,5},{5,4},{6,7},{7,6},{8,9},{9,8},{10,11... | collective-permute-start | bytes 884744 | tf_op jit(solution)/shard_map/ppermute | solution.py:39
  423.7 26.5 %collective-permute-start.63 = (bf16[1,192,768]{2,1,0:T(8,128)(2,1)S(1)}, bf16[1,192,768]{2,1,0:T(8,128)(2,1)S(1)}, u32[]{:S(2)}, u32[]{:S(2)}) collective-permute-start(bf16[1,192,768]{2,1,0:T(8,128)(2,1)S(1)} %get-tuple-element.321), channel_id=1, source_target_pairs={{0,2},{1,3},{2,0},{3,1},{4,6},{5,7},{6,4},{7,5},{8,10},{9,11},{10,... | collective-permute-start | bytes 884744 | tf_op jit(solution)/shard_map/ppermute | solution.py:39
  (78 other events, 1161.3 us)

commit v5 on v4

--- a/solution.py
+++ b/solution.py
@@ -1131,11 +1131,12 @@
     outer = math.prod(shape[:at]) * 2**place_of
     part_outer = outer // len(gots)
     inner_rows = keep.size // (outer * 2 * width)
+    rows_most = max(part_outer * inner_rows // 2, 16)
     rows_step = inner_rows
-    while rows_step > 512 and rows_step % 32 == 0:
+    while rows_step > rows_most and rows_step % 32 == 0:
         rows_step //= 2
     outer_step = 1
-    while part_outer % (2 * outer_step) == 0 and 2 * outer_step * rows_step <= 512:
+    while part_outer % (2 * outer_step) == 0 and 2 * outer_step * rows_step <= rows_most:
         outer_step *= 2
     part_steps = part_outer // outer_step
     block_in = (outer_step, 2, rows_step, width)

time: 460 us -> 459 us (level)
  transfers between devices with their start and end apart: 65 -> 65, of which waited for: 22 -> 22; matrix products, arithmetic and copies ran while one was open for 7% -> 7% of each run, Pallas kernels for 30% -> 29%
where the time goes in v5:
time: 459 us; the launch traced here: 454 us
  Pallas kernels  184 us (40%)
  waiting for transfers between devices  121 us (26%)
  starting transfers between devices  105 us (23%)
  other arithmetic  22.7 us (5%)
  local copies, waits for them, and re-layouts  19.7 us (4%)
    pallas_call x18, Pallas kernels, run_kernel(): pl.pallas_call(whole, in_specs=[pl.BlockSpec(memory_space=pl.ANY)] * coun...  184 us
    ppermute x65, waiting for transfers between devices, swap(): lax.ppermute(values, axis, [(spot, spot ^ step) for spot in range(size)])  121 us
    ppermute x65, starting transfers between devices, swap(): lax.ppermute(values, axis, [(spot, spot ^ step) for spot in range(size)])  105 us
  transfers between devices with their start and end apart: 65, of which 22 were waited for; matrix products, arithmetic and copies ran while one was open for 7% of the time, Pallas kernels for 29%

profile of v5, /device:TPU:1, one launch (start us, length us, event | category | flops | bytes accessed | tf_op | source)
XLA Modules:
  0.0 454.1 jit_solution(2870768719619183788)
XLA Ops:
  0.7 7.2 %shard_map.323 = (bf16[8,32,768]{2,1,0:T(8,128)(2,1)}, bf16[8,32,768]{2,1,0:T(8,128)(2,1)}, bf16[8,32,768]{2,1,0:T(8,128)(2,1)}, bf16[8,32,768]{2,1,0:T(8,128)(2...) custom-call(s32[1,128]{1,0:T(1,128)} %bitcast.223, ...), custom_call_target="tpu_custom_call" | custom-call | flops 1000 | bytes 1000 | tf_op jit(solution)/shard_map/pallas_call | solution.py:93
  12.4 18.8 %shard_map.324.refs_1_ = bf16[1024,8192]{1,0:T(8,128)(2,1)} custom-call(bf16[128,128]{1,0:T(8,128)(2,1)} %get-tuple-element.168.refs_0_, bf16[1024,32,256]{2,1,0:T(8,128)(2,1)} %bitcast.186), custom_call_target="tpu_custom_call" | custom-call | flops 1000 | bytes 1000 | tf_op jit(solution)/shard_map/pallas_call | solution.py:93
  44.5 8.3 %collective-permute-start.6 = (bf16[288,768]{1,0:T(8,128)(2,1)S(1)}, bf16[288,768]{1,0:T(8,128)(2,1)S(1)}, u32[]{:S(2)}, u32[]{:S(2)}) collective-permute-start(bf16[288,768]{1,0:T(8,128)(2,1)S(1)} %copy-done.11), channel_id=1, source_target_pairs={{0,2},{1,3},{2,0},{3,1},{4,6},{5,7},{6,4},{7,5},{8,10},{9,11},{10,... | collective-permute-start | bytes 1327112 | tf_op jit(solution)/shard_map/ppermute | solution.py:39
  52.8 19.0 %collective-permute-done.6.refs_3_ = bf16[288,768]{1,0:T(8,128)(2,1)S(1)} collective-permute-done((bf16[288,768]{1,0:T(8,128)(2,1)S(1)}, bf16[288,768]{1,0:T(8,128)(2,1)S(1)}, u32[]{:S(2)}, u32[]{:S(2)}) %collective-permute-start.6) | collective-permute-done | bytes 442400 | tf_op jit(solution)/shard_map/ppermute | solution.py:39
  76.8 11.0 %collective-permute-done.10.refs_2_ = bf16[288,768]{1,0:T(8,128)(2,1)S(1)} collective-permute-done((bf16[288,768]{1,0:T(8,128)(2,1)S(1)}, bf16[288,768]{1,0:T(8,128)(2,1)S(1)}, u32[]{:S(2)}, u32[]{:S(2)}) %collective-permute-start.10) | collective-permute-done | bytes 442400 | tf_op jit(solution)/shard_map/ppermute | solution.py:39
  87.8 9.1 %collective-permute-done.11.refs_4_ = bf16[288,768]{1,0:T(8,128)(2,1)S(1)} collective-permute-done((bf16[288,768]{1,0:T(8,128)(2,1)S(1)}, bf16[288,768]{1,0:T(8,128)(2,1)S(1)}, u32[]{:S(2)}, u32[]{:S(2)}) %collective-permute-start.11) | collective-permute-done | bytes 442400 | tf_op jit(solution)/shard_map/ppermute | solution.py:39
  96.9 10.3 %collective-permute-done.8.refs_11_.refs_14_ = bf16[2,16,32,768]{3,2,1,0:T(8,128)(2,1)S(1)} collective-permute-done((bf16[2,16,32,768]{3,2,1,0:T(8,128)(2,1)S(1)}, bf16[2,16,32,768]{3,2,1,0:T(8,128)(2,1)S(1)}, u32[]{:S(2)}, u32[]{:S(2)}) %collective-permute-start.8) | collective-permute-done | bytes 1572896 | tf_op jit(solution)/shard_map/ppermute | solution.py:39
  119.1 20.2 %shard_map.327 = (bf16[256,768]{1,0:T(8,128)(2,1)}, bf16[256,768]{1,0:T(8,128)(2,1)}, bf16[256,768]{1,0:T(8,128)(2,1)}, bf16[256,768]{1,0:T(8,128)(2,1)}) custom-call(s32[2]{0:T(128)} %pad_add_fusion.refs_0_.refs_12_.refs_7_, bf16[1024,8192]{1,0:T(8,128)(2,1)} %shard_map.324.refs_1_, bf16[1,32,32,768]{3,2,1,0:T(8,128)(2,1)} %bitcast.182, ...), custom_call_target="tpu_custom_call" | custom-call | flops 1000 | bytes 1000 | tf_op jit(solution)/shard_map/pallas_call | solution.py:93
  149.3 13.4 %collective-permute-done.19.refs_1_ = bf16[256,768]{1,0:T(8,128)(2,1)S(1)} collective-permute-done((bf16[256,768]{1,0:T(8,128)(2,1)}, bf16[256,768]{1,0:T(8,128)(2,1)S(1)}, u32[]{:S(2)}, u32[]{:S(2)}) %collective-permute-start.19) | collective-permute-done | bytes 393248 | tf_op jit(solution)/shard_map/ppermute | solution.py:39
  162.7 10.9 %collective-permute-done.20.refs_2_ = bf16[256,768]{1,0:T(8,128)(2,1)S(1)} collective-permute-done((bf16[256,768]{1,0:T(8,128)(2,1)}, bf16[256,768]{1,0:T(8,128)(2,1)S(1)}, u32[]{:S(2)}, u32[]{:S(2)}) %collective-permute-start.20) | collective-permute-done | bytes 393248 | tf_op jit(solution)/shard_map/ppermute | solution.py:39
  173.7 7.5 %collective-permute-done.18.refs_9_ = bf16[2,576,768]{2,1,0:T(8,128)(2,1)} collective-permute-done((bf16[2,576,768]{2,1,0:T(8,128)(2,1)S(1)}, bf16[2,576,768]{2,1,0:T(8,128)(2,1)}, u32[]{:S(2)}, u32[]{:S(2)}) %collective-permute-start.18) | collective-permute-done | bytes 1769504 | tf_op jit(solution)/shard_map/ppermute | solution.py:39
  196.9 25.6 %shard_map.328 = (bf16[256,768]{1,0:T(8,128)(2,1)}, bf16[256,768]{1,0:T(8,128)(2,1)}, bf16[256,13056]{1,0:T(8,128)(2,1)}, f32[8,768]{1,0:T(8,128)}) custom-call(bf16[256,768]{1,0:T(8,128)(2,1)} %get-tuple-element.197.refs_0_, bf16[256,768]{1,0:T(8,128)(2,1)} %copy-done.23, bf16[256,768]{1,0:T(8,128)(2,1)} %copy-done.24, bf16[256,768]{1,0:T(8,128)(2,1)} %copy-done.25, ...), custom_call_target="tpu_custom_call" | custom-call | flops 1000 | bytes 1000 | tf_op jit(solution)/shard_map/pallas_call | solution.py:93
  226.5 7.1 %collective-permute-done.29.refs_2_ = bf16[256,13056]{1,0:T(8,128)(2,1)} collective-permute-done((bf16[256,13056]{1,0:T(8,128)(2,1)}, bf16[256,13056]{1,0:T(8,128)(2,1)}, u32[]{:S(2)}, u32[]{:S(2)}) %collective-permute-start.29) | collective-permute-done | bytes 6684704 | tf_op jit(solution)/shard_map/ppermute | solution.py:39
  233.7 11.1 %shard_map.329 = (bf16[2,128,768]{2,1,0:T(8,128)(2,1)}, bf16[2,128,768]{2,1,0:T(8,128)(2,1)}, bf16[2,96,768]{2,1,0:T(8,128)(2,1)}, bf16[2,96,768]{2,1,0:T(8,128)...) custom-call(s32[2]{0:T(128)} %pad_add_fusion.refs_0_.refs_12_.refs_7, ...), custom_call_target="tpu_custom_call" | custom-call | flops 1000 | bytes 1000 | tf_op jit(solution)/shard_map/pallas_call | solution.py:93
  244.8 6.8 %collective-permute-done.27.refs_4_.refs_3_ = bf16[256,768]{1,0:T(8,128)(2,1)} collective-permute-done((bf16[256,768]{1,0:T(8,128)(2,1)}, bf16[256,768]{1,0:T(8,128)(2,1)}, u32[]{:S(2)}, u32[]{:S(2)}) %collective-permute-start.27) | collective-permute-done | bytes 393248 | tf_op jit(solution)/shard_map/ppermute | solution.py:39
  251.7 12.8 %shard_map.332 = (bf16[16,4,32,768]{3,2,1,0:T(8,128)(2,1)}, bf16[16,4,32,768]{3,2,1,0:T(8,128)(2,1)}) custom-call(s32[2]{0:T(128)} %pad_add_fusion.refs_0_.refs_12_.refs_7_, bf16[1024,8192]{1,0:T(8,128)(2,1)} %shard_map.324.refs_1_, bf16[256,768]{1,0:T(8,128)(2,1)} %get-tuple-element.223.refs_2_.refs_1_, bf16[256,768]{1,0:T(8,128)(2,1)} %copy-done.8, ...), custom_call_target="tpu_custom_call" | custom-call | flops 1000 | bytes 1000 | tf_op jit(solution)/shard_map/pallas_call | solution.py:93
  265.9 13.1 %shard_map.330 = (bf16[16,4,32,768]{3,2,1,0:T(8,128)(2,1)}, bf16[16,4,32,768]{3,2,1,0:T(8,128)(2,1)}) custom-call(s32[2]{0:T(128)} %pad_add_fusion.refs_0_.refs_12_.refs_7_, bf16[1024,8192]{1,0:T(8,128)(2,1)} %shard_map.324.refs_1_, bf16[256,768]{1,0:T(8,128)(2,1)} %get-tuple-element.223.refs_2_.refs_1_, bf16[256,768]{1,0:T(8,128)(2,1)} %copy-done.8, ...), custom_call_target="tpu_custom_call" | custom-call | flops 1000 | bytes 1000 | tf_op jit(solution)/shard_map/pallas_call | solution.py:93
  295.8 8.1 %collective-permute-start.36 = (bf16[2,104,768]{2,1,0:T(8,128)(2,1)}, bf16[2,104,768]{2,1,0:T(8,128)(2,1)S(1)}, u32[]{:S(2)}, u32[]{:S(2)}) collective-permute-start(bf16[2,104,768]{2,1,0:T(8,128)(2,1)} %get-tuple-element.317), channel_id=1, source_target_pairs={{0,1},{1,0},{2,3},{3,2},{4,5},{5,4},{6,7},{7,6},{8,9},{9,8},{10,11... | collective-permute-start | bytes 958472 | tf_op jit(solution)/shard_map/ppermute | solution.py:39
  306.1 20.4 %shard_map.334.refs_1_ = bf16[1024,8192]{1,0:T(8,128)(2,1)} custom-call(s32[2]{0:T(128)} %pad_add_fusion.refs_0_.refs_12_.refs_7_, bf16[256,768]{1,0:T(8,128)(2,1)} %get-tuple-element.223.refs_2_.refs_1_, bf16[256,768]{1,0:T(8,128)(2,1)} %copy-done.8, bf16[256,768]{1,0:T(8,128)(2,1)} %collective-permute-done.27.refs_4_.refs_3_, ...), custom_call_target="tpu_custom_call" | custom-call | flops 1000 | bytes 1000 | tf_op jit(solution)/shard_map/pallas_call | solution.py:93
  366.3 18.8 %shard_map.338 = bf16[1024,32,256]{2,1,0:T(8,128)(2,1)} custom-call(bf16[8,32,768]{2,1,0:T(8,128)(2,1)} %get-tuple-element.279.refs_0_.refs_2_, bf16[1024,8192]{1,0:T(8,128)(2,1)} %shard_map.334.refs_1_), custom_call_target="tpu_custom_call" | custom-call | flops 1000 | bytes 1000 | tf_op jit(solution)/shard_map/pallas_call | solution.py:93
  396.7 6.1 %collective-permute-start.49 = (f32[136,128]{1,0:T(8,128)}, f32[136,128]{1,0:T(8,128)S(1)}, u32[]{:S(2)}, u32[]{:S(2)}) collective-permute-start(f32[136,128]{1,0:T(8,128)} %get-tuple-element.285), channel_id=1, source_target_pairs={{0,1},{1,0},{2,3},{3,2},{4,5},{5,4},{6,7},{7,6},{8,9},{9,8},{10,11... | collective-permute-start | bytes 208904 | tf_op jit(solution)/shard_map/ppermute | solution.py:39
  411.7 6.3 %collective-permute-start.52 = (f32[136,128]{1,0:T(8,128)S(1)}, f32[136,128]{1,0:T(8,128)S(1)}, u32[]{:S(2)}, u32[]{:S(2)}) collective-permute-start(f32[136,128]{1,0:T(8,128)S(1)} %add_add_fusion), channel_id=1, source_target_pairs={{0,4},{4,0},{8,12},{12,8},{16,20},{20,16},{24,28},{28,24},{1,5},{5... | collective-permute-start | bytes 208904 | tf_op jit(solution)/shard_map/ppermute | solution.py:39
  432.4 8.1 %shard_map.340 = (f32[1,128]{1,0:T(1,128)}, f32[4,128,128]{2,1,0:T(8,128)}, f32[2,128]{1,0:T(2,128)}, f32[128,2048]{1,0:T(8,128)}, f32[2048,128]{1,0:T(8,128)}, /*index=5*/f32[128,768]{1,0:T(8,128)}) custom-call(f32[136,128]{1,0:T(8,128)} %add.277.refs_0_, bf16[4,128,128]{2,1,0:T(8,128)(2,1)} %refs_1_.5, bf16[2,128]{1,0:T(2,128)(2,1)} %refs_2_.5, ...), custom_call_target="tpu_custom_call" | custom-call | flops 1000 | bytes 1000 | tf_op jit(solution)/shard_map/pallas_call | solution.py:93
  440.5 8.9 %collective-permute-start.61 = (bf16[16,8,768]{2,1,0:T(8,128)(2,1)S(1)}, bf16[16,8,768]{2,1,0:T(8,128)(2,1)S(1)}, u32[]{:S(2)}, u32[]{:S(2)}) collective-permute-start(bf16[16,8,768]{2,1,0:T(8,128)(2,1)S(1)} %pad_maximum_fusion.10), channel_id=1, source_target_pairs={{0,4},{4,0},{8,12},{12,8},{16,20},{20,16},{24,28},{28,24},{1,5},{5... | collective-permute-start | bytes 589832 | tf_op jit(solution)/shard_map/ppermute | solution.py:39
  (314 shorter events, 163.4 us)
Async XLA Ops:
  7.9 25.7 %collective-permute-start = (bf16[32,8,768]{2,0,1:T(8,128)(2,1)}, bf16[32,8,768]{2,0,1:T(8,128)(2,1)S(1)}, u32[]{:S(2)}, u32[]{:S(2)}) collective-permute-start(bf16[32,8,768]{2,0,1:T(8,128)(2,1)} %bitcast.232), channel_id=1, source_target_pairs={{0,1},{1,0},{2,3},{3,2},{4,5},{5,4},{6,7},{7,6},{8,9},{9,8},{10,11... | collective-permute-start | bytes 1179656 | tf_op jit(solution)/shard_map/ppermute | solution.py:39
  38.6 33.1 %collective-permute-start.5 = (bf16[32,32,768]{2,1,0:T(8,128)(2,1)S(1)}, bf16[32,32,768]{2,1,0:T(8,128)(2,1)}, u32[]{:S(2)}, u32[]{:S(2)}) collective-permute-start(bf16[32,32,768]{2,1,0:T(8,128)(2,1)S(1)} %bitcast.181), channel_id=1, source_target_pairs={{0,4},{4,0},{8,12},{12,8},{16,20},{20,16},{24,28},{28,24},{1,5},{5... | collective-permute-start | bytes 4718600 | tf_op jit(solution)/shard_map/ppermute | solution.py:39
  42.0 29.8 %collective-permute-start.3 = (bf16[1,16,32,768]{3,2,1,0:T(8,128)(2,1)S(1)}, bf16[1,16,32,768]{3,2,1,0:T(8,128)(2,1)S(1)}, u32[]{:S(2)}, u32[]{:S(2)}) collective-permute-start(bf16[1,16,32,768]{3,2,1,0:T(8,128)(2,1)S(1)} %get-tuple-element.314), channel_id=1, source_target_pairs={{0,8},{4,12},{8,0},{12,4},{16,24},{20,28},{24,16},{28,20},{1,9},{5... | collective-permute-start | bytes 2359304 | tf_op jit(solution)/shard_map/ppermute | solution.py:39
  43.2 28.5 %collective-permute-start.4 = (bf16[1,16,32,768]{3,2,1,0:T(8,128)(2,1)S(1)}, bf16[1,16,32,768]{3,2,1,0:T(8,128)(2,1)S(1)}, u32[]{:S(2)}, u32[]{:S(2)}) collective-permute-start(bf16[1,16,32,768]{3,2,1,0:T(8,128)(2,1)S(1)} %get-tuple-element.313), channel_id=1, source_target_pairs={{0,16},{4,20},{8,24},{12,28},{16,0},{20,4},{24,8},{28,12},{1,17},{... | collective-permute-start | bytes 2359304 | tf_op jit(solution)/shard_map/ppermute | solution.py:39
  44.5 27.3 %collective-permute-start.6 = (bf16[288,768]{1,0:T(8,128)(2,1)S(1)}, bf16[288,768]{1,0:T(8,128)(2,1)S(1)}, u32[]{:S(2)}, u32[]{:S(2)}) collective-permute-start(bf16[288,768]{1,0:T(8,128)(2,1)S(1)} %copy-done.11), channel_id=1, source_target_pairs={{0,2},{1,3},{2,0},{3,1},{4,6},{5,7},{6,4},{7,5},{8,10},{9,11},{10,... | collective-permute-start | bytes 1327112 | tf_op jit(solution)/shard_map/ppermute | solution.py:39
  72.8 34.4 %collective-permute-start.8 = (bf16[2,16,32,768]{3,2,1,0:T(8,128)(2,1)S(1)}, bf16[2,16,32,768]{3,2,1,0:T(8,128)(2,1)S(1)}, u32[]{:S(2)}, u32[]{:S(2)}) collective-permute-start(bf16[2,16,32,768]{3,2,1,0:T(8,128)(2,1)S(1)} %pad_maximum_fusion.3), channel_id=1, source_target_pairs={{0,8},{4,12},{8,0},{12,4},{16,24},{20,28},{24,16},{28,20},{1,9},{5... | collective-permute-start | bytes 4718600 | tf_op jit(solution)/shard_map/ppermute | solution.py:39
  73.3 34.2 %collective-permute-start.7 = (bf16[2,16,32,768]{3,2,1,0:T(8,128)(2,1)S(1)}, bf16[2,16,32,768]{3,2,1,0:T(8,128)(2,1)}, u32[]{:S(2)}, u32[]{:S(2)}) collective-permute-start(bf16[2,16,32,768]{3,2,1,0:T(8,128)(2,1)S(1)} %pad_maximum_fusion.2), channel_id=1, source_target_pairs={{0,16},{4,20},{8,24},{12,28},{16,0},{20,4},{24,8},{28,12},{1,17},{... | collective-permute-start | bytes 4718600 | tf_op jit(solution)/shard_map/ppermute | solution.py:39
  113.8 25.6 %collective-permute-start.15 = (bf16[576,768]{1,0:T(8,128)(2,1)}, bf16[576,768]{1,0:T(8,128)(2,1)}, u32[]{:S(2)}, u32[]{:S(2)}) collective-permute-start(bf16[576,768]{1,0:T(8,128)(2,1)} %get-tuple-element.180), channel_id=1, source_target_pairs={{0,8},{4,12},{8,0},{12,4},{16,24},{20,28},{24,16},{28,20},{1,9},{5... | collective-permute-start | bytes 2654216 | tf_op jit(solution)/shard_map/ppermute | solution.py:39
  141.1 40.0 %collective-permute-start.18 = (bf16[2,576,768]{2,1,0:T(8,128)(2,1)S(1)}, bf16[2,576,768]{2,1,0:T(8,128)(2,1)}, u32[]{:S(2)}, u32[]{:S(2)}) collective-permute-start(bf16[2,576,768]{2,1,0:T(8,128)(2,1)S(1)} %pad_maximum_fusion.1.refs_8_), channel_id=1, source_target_pairs={{0,8},{4,12},{8,0},{12,4},{16,24},{20,28},{24,16},{28,20},{1,9},{5... | collective-permute-start | bytes 5308424 | tf_op jit(solution)/shard_map/ppermute | solution.py:39
  144.4 40.2 %collective-permute-start.17 = (bf16[2,576,768]{2,1,0:T(8,128)(2,1)}, bf16[2,576,768]{2,1,0:T(8,128)(2,1)}, u32[]{:S(2)}, u32[]{:S(2)}) collective-permute-start(bf16[2,576,768]{2,1,0:T(8,128)(2,1)} %pad_maximum_fusion.refs_4_), channel_id=1, source_target_pairs={{0,16},{4,20},{8,24},{12,28},{16,0},{20,4},{24,8},{28,12},{1,17},{... | collective-permute-start | bytes 5308424 | tf_op jit(solution)/shard_map/ppermute | solution.py:39
  145.6 28.0 %collective-permute-start.20 = (bf16[256,768]{1,0:T(8,128)(2,1)}, bf16[256,768]{1,0:T(8,128)(2,1)S(1)}, u32[]{:S(2)}, u32[]{:S(2)}) collective-permute-start(bf16[256,768]{1,0:T(8,128)(2,1)} %get-tuple-element.195), channel_id=1, source_target_pairs={{0,2},{1,3},{2,0},{3,1},{4,6},{5,7},{6,4},{7,5},{8,10},{9,11},{10,... | collective-permute-start | bytes 1179656 | tf_op jit(solution)/shard_map/ppermute | solution.py:39
  146.5 27.2 %collective-permute-start.21 = (bf16[256,768]{1,0:T(8,128)(2,1)}, bf16[256,768]{1,0:T(8,128)(2,1)S(1)}, u32[]{:S(2)}, u32[]{:S(2)}) collective-permute-start(bf16[256,768]{1,0:T(8,128)(2,1)} %get-tuple-element.196), channel_id=1, source_target_pairs={{0,3},{1,2},{2,1},{3,0},{4,7},{5,6},{6,5},{7,4},{8,11},{9,10},{10,... | collective-permute-start | bytes 1179656 | tf_op jit(solution)/shard_map/ppermute | solution.py:39
  223.0 28.7 %collective-permute-start.27 = (bf16[256,768]{1,0:T(8,128)(2,1)}, bf16[256,768]{1,0:T(8,128)(2,1)}, u32[]{:S(2)}, u32[]{:S(2)}) collective-permute-start(bf16[256,768]{1,0:T(8,128)(2,1)} %get-tuple-element.223.refs_2_.refs_1_), channel_id=1, source_target_pairs={{0,2},{1,3},{2,0},{3,1},{4,6},{5,7},{6,4},{7,5},{8,10},{9,11},{10,... | collective-permute-start | bytes 1179656 | tf_op jit(solution)/shard_map/ppermute | solution.py:39
  223.8 27.8 %collective-permute-start.28 = (bf16[256,768]{1,0:T(8,128)(2,1)}, bf16[256,768]{1,0:T(8,128)(2,1)}, u32[]{:S(2)}, u32[]{:S(2)}) collective-permute-start(bf16[256,768]{1,0:T(8,128)(2,1)} %get-tuple-element.223.refs_2_.refs_1_), channel_id=1, source_target_pairs={{0,3},{1,2},{2,1},{3,0},{4,7},{5,6},{6,5},{7,4},{8,11},{9,10},{10,... | collective-permute-start | bytes 1179656 | tf_op jit(solution)/shard_map/ppermute | solution.py:39
  290.0 39.0 %collective-permute-start.34 = (bf16[16,2,32,768]{3,2,1,0:T(8,128)(2,1)}, bf16[16,2,32,768]{3,2,1,0:T(8,128)(2,1)}, u32[]{:S(2)}, u32[]{:S(2)}) collective-permute-start(bf16[16,2,32,768]{3,2,1,0:T(8,128)(2,1)} %bitcast.226), channel_id=1, source_target_pairs={{0,8},{4,12},{8,0},{12,4},{16,24},{20,28},{24,16},{28,20},{1,9},{5... | collective-permute-start | bytes 4718600 | tf_op jit(solution)/shard_map/ppermute | solution.py:39
  290.6 38.4 %collective-permute-start.35 = (bf16[16,2,32,768]{3,2,1,0:T(8,128)(2,1)}, bf16[16,2,32,768]{3,2,1,0:T(8,128)(2,1)}, u32[]{:S(2)}, u32[]{:S(2)}) collective-permute-start(bf16[16,2,32,768]{3,2,1,0:T(8,128)(2,1)} %bitcast.225), channel_id=1, source_target_pairs={{0,16},{4,20},{8,24},{12,28},{16,0},{20,4},{24,8},{28,12},{1,17},{... | collective-permute-start | bytes 4718600 | tf_op jit(solution)/shard_map/ppermute | solution.py:39
  295.8 32.5 %collective-permute-start.36 = (bf16[2,104,768]{2,1,0:T(8,128)(2,1)}, bf16[2,104,768]{2,1,0:T(8,128)(2,1)S(1)}, u32[]{:S(2)}, u32[]{:S(2)}) collective-permute-start(bf16[2,104,768]{2,1,0:T(8,128)(2,1)} %get-tuple-element.317), channel_id=1, source_target_pairs={{0,1},{1,0},{2,3},{3,2},{4,5},{5,4},{6,7},{7,6},{8,9},{9,8},{10,11... | collective-permute-start | bytes 958472 | tf_op jit(solution)/shard_map/ppermute | solution.py:39
  338.8 46.2 %collective-permute-start.39 = (bf16[848,768]{1,0:T(8,128)(2,1)}, bf16[848,768]{1,0:T(8,128)(2,1)}, u32[]{:S(2)}, u32[]{:S(2)}) collective-permute-start(bf16[848,768]{1,0:T(8,128)(2,1)} %pad_maximum_fusion.4), channel_id=1, source_target_pairs={{0,16},{4,20},{8,24},{12,28},{16,0},{20,4},{24,8},{28,12},{1,17},{... | collective-permute-start | bytes 3907592 | tf_op jit(solution)/shard_map/ppermute | solution.py:39
  353.8 34.8 %collective-permute-start.45 = (bf16[840,768]{1,0:T(8,128)(2,1)}, bf16[840,768]{1,0:T(8,128)(2,1)}, u32[]{:S(2)}, u32[]{:S(2)}) collective-permute-start(bf16[840,768]{1,0:T(8,128)(2,1)} %pad_maximum_fusion.5), channel_id=1, source_target_pairs={{0,8},{4,12},{8,0},{12,4},{16,24},{20,28},{24,16},{28,20},{1,9},{5... | collective-permute-start | bytes 3870728 | tf_op jit(solution)/shard_map/ppermute | solution.py:39
  358.8 33.3 %collective-permute-start.46 = (bf16[8,32,768]{2,1,0:T(8,128)(2,1)}, bf16[8,32,768]{2,1,0:T(8,128)(2,1)}, u32[]{:S(2)}, u32[]{:S(2)}) collective-permute-start(bf16[8,32,768]{2,1,0:T(8,128)(2,1)} %get-tuple-element.269), channel_id=1, source_target_pairs={{0,1},{1,0},{2,3},{3,2},{4,5},{5,4},{6,7},{7,6},{8,9},{9,8},{10,11... | collective-permute-start | bytes 1179656 | tf_op jit(solution)/shard_map/ppermute | solution.py:39
  363.8 28.3 %collective-permute-start.47 = (bf16[8,32,768]{2,1,0:T(8,128)(2,1)}, bf16[8,32,768]{2,1,0:T(8,128)(2,1)}, u32[]{:S(2)}, u32[]{:S(2)}) collective-permute-start(bf16[8,32,768]{2,1,0:T(8,128)(2,1)} %get-tuple-element.270), channel_id=1, source_target_pairs={{0,2},{1,3},{2,0},{3,1},{4,6},{5,7},{6,4},{7,5},{8,10},{9,11},{10,... | collective-permute-start | bytes 1179656 | tf_op jit(solution)/shard_map/ppermute | solution.py:39
  365.1 27.0 %collective-permute-start.48 = (bf16[8,32,768]{2,1,0:T(8,128)(2,1)}, bf16[8,32,768]{2,1,0:T(8,128)(2,1)}, u32[]{:S(2)}, u32[]{:S(2)}) collective-permute-start(bf16[8,32,768]{2,1,0:T(8,128)(2,1)} %get-tuple-element.271), channel_id=1, source_target_pairs={{0,3},{1,2},{2,1},{3,0},{4,7},{5,6},{6,5},{7,4},{8,11},{9,10},{10,... | collective-permute-start | bytes 1179656 | tf_op jit(solution)/shard_map/ppermute | solution.py:39
  422.8 26.6 %collective-permute-start.62 = (bf16[1,192,768]{2,1,0:T(8,128)(2,1)S(1)}, bf16[1,192,768]{2,1,0:T(8,128)(2,1)S(1)}, u32[]{:S(2)}, u32[]{:S(2)}) collective-permute-start(bf16[1,192,768]{2,1,0:T(8,128)(2,1)S(1)} %get-tuple-element.319), channel_id=1, source_target_pairs={{0,1},{1,0},{2,3},{3,2},{4,5},{5,4},{6,7},{7,6},{8,9},{9,8},{10,11... | collective-permute-start | bytes 884744 | tf_op jit(solution)/shard_map/ppermute | solution.py:39
  422.8 26.5 %collective-permute-start.63 = (bf16[1,192,768]{2,1,0:T(8,128)(2,1)S(1)}, bf16[1,192,768]{2,1,0:T(8,128)(2,1)S(1)}, u32[]{:S(2)}, u32[]{:S(2)}) collective-permute-start(bf16[1,192,768]{2,1,0:T(8,128)(2,1)S(1)} %get-tuple-element.321), channel_id=1, source_target_pairs={{0,2},{1,3},{2,0},{3,1},{4,6},{5,7},{6,4},{7,5},{8,10},{9,11},{10,... | collective-permute-start | bytes 884744 | tf_op jit(solution)/shard_map/ppermute | solution.py:39
  (78 other events, 1159.6 us)
